TPU v7x, 512 devices: a whole 4x8x8 slice. The times are simulated.
512 devices in a mesh: section: 8 (over z), row: 4 (over x_hi, core), col: 16 (over x_lo, y).
Axes of the slice: x: 4 (x_hi: 2, x_lo: 2; x = x_hi * 2 + x_lo), y: 8, z: 8, core: 2. Of those that a mesh axis runs over, the one named last changes fastest.
Arguments:
- hidden_in: bfloat16 [8, 512, 8192], P('section', 'col', 'row'), may hold values from -600 to 600
- norm_gain: float32 [8, 8192], P('section', 'row'), may hold values from 0.1 to 1.9
- q_weight: bfloat16 [8, 8192, 8192], P('section', 'row', 'col'), may hold values from -0.0625 to 0.0625
- kv_weight: bfloat16 [8, 8192, 2048], P('section', 'row', 'col'), may hold values from -0.0625 to 0.0625
- kv_cache: bfloat16 [8, 32, 1024, 2, 1024], P('section', 'col', 'row'), may hold values from -110 to 110
- lengths: int32 [8, 32], P('section', 'col'), may hold values from 768 to 1024, as said below
Outputs:
- handed: bfloat16 [8, 512, 8192], P('section', 'col', 'row')
- new_kv: bfloat16 [8, 512, 2048], P('section', 'col')
Inputs may be any that keep to these rules, and one draw needn't show every extreme that they name: `lengths`: in every section some prompt uses exactly 1024 positions.
All inputs are finite; a program needn't handle non-finite values.
Results may differ from a plain program's by a relative error of at most 0.023.
Values may be sent and summed in bfloat16 or wider, within the bound.
No kernel may reach another device: no remote copies, remote signals or barrier semaphores. Data moves between devices by JAX's collectives and lax.ppermute only.
A program may use at most 64 MiB of HBM per device.

v0:
```python
import jax
import jax.numpy as jnp
from jax import lax
from jax.sharding import PartitionSpec as P

HEAD_DIM = 128


EPSILON = 1e-05
FLOOR = -1e30


def combined_all(value, axis, combine):
    everything = jax.tree.map(
        lambda part, kind: lax.all_gather(part.astype(kind), axis),
        value,
        (jnp.bfloat16, jnp.bfloat16, jnp.bfloat16),
    )

    def take(k):
        return jax.tree.map(lambda part, own: part[k].astype(own.dtype), everything, value)

    return lax.fori_loop(
        1, lax.axis_size(axis), lambda k, so_far: combine(so_far, take(k)), take(0)
    )


def shifted(block, axis, distance):
    devices = range(lax.axis_size(axis))
    route = [((i - distance) % len(devices), i) for i in devices]
    return lax.ppermute(block, axis, route)


def join_parts(former, latter):
    top_score = jnp.maximum(former[0], latter[0])
    keep_former = jnp.exp(former[0] - top_score)
    keep_latter = jnp.exp(latter[0] - top_score)
    return (
        top_score,
        former[1] * keep_former + latter[1] * keep_latter,
        former[2] * keep_former[..., None] + latter[2] * keep_latter[..., None],
    )


def finish(run_max, run_total, run_out, own_score, own_values):
    top_score = jnp.maximum(run_max, own_score)
    keep_part = jnp.exp(run_max - top_score)
    own_weight = jnp.exp(own_score - top_score)
    total_weight = run_total * keep_part + own_weight
    own_rounded = lax.optimization_barrier(own_weight.astype(jnp.bfloat16)).astype(jnp.float32)
    numerator = run_out * keep_part[..., None] + own_rounded[..., None] * own_values.astype(
        jnp.float32
    )
    attended = (numerator / total_weight[..., None]).astype(jnp.bfloat16)
    return attended.reshape(attended.shape[0], -1)


def shards(hidden_in, norm_gain, q_weight, kv_weight, kv_cache, lengths):
    row_count = lax.axis_size("row")
    col_count = lax.axis_size("col")
    row_index = lax.axis_index("row")
    rows_here = hidden_in.shape[1]
    width_part = hidden_in.shape[2]
    sub_rows = rows_here // row_count
    widened = hidden_in[0].astype(jnp.float32)
    squares = lax.psum(jnp.sum(widened * widened, axis=1), "row")
    scaling = lax.rsqrt(squares / (width_part * row_count) + EPSILON)
    normed = (widened * scaling[:, None] * norm_gain[0][None, :]).astype(jnp.bfloat16)
    gathered = lax.all_gather(
        normed.reshape(row_count, sub_rows, width_part), "col", axis=1, tiled=True
    )
    query_weight = q_weight[0]
    pair_weight = kv_weight[0]
    query_cols = query_weight.shape[1]
    pair_cols = pair_weight.shape[1]
    lead_shape = gathered.shape[:-1]
    flat_rows = gathered.reshape(-1, width_part)
    query_part = jnp.dot(flat_rows, query_weight, preferred_element_type=jnp.float32).reshape(
        lead_shape + (query_cols,)
    )
    pair_part = jnp.dot(flat_rows, pair_weight, preferred_element_type=jnp.float32).reshape(
        lead_shape + (pair_cols,)
    )
    query_part, pair_part = (query_part, pair_part)
    query_total, pair_total = lax.psum((query_part, pair_part), "row")
    query_blocks = query_total.astype(jnp.bfloat16).reshape(
        row_count, col_count, sub_rows, query_cols
    )
    pair_blocks = pair_total.astype(jnp.bfloat16).reshape(row_count, col_count, sub_rows, pair_cols)
    query_mine, pair_mine = (
        lax.all_to_all(query_blocks, "col", split_axis=1, concat_axis=3, tiled=True),
        lax.all_to_all(pair_blocks, "col", split_axis=1, concat_axis=3, tiled=True),
    )
    query = query_mine.reshape(rows_here, -1)
    new_kv = pair_mine.reshape(rows_here, -1)
    prompts_here = lengths.shape[1]
    samples = rows_here // prompts_here
    key_heads = new_kv.shape[1] // (2 * HEAD_DIM)
    head_count = query.shape[1] // HEAD_DIM
    group_size = head_count // key_heads
    score_scale = HEAD_DIM ** (-0.5)
    query_heads = query.reshape(prompts_here, samples, key_heads, group_size, HEAD_DIM)
    cache_local = kv_cache[0]
    positions_here = cache_local.shape[1]
    cache_keys = cache_local[:, :, 0].reshape(prompts_here, positions_here, key_heads, HEAD_DIM)
    cache_values = cache_local[:, :, 1].reshape(prompts_here, positions_here, key_heads, HEAD_DIM)
    scores = (
        jnp.einsum("psghd,ptgd->psght", query_heads, cache_keys, preferred_element_type=jnp.float32)
        * score_scale
    )
    positions = row_index * positions_here + jnp.arange(positions_here, dtype=jnp.int32)
    in_range = (positions[None, :] < lengths[0][:, None])[:, None, None, None, :]
    local_max = jnp.max(jnp.where(in_range, scores, FLOOR), axis=-1)
    weights = jnp.where(in_range, jnp.exp(scores - local_max[..., None]), 0.0)
    local_total = jnp.sum(weights, axis=-1)
    local_out = jnp.einsum(
        "psght,ptgd->psghd",
        weights.astype(jnp.bfloat16),
        cache_values,
        preferred_element_type=jnp.float32,
    )
    new_keys = new_kv[:, : key_heads * HEAD_DIM].reshape(prompts_here, samples, key_heads, HEAD_DIM)
    new_values = new_kv[:, key_heads * HEAD_DIM :].reshape(rows_here, key_heads, 1, HEAD_DIM)
    own_score = (
        jnp.einsum("psghd,psgd->psgh", query_heads, new_keys, preferred_element_type=jnp.float32)
        * score_scale
    )
    own_score = own_score.reshape(rows_here, head_count)
    own_values = jnp.broadcast_to(new_values, (rows_here, key_heads, group_size, HEAD_DIM)).reshape(
        rows_here, head_count, HEAD_DIM
    )
    part_heads = head_count // row_count
    first_head = row_index * part_heads
    flat_max = local_max.reshape(rows_here, head_count)
    flat_total = local_total.reshape(rows_here, head_count)
    flat_out = local_out.reshape(rows_here, head_count, HEAD_DIM)
    joined = combined_all((flat_max, flat_total, flat_out), "row", join_parts)
    run_max = lax.dynamic_slice_in_dim(joined[0], first_head, part_heads, 1)
    run_total = lax.dynamic_slice_in_dim(joined[1], first_head, part_heads, 1)
    run_out = lax.dynamic_slice_in_dim(joined[2], first_head, part_heads, 1)
    mine_score = lax.dynamic_slice_in_dim(own_score, first_head, part_heads, 1)
    mine_values = lax.dynamic_slice_in_dim(own_values, first_head, part_heads, 1)
    attended = finish(run_max, run_total, run_out, mine_score, mine_values)
    handed = shifted(attended[None], "section", 1)
    return (handed, new_kv[None])


def solution(mesh):
    return jax.shard_map(
        shards,
        mesh=mesh,
        in_specs=(
            P("section", "col", "row"),
            P("section", "row"),
            P("section", "row", "col"),
            P("section", "row", "col"),
            P("section", "col", "row", None, None),
            P("section", "col"),
        ),
        out_specs=(P("section", "col", "row"), P("section", "col", None)),
        check_vma=False,
    )
```

profile of v0, /device:TPU:1, one launch (start us, length us, event | category | flops | bytes accessed | tf_op | source)
XLA Modules:
  0.0 223.1 jit_solution(13363737782386620160)
XLA Ops:
  7.2 0.0 copy-start
  7.2 0.0 all-gather.3.cloned.1.call-start
  7.2 1.2 fusion.24
  8.4 13.4 %psum.21 = f32[32]{0:T(128)S(1)} all-reduce(f32[32]{0:T(128)S(1)} %fusion.24), channel_id=1, replica_groups=mesh['section'=8,'row'=4,'col'=16] {'row'}, use_global_device_ids=true, to_apply=%region_1.0 | all-reduce | flops 32 | bytes 256 | tf_op jit(solution)/shard_map/psum | solution.py:66
  21.8 0.1 mul.140
  21.9 1.7 fusion.23
  23.6 0.0 all-gather.3.cloned.1.call-update
  23.6 64.8 %all-gather.3.cloned.1.call-done = bf16[4,128,2048]{2,1,0:T(8,128)(2,1)} async-done(((bf16[4,8,2048]{2,1,0:T(8,128)(2,1)}), bf16[4,128,2048]{2,1,0:T(8,128)(2,1)}) %all-gather.3.cloned.1.call-update) | async-done | bytes 2097168 | tf_op jit(solution)/shard_map/all_gather | solution.py:69
  88.4 3.0 %fusion.6 = f32[4,128,512]{2,1,0:T(8,128)S(1)} fusion(bf16[4,128,2048]{2,1,0:T(8,128)(2,1)} %all-gather.3.cloned.1.call-done, bf16[1,2048,512]{2,1,0:T(8,128)(2,1)S(1)} %copy-done), kind=kOutput, calls=%fused_computation.13 | convolution fusion | flops 1073741824 | bytes 5242880 | tf_op jit(solution)/shard_map/dot_general | solution.py:78
  91.4 0.0 copy-done.2
  91.4 0.0 copy-done.5
  91.4 0.7 fusion.17
  92.1 41.9 %all-reduce.2 = (bf16[4,128,512]{2,1,0:T(8,128)(2,1)}, bf16[4,128,128]{2,1,0:T(8,128)(2,1)S(1)}) all-reduce(f32[4,128,512]{2,1,0:T(8,128)S(1)} %fusion.6, f32[4,128,128]{2,1,0:T(8,128)S(1)} %fusion.17), channel_id=1, replica_groups=mesh['section'=8,'row'=4,'col'=16] {'row'}, use_global_device_ids=true, to_apply=%region_2.0 | all-reduce | flops 327680 | bytes 1966080 | tf_op jit(solution)/shard_map/psum | solution.py:85
  134.0 1.9 copy.61
  135.9 4.2 %all-to-all-start = ((bf16[4,16,8,512]{3,2,0,1:T(8,128)(2,1)}), bf16[4,16,8,512]{3,2,0,1:T(8,128)(2,1)}, u32[]{:S(2)}, u32[]{:S(2)}) async-start(bf16[4,16,8,512]{3,2,0,1:T(8,128)(2,1)} %copy.61), calls=%async_computation | async-start | bytes 1048576 | tf_op jit(solution)/shard_map/all_to_all | solution.py:91
  140.1 0.0 all-gather.5.cloned.1.call-start
  140.2 0.0 copy-start.6
  140.2 6.1 %copy.63 = bf16[1,2,256,2,1024]{2,4,1,3,0:T(8,128)(2,1)} copy(bf16[1,2,256,2,1024]{4,3,2,1,0:T(2,128)(2,1)} %param.12) | data formatting | bytes 4194304 | tf_op args[4]
  146.4 0.0 copy-done.6
  146.4 0.1 broadcast_compare_fusion
  146.4 2.7 %fusion.34 = (bf16[2,256,1,1024]{1,3,0,2:T(8,128)(2,1)}, bf16[2,256,1,1024]{1,3,0,2:T(8,128)(2,1)S(1)}) fusion(bf16[2,256,2,1024]{1,3,0,2:T(8,128)(2,1)} %bitcast.123), kind=kLoop, calls=%fused_computation.58 | loop fusion | bytes 4194304 | tf_op jit(solution)/shard_map/slice | solution.py:106
  149.1 6.5 %all-to-all-done = bf16[4,16,8,512]{3,2,0,1:T(8,128)(2,1)} async-done(((bf16[4,16,8,512]{3,2,0,1:T(8,128)(2,1)}), bf16[4,16,8,512]{3,2,0,1:T(8,128)(2,1)}, u32[]{:S(2)}, u32[]{:S(2)}) %all-to-all-start) | async-done | bytes 524320 | tf_op jit(solution)/shard_map/all_to_all | solution.py:91
  155.6 2.1 copy.62
  157.8 2.2 reshape_reshape.3
  159.9 1.7 fusion.3
  161.6 0.6 fusion.10
  162.2 0.7 copy-done.1
  162.9 0.9 copy.73
  163.9 0.0 all-gather.5.cloned.1.call-update
  163.9 0.7 copy.75
  164.6 5.0 %all-to-all-start.1 = ((bf16[4,16,8,128]{3,2,0,1:T(8,128)(2,1)}), bf16[4,16,8,128]{3,2,0,1:T(8,128)(2,1)S(1)}, u32[]{:S(2)}, u32[]{:S(2)}) async-start(bf16[4,16,8,128]{3,2,0,1:T(8,128)(2,1)} %copy.75), calls=%async_computation.1 | async-start | bytes 262144 | tf_op jit(solution)/shard_map/all_to_all | solution.py:92
  169.6 7.4 %all-to-all-done.1 = bf16[4,16,8,128]{3,2,0,1:T(8,128)(2,1)S(1)} async-done(((bf16[4,16,8,128]{3,2,0,1:T(8,128)(2,1)}), bf16[4,16,8,128]{3,2,0,1:T(8,128)(2,1)S(1)}, u32[]{:S(2)}, u32[]{:S(2)}) %all-to-all-start.1) | async-done | bytes 131104 | tf_op jit(solution)/shard_map/all_to_all | solution.py:92
  177.0 0.1 copy.100
  177.1 0.1 reshape.155
  177.2 1.0 broadcast_bitcast_fusion
  178.1 0.1 copy.66
  178.2 0.4 fusion.36
  178.7 0.1 copy.85
  178.8 0.1 reshape.139
  178.9 2.3 %fusion.9 = bf16[2,16,8,8]{3,1,2,0:T(8,128)(2,1)S(1)} fusion(f32[2,8,16,8,256]{4,3,2,1,0:T(8,128)} %copy-done.1, f32[2,16,8,8]{3,1,2,0:T(8,128)S(1)} %get-tuple-element.219, pred[2,256]{1,0:T(4,128)(4,1)S(1)} %broadcast_compare_fusion), kind=kLoop, calls=%fused_computation.16 | loop fusion | flops 2095104 | bytes 2109952 | tf_op jit(solution)/shard_map/reduce_sum | solution.py:115
  181.2 0.1 copy.69
  181.4 0.1 convert_element_type.144
  181.5 0.1 copy.71
  181.6 0.1 convert_element_type.140
  181.7 0.1 copy.68
  181.8 8.7 %all_gather.16 = bf16[4,32,64]{2,1,0:T(8,128)(2,1)S(1)} all-gather(bf16[1,32,64]{2,1,0:T(8,128)(2,1)S(1)} %copy.68), channel_id=1, replica_groups=mesh['section'=8,'row'=4,'col'=16] {'row'}, dimensions={0}, use_global_device_ids=true | all-gather | bytes 20480 | tf_op jit(solution)/shard_map/all_gather | solution.py:15
  190.5 6.7 %all_gather.17 = bf16[4,32,64]{2,1,0:T(8,128)(2,1)S(1)} all-gather(bf16[1,32,64]{2,1,0:T(8,128)(2,1)S(1)} %copy.71), channel_id=1, replica_groups=mesh['section'=8,'row'=4,'col'=16] {'row'}, dimensions={0}, use_global_device_ids=true | all-gather | bytes 20480 | tf_op jit(solution)/shard_map/all_gather | solution.py:15
  197.2 0.0 all-gather.5.cloned.1.call-done
  197.2 1.1 fusion.16
  198.4 6.2 %while.19 = (s32[]{:T(128)}, f32[32,64]{1,0:T(8,128)S(1)}, f32[32,64]{1,0:T(8,128)S(1)}, f32[32,64,128]{2,1,0:T(8,128)S(1)}, bf16[4,32,64]{2,1,0:T(8,128)(2,1)S(...) while((s32[]{:T(128)}, f32[32,64]{1,0:T(8,128)S(1)}, ...), condition=%wide.region_6.7_spmd, body=%wide.region_5.6_spmd.sunk | while | flops 1064965 | bytes 2695311 | solution.py:23
  198.4 2.0 fusion.46
  200.5 2.0 fusion.46
  202.5 2.0 fusion.46
  204.6 0.1 copy.74
  204.6 0.1 copy.79
  204.7 0.1 copy.80
  204.8 0.1 copy.77
  204.9 0.1 copy.78
  205.0 1.2 divide_convert_fusion
  206.2 0.1 broadcast_in_dim_reshape.6
  206.2 3.3 %collective-permute-start = (bf16[1,32,2048]{2,1,0:T(8,128)(2,1)S(1)}, bf16[1,32,2048]{2,1,0:T(8,128)(2,1)S(1)}, u32[]{:S(2)}, u32[]{:S(2)}) collective-permute-start(bf16[1,32,2048]{2,1,0:T(8,128)(2,1)S(1)} %broadcast_in_dim_reshape.6), channel_id=1, source_target_pairs={{448,0},{0,64},{64,128},{128,192},{192,256},{256,320},{320,384},{3... | collective-permute-start | bytes 393224 | tf_op jit(solution)/shard_map/ppermute | solution.py:31
  209.5 0.7 broadcast_in_dim_reshape.7
  210.2 5.4 %collective-permute-done = bf16[1,32,2048]{2,1,0:T(8,128)(2,1)S(1)} collective-permute-done((bf16[1,32,2048]{2,1,0:T(8,128)(2,1)S(1)}, bf16[1,32,2048]{2,1,0:T(8,128)(2,1)S(1)}, u32[]{:S(2)}, u32[]{:S(2)}) %collective-permute-start) | collective-permute-done | bytes 131104 | tf_op jit(solution)/shard_map/ppermute | solution.py:31
  215.6 0.7 copy.118
  (22 shorter events, 0.3 us)
Async XLA Ops:
  7.2 81.2 %copy-start = (bf16[1,2048,512]{2,1,0:T(8,128)(2,1)S(1)}, bf16[1,2048,512]{2,1,0:T(8,128)(2,1)}, u32[]{:S(2)}) copy-start(bf16[1,2048,512]{2,1,0:T(8,128)(2,1)} %param.10) | copy-start | bytes 6291460
  7.2 81.2 %all-gather.3.cloned.1.call-start = ((), (), s32[]{:S(2)}) async-start(), calls=%async_computation.2 | async-start | bytes 2228224 | tf_op jit(solution)/shard_map/all_gather | solution.py:69
  88.4 3.0 %copy-start.2 = (bf16[4,128,2048]{2,1,0:T(8,128)(2,1)S(1)}, bf16[4,128,2048]{2,1,0:T(8,128)(2,1)}, u32[]{:S(2)}) copy-start(bf16[4,128,2048]{2,1,0:T(8,128)(2,1)} %all-gather.3.cloned.1.call-done) | copy-start | bytes 6291460
  88.4 3.0 %copy-start.5 = (bf16[1,2048,128]{2,1,0:T(8,128)(2,1)S(1)}, bf16[1,2048,128]{2,1,0:T(8,128)(2,1)}, u32[]{:S(2)}) copy-start(bf16[1,2048,128]{2,1,0:T(8,128)(2,1)} %param.11) | copy-start | bytes 1572868
  135.9 19.8 %all-to-all-start = ((bf16[4,16,8,512]{3,2,0,1:T(8,128)(2,1)}), bf16[4,16,8,512]{3,2,0,1:T(8,128)(2,1)}, u32[]{:S(2)}, u32[]{:S(2)}) async-start(bf16[4,16,8,512]{3,2,0,1:T(8,128)(2,1)} %copy.61), calls=%async_computation | async-start | bytes 1048576 | tf_op jit(solution)/shard_map/all_to_all | solution.py:91
  140.1 57.1 %all-gather.5.cloned.1.call-start = ((), (), s32[]{:S(2)}) async-start(), calls=%async_computation.3 | async-start | bytes 2621440 | tf_op jit(solution)/shard_map/all_gather | solution.py:15
  140.2 6.2 %copy-start.6 = (s32[1,2]{1,0:T(1,128)S(1)}, s32[1,2]{1,0:T(1,128)}, u32[]{:S(2)}) copy-start(s32[1,2]{1,0:T(1,128)} %param.13) | copy-start | bytes 28
  159.9 1.7 copy-start.4
  161.6 1.3 copy-start.1
  162.9 15.3 %copy-start.3 = (bf16[2,16,8,8,128]{4,3,2,1,0:T(8,128)(2,1)S(1)}, bf16[2,16,8,8,128]{4,3,2,1,0:T(8,128)(2,1)}, u32[]{:S(2)}) copy-start(bf16[2,16,8,8,128]{4,3,2,1,0:T(8,128)(2,1)} %reshape_reshape.3) | copy-start | bytes 1572868
  164.6 12.4 %all-to-all-start.1 = ((bf16[4,16,8,128]{3,2,0,1:T(8,128)(2,1)}), bf16[4,16,8,128]{3,2,0,1:T(8,128)(2,1)S(1)}, u32[]{:S(2)}, u32[]{:S(2)}) async-start(bf16[4,16,8,128]{3,2,0,1:T(8,128)(2,1)} %copy.75), calls=%async_computation.1 | async-start | bytes 262144 | tf_op jit(solution)/shard_map/all_to_all | solution.py:92
  206.2 9.4 %collective-permute-start = (bf16[1,32,2048]{2,1,0:T(8,128)(2,1)S(1)}, bf16[1,32,2048]{2,1,0:T(8,128)(2,1)S(1)}, u32[]{:S(2)}, u32[]{:S(2)}) collective-permute-start(bf16[1,32,2048]{2,1,0:T(8,128)(2,1)S(1)} %broadcast_in_dim_reshape.6), channel_id=1, source_target_pairs={{448,0},{0,64},{64,128},{128,192},{192,256},{256,320},{320,384},{3... | collective-permute-start | bytes 393224 | tf_op jit(solution)/shard_map/ppermute | solution.py:31
Sparse Core Ops, SparseCore 0:
  23.7 64.6 all-gather.2
  164.0 30.6 all-gather.4
where the time goes:
time: 224 us; the launch traced here: 223 us
  waiting for transfers between devices  84.2 us (38%)
  blocking collectives  70.7 us (32%)
  local copies, waits for them, and re-layouts  21.2 us (9%)
  between operations  14.3 us (6%)
  other arithmetic  13.7 us (6%)
  starting transfers between devices  12.6 us (6%)
  matrix products  6.38 us (3%)
    all_gather x1, waiting for transfers between devices, shards(): lax.all_gather(normed.reshape(row_count, sub_rows, width_part), 'col', ax...  64.8 us
    psum x1, blocking collectives, shards(): query_total, pair_total = lax.psum((query_part, pair_part), 'row')  41.9 us
    all_gather x2, blocking collectives, combined_all(): lax.all_gather(part.astype(kind), axis)  15.4 us
    psum x1, blocking collectives, shards(): squares = lax.psum(jnp.sum(widened * widened, axis=1), 'row')  13.4 us
    unnamed x19, local copies, waits for them, and re-layouts  7.6 us
    all_to_all x1, waiting for transfers between devices, shards(): lax.all_to_all(pair_blocks, 'col', split_axis=1, concat_axis=3, tiled=True)  7.43 us
    all_to_all x1, waiting for transfers between devices, shards(): lax.all_to_all(query_blocks, 'col', split_axis=1, concat_axis=3, tiled=True)  6.54 us
    add x3, other arithmetic, join_parts(): former[2] * keep_former[..., None] + latter[2] * keep_latter[..., None]  6 us
  transfers between devices with their start and end apart: 5, of which 4 were waited for; matrix products, arithmetic and copies ran while one was open for 7% of the time, Pallas kernels for 0%

commit v1 on v0

v1 whole, which is shorter than its diff:
```python
import jax
import jax.numpy as jnp
from jax import lax
from jax.experimental import pallas as pl
from jax.experimental.pallas import tpu as pltpu
from jax.sharding import Mesh
from jax.sharding import PartitionSpec as P

HEAD_DIM = 128
EPSILON = 1e-05
FLOOR = -1e30
ROW = ("xh", "co")
COL = ("xl", "y")
BF = jnp.bfloat16
F32 = jnp.float32


def attend_kernel(lengths_ref, parts_ref, scale_ref, cache_ref, out_ref, pair_ref):
    sources, blocks, rows, _ = parts_ref.shape
    _, prompts, _, heads, chunk, dim = cache_ref.shape
    samples = rows // prompts
    scale = scale_ref[...]
    total = []
    for j in range(blocks):
        part = parts_ref[0, j].astype(F32)
        for s in range(1, sources):
            part = part + parts_ref[s, j].astype(F32)
        total.append((part * scale).astype(BF))
    per_block = 512 // dim
    for j in range(blocks):
        pair_ref[j] = total[j][:, 512:]
    for p in range(prompts):
        length = lengths_ref[0, p]
        here = slice(p * samples, (p + 1) * samples)
        for g in range(heads):
            names = [(j, h) for j in (2 * g, 2 * g + 1) for h in range(per_block)]
            query = jnp.concatenate(
                [total[j][here, h * dim : (h + 1) * dim] for j, h in names], axis=0
            )
            new_key = total[g][here, 512:].astype(F32)
            new_value = total[2 + g][here, 512:].astype(F32)
            new_key = jnp.concatenate([new_key] * len(names), axis=0)
            new_value = jnp.concatenate([new_value] * len(names), axis=0)
            factor = dim**-0.5
            own = jnp.sum(query.astype(F32) * new_key, axis=1, keepdims=True) * factor
            scores = []
            top = own
            for s in range(sources):
                block = lax.dot_general(
                    query,
                    cache_ref[s, p, 0, g],
                    (((1,), (1,)), ((), ())),
                    preferred_element_type=F32,
                )
                place = s * chunk + lax.broadcasted_iota(jnp.int32, block.shape, 1)
                block = jnp.where(place < length, block * factor, FLOOR)
                top = jnp.maximum(top, jnp.max(block, axis=1, keepdims=True))
                scores.append(block)
            own_weight = jnp.exp(own - top)
            weight_sum = own_weight
            value = own_weight.astype(BF).astype(F32) * new_value
            for s in range(sources):
                weight = jnp.exp(scores[s] - top)
                weight_sum = weight_sum + jnp.sum(weight, axis=1, keepdims=True)
                value = value + jnp.dot(
                    weight.astype(BF), cache_ref[s, p, 1, g], preferred_element_type=F32
                )
            result = (value / weight_sum).astype(BF)
            for n, (j, h) in enumerate(names):
                at = (j * per_block + h) * dim
                out_ref[here, at : at + dim] = result[n * samples : (n + 1) * samples]


def attend(lengths, parts, scale, cache):
    rows = parts.shape[2]
    vmem = pl.BlockSpec(memory_space=pltpu.VMEM)
    return pl.pallas_call(
        attend_kernel,
        out_shape=(
            jax.ShapeDtypeStruct((rows, 2048), BF),
            jax.ShapeDtypeStruct((4, rows, HEAD_DIM), BF),
        ),
        in_specs=[pl.BlockSpec(memory_space=pltpu.SMEM), vmem, vmem, vmem],
        out_specs=(vmem, vmem),
        compiler_params=pltpu.CompilerParams(vmem_limit_bytes=32 * 1024 * 1024),
        name="attend",
    )(lengths, parts, scale, cache)


def shards(hidden_in, norm_gain, q_weight, kv_weight, kv_cache, lengths):
    rows = hidden_in.shape[1]
    width = hidden_in.shape[2]
    col_count = 16
    row_count = 4
    widened = hidden_in[0].astype(F32)
    sent = (widened * norm_gain[0][None, :]).astype(BF)
    gathered = lax.all_to_all(
        jnp.broadcast_to(sent[None], (col_count, rows, width)), COL, 0, 0
    )
    squares = lax.psum(jnp.sum(widened * widened, axis=1), ROW)
    scale = lax.rsqrt(squares / (width * row_count) + EPSILON)[:, None]
    prompts, chunk = kv_cache.shape[1], kv_cache.shape[2]
    cache = kv_cache[0].reshape(prompts, chunk, 2, row_count, 2, HEAD_DIM)
    cache = lax.all_to_all(cache.transpose(3, 0, 2, 4, 1, 5), ROW, 0, 0)
    flat = gathered.reshape(col_count * rows, width)
    query_part = jnp.dot(flat, q_weight[0], preferred_element_type=F32).astype(BF)
    pair_part = jnp.dot(flat, kv_weight[0], preferred_element_type=F32).astype(BF)
    both = jnp.concatenate([query_part, pair_part], axis=1).reshape(col_count, rows, -1)
    both = lax.all_to_all(both, COL, 0, 0)
    query_blocks = both[:, :, :512].reshape(row_count, 4, rows, 512)
    pair_blocks = both[:, :, 512:].reshape(2, row_count, 2, rows, HEAD_DIM)
    pair_blocks = pair_blocks.transpose(1, 0, 2, 3, 4).reshape(row_count, 4, rows, HEAD_DIM)
    parts = jnp.concatenate([query_blocks, pair_blocks], axis=3)
    parts = lax.all_to_all(parts, ROW, 0, 0)
    attended, pairs = attend(lengths, parts, scale, cache)
    count = 8
    handed = lax.ppermute(attended[None], "z", [((i - 1) % count, i) for i in range(count)])
    pairs = lax.all_gather(pairs, ROW)
    new_kv = pairs.reshape(row_count, 2, 2, rows, HEAD_DIM).transpose(3, 1, 0, 2, 4)
    return (handed, new_kv.reshape(1, rows, -1))


def solution(mesh):
    fine = Mesh(mesh.devices.reshape(8, 2, 2, 2, 8), ("z", "xh", "co", "xl", "y"))
    return jax.shard_map(
        shards,
        mesh=fine,
        in_specs=(
            P("z", COL, ROW),
            P("z", ROW),
            P("z", ROW, COL),
            P("z", ROW, COL),
            P("z", COL, ROW, None, None),
            P("z", COL),
        ),
        out_specs=(P("z", COL, ROW), P("z", COL, None)),
        check_vma=False,
    )
```

time: 224 us -> 153 us (0.68)
  waiting for transfers between devices: 84.2 us -> 31.9 us
  between operations: 14.3 us -> 0.74 us
  other arithmetic: 13.7 us -> 2.17 us
  starting transfers between devices: 12.6 us -> 22.7 us
  local copies, waits for them, and re-layouts: 21.2 us -> 13.2 us
  blocking collectives: 70.7 us -> 75.7 us
  matrix products: 6.38 us -> 2.14 us
  Pallas kernels: 0 us -> 3.17 us
    all_gather x2 -> x0, waiting for transfers between devices: 64.8 us -> none  [the longest x1 64.8 us: shards(): lax.all_gather(normed.reshape(row_count, sub_rows, width_part), 'col', ax...]
    all_to_all x0 -> x1, blocking collectives: none -> 55.4 us  [shards(): lax.all_to_all(jnp.broadcast_to(sent[None], (col_count, rows, width)), CO...]
    psum x2 -> x1, blocking collectives: 55.3 us -> 12.2 us  [shards(): squares = lax.psum(jnp.sum(widened * widened, axis=1), ROW)]
    all_to_all x2 -> x3, waiting for transfers between devices: 14 us -> 31.2 us  [the longest x1 25.4 us: shards(): cache = lax.all_to_all(cache.transpose(3, 0, 2, 4, 1, 5), ROW, 0, 0)]
    all_to_all x2 -> x3, starting transfers between devices: 9.2 us -> 18.6 us  [the longest x1 7.74 us: shards(): cache = lax.all_to_all(cache.transpose(3, 0, 2, 4, 1, 5), ROW, 0, 0)]
    all_gather x2 -> x1, blocking collectives: 15.4 us -> 8.05 us  [shards(): pairs = lax.all_gather(pairs, ROW)]
    add x8 -> x0, other arithmetic: 6.09 us -> none  [the longest x3 6 us: join_parts(): former[2] * keep_former[..., None] + latter[2] * keep_latter[..., None]]
    ppermute x1, waiting for transfers between devices: 5.37 us -> 0.61 us  [shards(): lax.ppermute(attended[None], 'z', [((i - 1) % count, i) for i in range(co...]
  transfers between devices with their start and end apart: 5 -> 4, of which waited for: 4 -> 3; matrix products, arithmetic and copies ran while one was open for 7% -> 8% of each run, Pallas kernels for 0% -> 0%
where the time goes in v1:
time: 153 us; the launch traced here: 152 us
  blocking collectives  75.7 us (49%)
  waiting for transfers between devices  31.9 us (21%)
  starting transfers between devices  22.7 us (15%)
  local copies, waits for them, and re-layouts  13.2 us (9%)
  Pallas kernels  3.17 us (2%)
  other arithmetic  2.17 us (1%)
  matrix products  2.14 us (1%)
    all_to_all x1, blocking collectives, shards(): lax.all_to_all(jnp.broadcast_to(sent[None], (col_count, rows, width)), CO...  55.4 us
    all_to_all x1, waiting for transfers between devices, shards(): cache = lax.all_to_all(cache.transpose(3, 0, 2, 4, 1, 5), ROW, 0, 0)  25.4 us
    psum x1, blocking collectives, shards(): squares = lax.psum(jnp.sum(widened * widened, axis=1), ROW)  12.2 us
    all_gather x1, blocking collectives, shards(): pairs = lax.all_gather(pairs, ROW)  8.05 us
    all_to_all x1, starting transfers between devices, shards(): cache = lax.all_to_all(cache.transpose(3, 0, 2, 4, 1, 5), ROW, 0, 0)  7.74 us
    unnamed x8, local copies, waits for them, and re-layouts  6.78 us
    all_to_all x1, starting transfers between devices, shards(): both = lax.all_to_all(both, COL, 0, 0)  6.54 us
    all_to_all x1, waiting for transfers between devices, shards(): both = lax.all_to_all(both, COL, 0, 0)  5.83 us
  transfers between devices with their start and end apart: 4, of which 3 were waited for; matrix products, arithmetic and copies ran while one was open for 8% of the time, Pallas kernels for 0%

profile of v1, /device:TPU:1, one launch (start us, length us, event | category | flops | bytes accessed | tf_op | source)
XLA Modules:
  0.0 151.7 jit_solution(13784297019341192962)
XLA Ops:
  0.6 0.0 copy-start
  0.6 1.2 fusion.7
  1.8 0.2 broadcast_in_dim.15
  2.1 0.0 copy-start.2
  2.1 55.4 %all_to_all.20 = bf16[16,32,2048]{2,1,0:T(8,128)(2,1)S(1)} all-to-all(bf16[16,32,2048]{2,1,0:T(8,128)(2,1)S(1)} %broadcast_in_dim.15), channel_id=1, replica_groups=mesh['z'=8,'xh'=2,'co'=2,'xl'=2,'y'=8] {'xl','y'}, dimensions={0} | all-to-all | bytes 4194304 | tf_op jit(solution)/shard_map/all_to_all | solution.py:97
  57.6 0.0 copy-done.2
  57.6 0.8 convolution_convert_fusion
  58.4 0.0 copy-done
  58.4 1.3 fusion.2
  59.8 1.1 copy.17
  60.9 6.5 %all-to-all-start.1 = ((bf16[16,32,640]{2,1,0:T(8,128)(2,1)}), bf16[16,32,640]{2,1,0:T(8,128)(2,1)S(1)}, u32[]{:S(2)}, u32[]{:S(2)}) async-start(bf16[16,32,640]{2,1,0:T(8,128)(2,1)} %bitcast.5), calls=%async_computation.1 | async-start | bytes 1310720 | tf_op jit(solution)/shard_map/all_to_all | solution.py:109
  67.4 6.1 %copy.19 = bf16[1,2,256,2,1024]{2,4,3,1,0:T(8,128)(2,1)} copy(bf16[1,2,256,2,1024]{4,3,2,1,0:T(2,128)(2,1)} %param.10) | data formatting | bytes 4194304 | tf_op args[4]
  73.5 4.1 %copy.20 = bf16[2,256,2,4,2,128]{5,1,4,2,0,3:T(8,128)(2,1)} copy(bf16[2,256,2,4,2,128]{1,5,4,3,2,0:T(8,128)(2,1)} %bitcast.32) | data formatting | bytes 4194304 | tf_op jit(solution)/shard_map/reshape;squeeze | solution.py:103
  77.6 5.8 %all-to-all-done.1 = bf16[16,32,640]{2,1,0:T(8,128)(2,1)S(1)} async-done(((bf16[16,32,640]{2,1,0:T(8,128)(2,1)}), bf16[16,32,640]{2,1,0:T(8,128)(2,1)S(1)}, u32[]{:S(2)}, u32[]{:S(2)}) %all-to-all-start.1) | async-done | bytes 655392 | tf_op jit(solution)/shard_map/all_to_all | solution.py:109
  83.5 7.7 %all-to-all-start.3 = ((bf16[4,2,2,2,256,128]{5,4,3,2,1,0:T(8,128)(2,1)}), bf16[4,2,2,2,256,128]{5,4,3,2,1,0:T(8,128)(2,1)}, u32[]{:S(2)}, u32[]{:S(2)}) async-start(bf16[4,2,2,2,256,128]{5,4,3,2,1,0:T(8,128)(2,1)} %bitcast.29), calls=%async_computation.3 | async-start | bytes 4194304 | tf_op jit(solution)/shard_map/all_to_all | solution.py:104
  91.2 0.0 copy-start.1
  91.3 0.9 pad_maximum_fusion.1
  92.2 25.4 %all-to-all-done.3.cache_ref = bf16[4,2,2,2,256,128]{5,4,3,2,1,0:T(8,128)(2,1)} async-done(((bf16[4,2,2,2,256,128]{5,4,3,2,1,0:T(8,128)(2,1)}), bf16[4,2,2,2,256,128]{5,4,3,2,1,0:T(8,128)(2,1)}, u32[]{:S(2)}, u32[]{:S(2)}) %all-to-all-start.3) | async-done | bytes 2097184 | tf_op jit(solution)/shard_map/all_to_all | solution.py:104
  117.7 4.3 %all-to-all-start.2 = ((bf16[4,4,32,640]{3,2,1,0:T(8,128)(2,1)}), bf16[4,4,32,640]{3,2,1,0:T(8,128)(2,1)S(1)}, u32[]{:S(2)}, u32[]{:S(2)}) async-start(bf16[4,4,32,640]{3,2,1,0:T(8,128)(2,1)} %pad_maximum_fusion.1), calls=%async_computation.2 | async-start | bytes 1310720 | tf_op jit(solution)/shard_map/all_to_all | solution.py:114
  122.0 12.2 %psum.7 = f32[32]{0:T(128)S(1)} all-reduce(f32[32]{0:T(128)S(1)} %get-tuple-element.6), channel_id=1, replica_groups=mesh['z'=8,'xh'=2,'co'=2,'xl'=2,'y'=8] {'xh','co'}, use_global_device_ids=true, to_apply=%region_1.0 | all-reduce | flops 32 | bytes 256 | tf_op jit(solution)/shard_map/psum | solution.py:100
  134.2 0.1 copy.21.scale_ref
  134.3 0.0 all-to-all-done.2.parts_ref
  134.3 0.0 copy-done.1
  134.3 3.2 %attend.1 = (bf16[32,2048]{1,0:T(8,128)(2,1)S(1)}, bf16[4,32,128]{2,1,0:T(8,128)(2,1)S(1)}) custom-call(s32[1,2]{1,0:T(1,128)S(1)} %copy-done.1, bf16[4,4,32,640]{3,2,1,0:T(8,128)(2,1)S(1)} %all-to-all-done.2.parts_ref, f32[32,1]{1,0:T(8,128)S(1)} %copy.21.scale_ref, bf16[4,2,2,2,256,128]{5,4,3,2,1,0:T(8,128)(2,1)} %all-to-all-done.3.cache_ref), custom_call_target="tpu_custom_call" | custom-call | tf_op jit(solution)/shard_map/attend/pallas_call | solution.py:77
  137.5 4.0 %collective-permute-start = (bf16[1,32,2048]{2,1,0:T(8,128)(2,1)S(1)}, bf16[1,32,2048]{2,1,0:T(8,128)(2,1)S(1)}, u32[]{:S(2)}, u32[]{:S(2)}) collective-permute-start(bf16[1,32,2048]{2,1,0:T(8,128)(2,1)S(1)} %bitcast.28), channel_id=1, source_target_pairs={{448,0},{0,64},{64,128},{128,192},{192,256},{256,320},{320,384},{3... | collective-permute-start | bytes 393224 | tf_op jit(solution)/shard_map/ppermute | solution.py:117
  141.5 8.1 %all-gather = bf16[16,32,128]{2,1,0:T(8,128)(2,1)S(1)} all-gather(bf16[4,32,128]{2,1,0:T(8,128)(2,1)S(1)} %get-tuple-element.5), channel_id=2, replica_groups=mesh['z'=8,'xh'=2,'co'=2,'xl'=2,'y'=8] {'xh','co'}, dimensions={0}, use_global_device_ids=true | all-gather | bytes 163840 | tf_op jit(solution)/shard_map/all_gather | solution.py:118
  149.6 0.1 copy.22
  149.7 0.7 reshape.39
  150.4 0.6 collective-permute-done
  151.0 0.7 copy.24
  (5 shorter events, 0.1 us)
Async XLA Ops:
  0.6 57.8 %copy-start = (bf16[1,2048,512]{2,1,0:T(8,128)(2,1)S(1)}, bf16[1,2048,512]{2,1,0:T(8,128)(2,1)}, u32[]{:S(2)}) copy-start(bf16[1,2048,512]{2,1,0:T(8,128)(2,1)} %param.8) | copy-start | bytes 6291460
  2.1 55.5 %copy-start.2 = (bf16[1,2048,128]{2,1,0:T(8,128)(2,1)S(1)}, bf16[1,2048,128]{2,1,0:T(8,128)(2,1)}, u32[]{:S(2)}) copy-start(bf16[1,2048,128]{2,1,0:T(8,128)(2,1)} %param.9) | copy-start | bytes 1572868
  60.9 22.6 %all-to-all-start.1 = ((bf16[16,32,640]{2,1,0:T(8,128)(2,1)}), bf16[16,32,640]{2,1,0:T(8,128)(2,1)S(1)}, u32[]{:S(2)}, u32[]{:S(2)}) async-start(bf16[16,32,640]{2,1,0:T(8,128)(2,1)} %bitcast.5), calls=%async_computation.1 | async-start | bytes 1310720 | tf_op jit(solution)/shard_map/all_to_all | solution.py:109
  83.5 34.2 %all-to-all-start.3 = ((bf16[4,2,2,2,256,128]{5,4,3,2,1,0:T(8,128)(2,1)}), bf16[4,2,2,2,256,128]{5,4,3,2,1,0:T(8,128)(2,1)}, u32[]{:S(2)}, u32[]{:S(2)}) async-start(bf16[4,2,2,2,256,128]{5,4,3,2,1,0:T(8,128)(2,1)} %bitcast.29), calls=%async_computation.3 | async-start | bytes 4194304 | tf_op jit(solution)/shard_map/all_to_all | solution.py:104
  91.2 43.1 %copy-start.1 = (s32[1,2]{1,0:T(1,128)S(1)}, s32[1,2]{1,0:T(1,128)}, u32[]{:S(2)}) copy-start(s32[1,2]{1,0:T(1,128)} %lengths_ref.1) | copy-start | bytes 28
  117.7 16.6 %all-to-all-start.2 = ((bf16[4,4,32,640]{3,2,1,0:T(8,128)(2,1)}), bf16[4,4,32,640]{3,2,1,0:T(8,128)(2,1)S(1)}, u32[]{:S(2)}, u32[]{:S(2)}) async-start(bf16[4,4,32,640]{3,2,1,0:T(8,128)(2,1)} %pad_maximum_fusion.1), calls=%async_computation.2 | async-start | bytes 1310720 | tf_op jit(solution)/shard_map/all_to_all | solution.py:114
  137.5 13.6 %collective-permute-start = (bf16[1,32,2048]{2,1,0:T(8,128)(2,1)S(1)}, bf16[1,32,2048]{2,1,0:T(8,128)(2,1)S(1)}, u32[]{:S(2)}, u32[]{:S(2)}) collective-permute-start(bf16[1,32,2048]{2,1,0:T(8,128)(2,1)S(1)} %bitcast.28), channel_id=1, source_target_pairs={{448,0},{0,64},{64,128},{128,192},{192,256},{256,320},{320,384},{3... | collective-permute-start | bytes 393224 | tf_op jit(solution)/shard_map/ppermute | solution.py:117

commit v2 on v1

v2 whole, which is shorter than its diff:
```python
import jax
import jax.numpy as jnp
from jax import lax
from jax.experimental import pallas as pl
from jax.experimental.pallas import tpu as pltpu
from jax.sharding import Mesh
from jax.sharding import PartitionSpec as P

HEAD_DIM = 128
EPSILON = 1e-05
FLOOR = -1e30
ROW = ("xh", "co")
COL = ("xl", "y")
BF = jnp.bfloat16
F32 = jnp.float32
VMEM = pl.BlockSpec(memory_space=pltpu.VMEM)
SMEM = pl.BlockSpec(memory_space=pltpu.SMEM)
PARAMS = pltpu.CompilerParams(vmem_limit_bytes=40 * 1024 * 1024)


def project_kernel(place_ref, ring_ref, direct_ref, query_ref, pair_ref, out_ref):
    count, rows, width = ring_ref.shape
    half = rows // 2
    mine = place_ref[0] * count
    other = (1 - place_ref[0]) * count
    own = ring_ref[...].reshape(count * rows, width)
    theirs = direct_ref[...].reshape(count * rows, width)

    def store(block, start, lanes):
        block = block.astype(BF).reshape(count, 2, half, block.shape[1])
        for h in range(2):
            out_ref[h, pl.ds(start, count), :, lanes] = block[:, h]

    for weight_ref, lanes in ((query_ref, slice(0, 512)), (pair_ref, slice(512, 640))):
        store(jnp.dot(theirs, weight_ref[...], preferred_element_type=F32), other, lanes)
        store(jnp.dot(own, weight_ref[...], preferred_element_type=F32), mine, lanes)


def project(place, ring, direct, query_weight, pair_weight):
    return pl.pallas_call(
        project_kernel,
        out_shape=jax.ShapeDtypeStruct((2, 16, 16, 640), BF),
        in_specs=[SMEM, VMEM, VMEM, VMEM, VMEM],
        out_specs=VMEM,
        compiler_params=PARAMS,
        name="project",
    )(place, ring, direct, query_weight, pair_weight)


def attend_kernel(lengths_ref, place_ref, parts_ref, scale_ref, *refs):
    caches, out_ref, pair_ref = refs[:4], refs[4], refs[5]
    _, prompts, blocks, samples, _ = parts_ref.shape
    _, _, heads, chunk, dim = caches[0].shape
    per_block = 512 // dim
    factor = dim**-0.5
    place = place_ref[0]
    for p in range(prompts):
        length = lengths_ref[0, p]
        here = slice(p * samples, (p + 1) * samples)
        scale = scale_ref[here]
        total = []
        for j in range(blocks):
            part = parts_ref[0, p, j].astype(F32) + parts_ref[1, p, j].astype(F32)
            total.append((part * scale).astype(BF))
            pair_ref[j, here] = total[j][:, 512:]
        for g in range(heads):
            names = [(j, h) for j in (2 * g, 2 * g + 1) for h in range(per_block)]
            query = jnp.concatenate([total[j][:, h * dim : (h + 1) * dim] for j, h in names], axis=0)
            new_key = jnp.concatenate([total[g][:, 512:].astype(F32)] * len(names), axis=0)
            new_value = jnp.concatenate([total[2 + g][:, 512:].astype(F32)] * len(names), axis=0)
            own = jnp.sum(query.astype(F32) * new_key, axis=1, keepdims=True) * factor
            scores = []
            top = own
            for k in range(len(caches)):
                block = lax.dot_general(
                    query, caches[k][p, 0, g], (((1,), (1,)), ((), ())), preferred_element_type=F32
                )
                first = lax.rem(place + len(caches) - k, len(caches)) * chunk
                position = first + lax.broadcasted_iota(jnp.int32, block.shape, 1)
                block = jnp.where(position < length, block * factor, FLOOR)
                top = jnp.maximum(top, jnp.max(block, axis=1, keepdims=True))
                scores.append(block)
            own_weight = jnp.exp(own - top)
            weight_sum = own_weight
            value = own_weight.astype(BF).astype(F32) * new_value
            for k in range(len(caches)):
                weight = jnp.exp(scores[k] - top)
                weight_sum = weight_sum + jnp.sum(weight, axis=1, keepdims=True)
                value = value + jnp.dot(
                    weight.astype(BF), caches[k][p, 1, g], preferred_element_type=F32
                )
            result = (value / weight_sum).astype(BF)
            for n, (j, h) in enumerate(names):
                at = (j * per_block + h) * dim
                out_ref[here, at : at + dim] = result[n * samples : (n + 1) * samples]


def attend(lengths, place, parts, scale, caches):
    rows = parts.shape[1] * parts.shape[3]
    return pl.pallas_call(
        attend_kernel,
        out_shape=(
            jax.ShapeDtypeStruct((rows, 2048), BF),
            jax.ShapeDtypeStruct((4, rows, HEAD_DIM), BF),
        ),
        in_specs=[SMEM, SMEM] + [VMEM] * 6,
        out_specs=(VMEM, VMEM),
        compiler_params=PARAMS,
        name="attend",
    )(lengths, place, parts, scale, *caches)


def shards(hidden_in, norm_gain, q_weight, kv_weight, kv_cache, lengths):
    rows, width = hidden_in.shape[1:]
    row_count = 4
    row_index = lax.axis_index(ROW)
    widened = hidden_in[0].astype(F32)
    sent = (widened * norm_gain[0][None, :]).astype(BF)
    local_squares = jnp.sum(widened * widened, axis=1)

    ring = lax.all_gather(sent, "y")
    theirs = lax.ppermute(sent, "xl", [(0, 1), (1, 0)])
    direct = lax.all_to_all(jnp.broadcast_to(theirs[None], (8, rows, width)), "y", 0, 0)

    prompts, chunk = kv_cache.shape[1], kv_cache.shape[2]
    cache = kv_cache[0].reshape(prompts, chunk, 2, row_count, 2, HEAD_DIM).transpose(3, 0, 2, 4, 1, 5)
    caches = []
    for k in range(row_count):
        piece = lax.dynamic_index_in_dim(cache, (row_index + k) % row_count, 0, keepdims=False)
        if k:
            piece = lax.ppermute(piece, ROW, [(i, (i + k) % row_count) for i in range(row_count)])
        caches.append(piece)
    ring, direct, caches = lax.optimization_barrier((ring, direct, caches))

    partial = project(lax.axis_index("xl")[None], ring, direct, q_weight[0], kv_weight[0])
    partial = lax.all_to_all(partial, "co", 0, 0)
    both = (partial[0].astype(F32) + partial[1].astype(F32)).astype(BF)
    both = lax.all_to_all(both, COL, 0, 0)
    samples = both.shape[1]
    query_blocks = both[:, :, :512].reshape(row_count, 4, samples, 512)
    pair_blocks = both[:, :, 512:].reshape(2, row_count, 2, samples, HEAD_DIM)
    pair_blocks = pair_blocks.transpose(1, 0, 2, 3, 4).reshape(row_count, 4, samples, HEAD_DIM)
    parts = jnp.concatenate([query_blocks, pair_blocks], axis=3)
    parts = lax.all_to_all(parts, ROW, 0, 0).reshape((2, 2) + parts.shape[1:])

    squares = lax.psum(local_squares, ROW)
    scale = lax.rsqrt(squares / (width * row_count) + EPSILON)[:, None]
    attended, pairs = attend(lengths, row_index[None], parts, scale, caches)
    count = 8
    handed = lax.ppermute(attended[None], "z", [((i - 1) % count, i) for i in range(count)])
    pairs = lax.all_gather(pairs, ROW)
    new_kv = pairs.reshape(row_count, 2, 2, rows, HEAD_DIM).transpose(3, 1, 0, 2, 4)
    return (handed, new_kv.reshape(1, rows, -1))


def solution(mesh):
    fine = Mesh(mesh.devices.reshape(8, 2, 2, 2, 8), ("z", "xh", "co", "xl", "y"))
    return jax.shard_map(
        shards,
        mesh=fine,
        in_specs=(
            P("z", COL, ROW),
            P("z", ROW),
            P("z", ROW, COL),
            P("z", ROW, COL),
            P("z", COL, ROW, None, None),
            P("z", COL),
        ),
        out_specs=(P("z", COL, ROW), P("z", COL, None)),
        check_vma=False,
    )
```

time: 153 us -> 129 us (0.84)
  blocking collectives: 75.7 us -> 38.3 us
  waiting for transfers between devices: 31.9 us -> 15 us
  between operations: 0.74 us -> 14.2 us
  starting transfers between devices: 22.7 us -> 33.4 us
  local copies, waits for them, and re-layouts: 13.2 us -> 19.4 us
  matrix products: 2.14 us -> 0 us
  Pallas kernels: 3.17 us -> 4.74 us
    all_to_all x1 -> x2, blocking collectives: 55.4 us -> 20.8 us  [the longest x1 14.5 us: shards(): both = lax.all_to_all(both, COL, 0, 0)]
    all_to_all x3 -> x2, waiting for transfers between devices: 31.2 us -> 0.01 us  [the longest x1 0.01 us: shards(): lax.all_to_all(jnp.broadcast_to(theirs[None], (8, rows, width)), 'y', 0, 0)]
    ppermute x0 -> x4, starting transfers between devices: none -> 16 us  [the longest x3 12 us: shards(): lax.ppermute(piece, ROW, [(i, (i + k) % row_count) for i in range(row_cou...]
    ppermute x0 -> x4, waiting for transfers between devices: none -> 14.4 us  [the longest x3 13.7 us: shards(): lax.ppermute(piece, ROW, [(i, (i + k) % row_count) for i in range(row_cou...]
    unnamed x8 -> x16, local copies, waits for them, and re-layouts: 6.78 us -> 16 us
    all_to_all x3 -> x2, starting transfers between devices: 18.6 us -> 13.5 us  [the longest x1 7.61 us: shards(): lax.all_to_all(jnp.broadcast_to(theirs[None], (8, rows, width)), 'y', 0, 0)]
    psum x1, blocking collectives: 12.2 us -> 8.68 us  [shards(): squares = lax.psum(local_squares, ROW)]
    another operation x1, local copies, waits for them, and re-layouts: 4.13 us -> 1.35 us  [shards(): cache = kv_cache[0].reshape(prompts, chunk, 2, row_count, 2, HEAD_DIM)]
  transfers between devices with their start and end apart: 4 -> 8, of which waited for: 3 -> 4; matrix products, arithmetic and copies ran while one was open for 8% -> 14% of each run, Pallas kernels for 0% -> 0%
where the time goes in v2:
time: 129 us
  blocking collectives  38.3 us (30%)
  starting transfers between devices  33.4 us (26%)
  local copies, waits for them, and re-layouts  19.4 us (15%)
  waiting for transfers between devices  15 us (12%)
  between operations  14.2 us (11%)
  Pallas kernels  4.74 us (4%)
  other arithmetic  3.5 us (3%)
    unnamed x16, local copies, waits for them, and re-layouts  16 us
    all_to_all x1, blocking collectives, shards(): both = lax.all_to_all(both, COL, 0, 0)  14.5 us
    ppermute x3, waiting for transfers between devices, shards(): lax.ppermute(piece, ROW, [(i, (i + k) % row_count) for i in range(row_cou...  13.7 us
    ppermute x3, starting transfers between devices, shards(): lax.ppermute(piece, ROW, [(i, (i + k) % row_count) for i in range(row_cou...  12 us
    all_gather x1, blocking collectives, shards(): pairs = lax.all_gather(pairs, ROW)  8.78 us
    psum x1, blocking collectives, shards(): squares = lax.psum(local_squares, ROW)  8.68 us
    all_to_all x1, starting transfers between devices, shards(): lax.all_to_all(jnp.broadcast_to(theirs[None], (8, rows, width)), 'y', 0, 0)  7.61 us
    all_to_all x1, blocking collectives, shards(): partial = lax.all_to_all(partial, 'co', 0, 0)  6.3 us
  transfers between devices with their start and end apart: 8, of which 4 were waited for; matrix products, arithmetic and copies ran while one was open for 14% of the time, Pallas kernels for 0%

profile of v2, /device:TPU:1, one launch (start us, length us, event | category | flops | bytes accessed | tf_op | source)
XLA Modules:
  0.0 128.5 jit_solution(18335852233271688118)
XLA Ops:
  7.2 0.0 all-gather.3.cloned.1.call-start
  7.2 1.1 fusion.4
  8.3 3.9 %collective-permute-start = (bf16[32,2048]{1,0:T(8,128)(2,1)S(1)}, bf16[32,2048]{1,0:T(8,128)(2,1)S(1)}, u32[]{:S(2)}, u32[]{:S(2)}) collective-permute-start(bf16[32,2048]{1,0:T(8,128)(2,1)S(1)} %get-tuple-element.23), channel_id=1, source_target_pairs={{0,8},{8,0},{1,9},{9,1},{2,10},{10,2},{3,11},{11,3},{4,12},{12,4},... | collective-permute-start | bytes 393224 | tf_op jit(solution)/shard_map/ppermute | solution.py:122
  12.2 1.6 %fusion.5 = bf16[1,32,2048]{2,1,0:T(8,128)(2,1)} fusion(bf16[1,32,2048]{2,1,0:T(8,128)(2,1)} %param.6, f32[2048]{0:T(1024)} %bitcast.56), kind=kLoop, calls=%fused_computation.9 | loop fusion | flops 196608 | bytes 270336 | tf_op jit(solution)/shard_map/convert_element_type | solution.py:118
  13.8 0.0 all-gather.3.cloned.1.call-update
  13.8 0.7 collective-permute-done
  14.6 1.1 broadcast_in_dim.20
  15.7 7.6 %all-to-all-start = ((bf16[8,32,2048]{2,1,0:T(8,128)(2,1)}), bf16[8,32,2048]{2,1,0:T(8,128)(2,1)S(1)}, u32[]{:S(2)}, u32[]{:S(2)}) async-start(bf16[8,32,2048]{2,1,0:T(8,128)(2,1)} %broadcast_in_dim.20), calls=%async_computation | async-start | bytes 2097152 | tf_op jit(solution)/shard_map/all_to_all | solution.py:123
  23.3 4.7 %copy.19 = bf16[1,2,256,2,1024]{2,4,3,1,0:T(8,128)(2,1)S(1)} copy(bf16[1,2,256,2,1024]{4,3,2,1,0:T(2,128)(2,1)} %param.10) | data formatting | bytes 4194304 | tf_op args[4]
  28.0 1.4 %constant_dynamic-slice_fusion = (bf16[2,256,2,1,2,128]{1,5,4,3,2,0:T(8,128)(2,1)}, bf16[2,256,2,1,2,128]{1,5,4,3,2,0:T(8,128)(2,1)}, bf16[2,256,2,1,2,128]{1,5,...) fusion(bf16[2,256,2,4,2,128]{1,5,4,3,2,0:T(8,128)(2,1)S(1)} %bitcast.47, s32[]{:T(128)S(6)} %select_n.39, s32[]{:T(128)S(6)} %select_n.37, ...), kind=kLoop, calls=%fused_computation.10 | loop fusion | bytes 4194320 | tf_op jit(solution)/shard_map/dynamic-slice.3
  29.4 0.0 copy-start
  29.4 2.2 %copy.28 = bf16[2,256,2,1,2,128]{5,1,4,2,0,3:T(8,128)(2,1)} copy(bf16[2,256,2,1,2,128]{1,5,4,3,2,0:T(8,128)(2,1)} %get-tuple-element.20) | data formatting | bytes 1048576
  31.5 6.4 %collective-permute-start.1 = (bf16[2,2,2,256,128]{4,3,2,1,0:T(8,128)(2,1)}, bf16[2,2,2,256,128]{4,3,2,1,0:T(8,128)(2,1)}, u32[]{:S(2)}, u32[]{:S(2)}) collective-permute-start(bf16[2,2,2,256,128]{4,3,2,1,0:T(8,128)(2,1)} %bitcast.50), channel_id=1, source_target_pairs={{0,16},{16,32},{32,48},{48,0},{1,17},{17,33},{33,49},{49,1},{2,18}... | collective-permute-start | bytes 1572872 | tf_op jit(solution)/shard_map/ppermute | solution.py:131
  37.9 2.1 %copy.29 = bf16[2,256,2,1,2,128]{5,1,4,2,0,3:T(8,128)(2,1)} copy(bf16[2,256,2,1,2,128]{1,5,4,3,2,0:T(8,128)(2,1)} %get-tuple-element.19) | data formatting | bytes 1048576
  40.0 3.8 %collective-permute-start.2 = (bf16[2,2,2,256,128]{4,3,2,1,0:T(8,128)(2,1)}, bf16[2,2,2,256,128]{4,3,2,1,0:T(8,128)(2,1)}, u32[]{:S(2)}, u32[]{:S(2)}) collective-permute-start(bf16[2,2,2,256,128]{4,3,2,1,0:T(8,128)(2,1)} %bitcast.51), channel_id=1, source_target_pairs={{0,32},{16,48},{32,0},{48,16},{1,33},{17,49},{33,1},{49,17},{2,34}... | collective-permute-start | bytes 1572872 | tf_op jit(solution)/shard_map/ppermute | solution.py:131
  43.7 2.1 %copy.30 = bf16[2,256,2,1,2,128]{5,1,4,2,0,3:T(8,128)(2,1)} copy(bf16[2,256,2,1,2,128]{1,5,4,3,2,0:T(8,128)(2,1)} %get-tuple-element.18) | data formatting | bytes 1048576
  45.8 1.9 %collective-permute-start.3 = (bf16[2,2,2,256,128]{4,3,2,1,0:T(8,128)(2,1)}, bf16[2,2,2,256,128]{4,3,2,1,0:T(8,128)(2,1)}, u32[]{:S(2)}, u32[]{:S(2)}) collective-permute-start(bf16[2,2,2,256,128]{4,3,2,1,0:T(8,128)(2,1)} %bitcast.52), channel_id=1, source_target_pairs={{0,48},{16,0},{32,16},{48,32},{1,49},{17,1},{33,17},{49,33},{2,50}... | collective-permute-start | bytes 1572872 | tf_op jit(solution)/shard_map/ppermute | solution.py:131
  47.7 2.0 %copy.27 = bf16[2,256,2,1,2,128]{5,1,4,2,0,3:T(8,128)(2,1)} copy(bf16[2,256,2,1,2,128]{1,5,4,3,2,0:T(8,128)(2,1)} %get-tuple-element.21) | data formatting | bytes 1048576
  49.8 0.0 collective-permute-done.1.refs_1_
  49.8 9.2 %collective-permute-done.2.refs_2_ = bf16[2,2,2,256,128]{4,3,2,1,0:T(8,128)(2,1)} collective-permute-done((bf16[2,2,2,256,128]{4,3,2,1,0:T(8,128)(2,1)}, bf16[2,2,2,256,128]{4,3,2,1,0:T(8,128)(2,1)}, u32[]{:S(2)}, u32[]{:S(2)}) %collective-permute-start.2) | collective-permute-done | bytes 524320 | tf_op jit(solution)/shard_map/ppermute | solution.py:131
  59.0 4.5 %collective-permute-done.3.refs_3_ = bf16[2,2,2,256,128]{4,3,2,1,0:T(8,128)(2,1)} collective-permute-done((bf16[2,2,2,256,128]{4,3,2,1,0:T(8,128)(2,1)}, bf16[2,2,2,256,128]{4,3,2,1,0:T(8,128)(2,1)}, u32[]{:S(2)}, u32[]{:S(2)}) %collective-permute-start.3) | collective-permute-done | bytes 524320 | tf_op jit(solution)/shard_map/ppermute | solution.py:131
  63.5 0.6 all-gather.3.cloned.1.call-done.ring_ref
  64.0 0.0 all-to-all-done.direct_ref
  64.0 0.0 copy-done
  64.0 0.0 copy-start.2
  64.0 1.2 copy-done.2
  65.3 0.0 copy-start.3
  65.3 1.0 copy-done.3
  66.3 1.8 %project.1 = bf16[2,16,16,640]{3,2,1,0:T(8,128)(2,1)S(1)} custom-call(s32[1]{0:T(128)} %bitcast.1.place_ref, bf16[8,32,2048]{2,1,0:T(8,128)(2,1)S(1)} %copy-done.2, bf16[8,32,2048]{2,1,0:T(8,128)(2,1)S(1)} %all-to-all-done.direct_ref, bf16[2048,512]{1,0:T(8,128)(2,1)S(1)} %bitcast.42, bf16[2048,128]{1,0:T(8,128)(2,1)S(1)} %bitcast.45), custom_call_target="tpu_custom_call" | custom-call | tf_op jit(solution)/shard_map/project/pallas_call | solution.py:40
  68.1 6.3 %all_to_all.20 = bf16[2,16,16,640]{3,2,1,0:T(8,128)(2,1)S(1)} all-to-all(bf16[2,16,16,640]{3,2,1,0:T(8,128)(2,1)S(1)} %project.1), channel_id=1, replica_groups=mesh['z'=8,'xh'=2,'co'=2,'xl'=2,'y'=8] {'co'}, dimensions={0} | all-to-all | bytes 1310720 | tf_op jit(solution)/shard_map/all_to_all | solution.py:136
  74.4 0.0 copy-start.1
  74.4 0.0 copy-start.4
  74.4 0.1 fusion.2
  74.5 14.5 %all_to_all.21 = bf16[16,16,640]{2,1,0:T(8,128)(2,1)S(1)} all-to-all(bf16[16,16,640]{2,1,0:T(8,128)(2,1)S(1)} %fusion.2), channel_id=1, replica_groups=mesh['z'=8,'xh'=2,'co'=2,'xl'=2,'y'=8] {'xl','y'}, dimensions={0} | all-to-all | bytes 655360 | tf_op jit(solution)/shard_map/all_to_all | solution.py:138
  89.1 0.8 pad_maximum_fusion
  89.8 5.9 %all-to-all-start.3 = ((bf16[4,4,16,640]{3,2,1,0:T(8,128)(2,1)}), bf16[4,4,16,640]{3,2,1,0:T(8,128)(2,1)S(1)}, u32[]{:S(2)}, u32[]{:S(2)}) async-start(bf16[4,4,16,640]{3,2,1,0:T(8,128)(2,1)} %pad_maximum_fusion), calls=%async_computation.3 | async-start | bytes 655360 | tf_op jit(solution)/shard_map/all_to_all | solution.py:144
  95.7 8.7 %psum.7 = f32[32]{0:T(128)S(1)} all-reduce(f32[32]{0:T(128)S(1)} %get-tuple-element.22), channel_id=1, replica_groups=mesh['z'=8,'xh'=2,'co'=2,'xl'=2,'y'=8] {'xh','co'}, use_global_device_ids=true, to_apply=%region_1.2 | all-reduce | flops 32 | bytes 256 | tf_op jit(solution)/shard_map/psum | solution.py:146
  104.4 0.1 copy.25.scale_ref
  104.5 0.0 all-to-all-done.3
  104.5 0.0 copy-done.1
  104.5 0.0 copy-done.4
  104.5 2.9 %attend.1 = (bf16[32,2048]{1,0:T(8,128)(2,1)S(1)}, bf16[4,32,128]{2,1,0:T(8,128)(2,1)S(1)}) custom-call(s32[1,2]{1,0:T(1,128)S(1)} %copy-done.4, s32[1]{0:T(128)} %bitcast.place_ref, bf16[2,2,4,16,640]{4,3,2,1,0:T(8,128)(2,1)S(1)} %bitcast.44, f32[32,1]{1,0:T(8,128)S(1)} %copy.25.scale_ref, bf16[2,2,2,256,128]{4,3,2,1,0:T(8,128)(2,1)S(1)} %bitcast.43, ...), custom_call_target="tpu_custom_call" | custom-call | tf_op jit(solution)/shard_map/attend/pallas_call | solution.py:100
  107.5 3.9 %collective-permute-start.4 = (bf16[1,32,2048]{2,1,0:T(8,128)(2,1)S(1)}, bf16[1,32,2048]{2,1,0:T(8,128)(2,1)S(1)}, u32[]{:S(2)}, u32[]{:S(2)}) collective-permute-start(bf16[1,32,2048]{2,1,0:T(8,128)(2,1)S(1)} %bitcast.46), channel_id=1, source_target_pairs={{448,0},{0,64},{64,128},{128,192},{192,256},{256,320},{320,384},{3... | collective-permute-start | bytes 393224 | tf_op jit(solution)/shard_map/ppermute | solution.py:150
  111.4 8.8 %all-gather = bf16[16,32,128]{2,1,0:T(8,128)(2,1)S(1)} all-gather(bf16[4,32,128]{2,1,0:T(8,128)(2,1)S(1)} %get-tuple-element.17), channel_id=2, replica_groups=mesh['z'=8,'xh'=2,'co'=2,'xl'=2,'y'=8] {'xh','co'}, dimensions={0}, use_global_device_ids=true | all-gather | bytes 163840 | tf_op jit(solution)/shard_map/all_gather | solution.py:151
  120.2 0.1 copy.26
  120.3 0.7 reshape.40
  121.0 0.0 collective-permute-done.4
  121.0 0.7 copy.32
  (4 shorter events, 0.0 us)
Async XLA Ops:
  7.2 56.9 %all-gather.3.cloned.1.call-start = ((), (), s32[]{:S(2)}) async-start(), calls=%async_computation.4 | async-start | bytes 1179648 | tf_op jit(solution)/shard_map/all_gather | solution.py:121
  8.3 6.3 %collective-permute-start = (bf16[32,2048]{1,0:T(8,128)(2,1)S(1)}, bf16[32,2048]{1,0:T(8,128)(2,1)S(1)}, u32[]{:S(2)}, u32[]{:S(2)}) collective-permute-start(bf16[32,2048]{1,0:T(8,128)(2,1)S(1)} %get-tuple-element.23), channel_id=1, source_target_pairs={{0,8},{8,0},{1,9},{9,1},{2,10},{10,2},{3,11},{11,3},{4,12},{12,4},... | collective-permute-start | bytes 393224 | tf_op jit(solution)/shard_map/ppermute | solution.py:122
  15.7 48.4 %all-to-all-start = ((bf16[8,32,2048]{2,1,0:T(8,128)(2,1)}), bf16[8,32,2048]{2,1,0:T(8,128)(2,1)S(1)}, u32[]{:S(2)}, u32[]{:S(2)}) async-start(bf16[8,32,2048]{2,1,0:T(8,128)(2,1)} %broadcast_in_dim.20), calls=%async_computation | async-start | bytes 2097152 | tf_op jit(solution)/shard_map/all_to_all | solution.py:123
  29.4 34.7 %copy-start = (bf16[1,2048,512]{2,1,0:T(8,128)(2,1)S(1)}, bf16[1,2048,512]{2,1,0:T(8,128)(2,1)}, u32[]{:S(2)}) copy-start(bf16[1,2048,512]{2,1,0:T(8,128)(2,1)} %param.8) | copy-start | bytes 6291460
  31.5 18.2 %collective-permute-start.1 = (bf16[2,2,2,256,128]{4,3,2,1,0:T(8,128)(2,1)}, bf16[2,2,2,256,128]{4,3,2,1,0:T(8,128)(2,1)}, u32[]{:S(2)}, u32[]{:S(2)}) collective-permute-start(bf16[2,2,2,256,128]{4,3,2,1,0:T(8,128)(2,1)} %bitcast.50), channel_id=1, source_target_pairs={{0,16},{16,32},{32,48},{48,0},{1,17},{17,33},{33,49},{49,1},{2,18}... | collective-permute-start | bytes 1572872 | tf_op jit(solution)/shard_map/ppermute | solution.py:131
  40.0 19.0 %collective-permute-start.2 = (bf16[2,2,2,256,128]{4,3,2,1,0:T(8,128)(2,1)}, bf16[2,2,2,256,128]{4,3,2,1,0:T(8,128)(2,1)}, u32[]{:S(2)}, u32[]{:S(2)}) collective-permute-start(bf16[2,2,2,256,128]{4,3,2,1,0:T(8,128)(2,1)} %bitcast.51), channel_id=1, source_target_pairs={{0,32},{16,48},{32,0},{48,16},{1,33},{17,49},{33,1},{49,17},{2,34}... | collective-permute-start | bytes 1572872 | tf_op jit(solution)/shard_map/ppermute | solution.py:131
  45.8 17.7 %collective-permute-start.3 = (bf16[2,2,2,256,128]{4,3,2,1,0:T(8,128)(2,1)}, bf16[2,2,2,256,128]{4,3,2,1,0:T(8,128)(2,1)}, u32[]{:S(2)}, u32[]{:S(2)}) collective-permute-start(bf16[2,2,2,256,128]{4,3,2,1,0:T(8,128)(2,1)} %bitcast.52), channel_id=1, source_target_pairs={{0,48},{16,0},{32,16},{48,32},{1,49},{17,1},{33,17},{49,33},{2,50}... | collective-permute-start | bytes 1572872 | tf_op jit(solution)/shard_map/ppermute | solution.py:131
  64.0 1.2 copy-start.2
  65.3 1.0 copy-start.3
  74.4 30.1 %copy-start.1 = (bf16[2,256,2,1,2,128]{5,1,4,2,0,3:T(8,128)(2,1)S(1)}, bf16[2,256,2,1,2,128]{5,1,4,2,0,3:T(8,128)(2,1)}, u32[]{:S(2)}) copy-start(bf16[2,256,2,1,2,128]{5,1,4,2,0,3:T(8,128)(2,1)} %copy.27) | copy-start | bytes 1572868
  74.4 30.1 %copy-start.4 = (s32[1,2]{1,0:T(1,128)S(1)}, s32[1,2]{1,0:T(1,128)}, u32[]{:S(2)}) copy-start(s32[1,2]{1,0:T(1,128)} %lengths_ref.1) | copy-start | bytes 28
  89.8 14.7 %all-to-all-start.3 = ((bf16[4,4,16,640]{3,2,1,0:T(8,128)(2,1)}), bf16[4,4,16,640]{3,2,1,0:T(8,128)(2,1)S(1)}, u32[]{:S(2)}, u32[]{:S(2)}) async-start(bf16[4,4,16,640]{3,2,1,0:T(8,128)(2,1)} %pad_maximum_fusion), calls=%async_computation.3 | async-start | bytes 655360 | tf_op jit(solution)/shard_map/all_to_all | solution.py:144
  107.5 13.6 %collective-permute-start.4 = (bf16[1,32,2048]{2,1,0:T(8,128)(2,1)S(1)}, bf16[1,32,2048]{2,1,0:T(8,128)(2,1)S(1)}, u32[]{:S(2)}, u32[]{:S(2)}) collective-permute-start(bf16[1,32,2048]{2,1,0:T(8,128)(2,1)S(1)} %bitcast.46), channel_id=1, source_target_pairs={{448,0},{0,64},{64,128},{128,192},{192,256},{256,320},{320,384},{3... | collective-permute-start | bytes 393224 | tf_op jit(solution)/shard_map/ppermute | solution.py:150
Sparse Core Ops, SparseCore 0:
  14.0 50.0 all-gather.2

commit v3 on v2

--- a/solution.py
+++ b/solution.py
@@ -13,47 +13,108 @@
 COL = ("xl", "y")
 BF = jnp.bfloat16
 F32 = jnp.float32
+FIRST = 1152
 VMEM = pl.BlockSpec(memory_space=pltpu.VMEM)
+HBM = pl.BlockSpec(memory_space=pltpu.HBM)
 SMEM = pl.BlockSpec(memory_space=pltpu.SMEM)
-PARAMS = pltpu.CompilerParams(vmem_limit_bytes=40 * 1024 * 1024)
-
-
-def project_kernel(place_ref, ring_ref, direct_ref, query_ref, pair_ref, out_ref):
-    count, rows, width = ring_ref.shape
+PARAMS = pltpu.CompilerParams(vmem_limit_bytes=32 * 1024 * 1024)
+
+
+def project_kernel(place_ref, own_ref, theirs_ref, rest_ref, query_ref, pair_ref, out_ref, query, pair, sems):
+    count, rows, first = own_ref.shape
+    remainder = rest_ref.shape[2] // 2
     half = rows // 2
     mine = place_ref[0] * count
     other = (1 - place_ref[0]) * count
-    own = ring_ref[...].reshape(count * rows, width)
-    theirs = direct_ref[...].reshape(count * rows, width)
-
-    def store(block, start, lanes):
-        block = block.astype(BF).reshape(count, 2, half, block.shape[1])
-        for h in range(2):
-            out_ref[h, pl.ds(start, count), :, lanes] = block[:, h]
-
-    for weight_ref, lanes in ((query_ref, slice(0, 512)), (pair_ref, slice(512, 640))):
-        store(jnp.dot(theirs, weight_ref[...], preferred_element_type=F32), other, lanes)
-        store(jnp.dot(own, weight_ref[...], preferred_element_type=F32), mine, lanes)
-
-
-def project(place, ring, direct, query_weight, pair_weight):
+    copies = []
+    for lines in (pl.ds(0, first), pl.ds(first, remainder)):
+        for source, target in ((query_ref, query), (pair_ref, pair)):
+            n = len(copies)
+            copies.append(pltpu.make_async_copy(source.at[lines], target.at[lines], sems.at[n]))
+    for copy in copies:
+        copy.start()
+
+    def flat(block):
+        return block.reshape(count * rows, block.shape[2])
+
+    def times(block, lines):
+        return [
+            jnp.dot(block, weight[lines], preferred_element_type=F32) for weight in (query, pair)
+        ]
+
+    copies[0].wait()
+    copies[1].wait()
+    former = [times(flat(ref[...]), slice(0, first)) for ref in (own_ref, theirs_ref)]
+    copies[2].wait()
+    copies[3].wait()
+    for n, start in enumerate((mine, other)):
+        block = flat(rest_ref[:, :, n * remainder : (n + 1) * remainder])
+        latter = times(block, slice(first, first + remainder))
+        for part, more, lanes in zip(former[n], latter, (slice(0, 512), slice(512, 640))):
+            part = (part + more).astype(BF).reshape(count, 2, half, part.shape[1])
+            for h in range(2):
+                out_ref[h, pl.ds(start, count), :, lanes] = part[:, h]
+
+
+def project(place, own, theirs, rest, query_weight, pair_weight):
     return pl.pallas_call(
         project_kernel,
         out_shape=jax.ShapeDtypeStruct((2, 16, 16, 640), BF),
-        in_specs=[SMEM, VMEM, VMEM, VMEM, VMEM],
+        in_specs=[SMEM, VMEM, VMEM, VMEM, HBM, HBM],
         out_specs=VMEM,
+        scratch_shapes=[
+            pltpu.VMEM(query_weight.shape, BF),
+            pltpu.VMEM(pair_weight.shape, BF),
+            pltpu.SemaphoreType.DMA((4,)),
+        ],
         compiler_params=PARAMS,
         name="project",
-    )(place, ring, direct, query_weight, pair_weight)
+    )(place, own, theirs, rest, query_weight, pair_weight)
+
+
+def pick_kernel(cache_ref, *refs):
+    pieces, sems = refs[:4], refs[4]
+    place = lax.axis_index(ROW)
+    copies = []
+    for k in range(4):
+        for p in range(2):
+            for g in range(2):
+                at = pl.multiple_of((place ^ k) * 256 + g * HEAD_DIM, HEAD_DIM)
+                source = cache_ref.at[p, :, :, pl.ds(at, HEAD_DIM)]
+                n = len(copies)
+                copies.append(pltpu.make_async_copy(source, pieces[k].at[p, g], sems.at[n]))
+    for copy in copies:
+        copy.start()
+    for copy in copies:
+        copy.wait()
+
+
+def pick(cache):
+    prompts, chunk = cache.shape[:2]
+    piece = jax.ShapeDtypeStruct((prompts, 2, chunk, 2, HEAD_DIM), BF)
+    return pl.pallas_call(
+        pick_kernel,
+        out_shape=[piece] * 4,
+        in_specs=[HBM],
+        out_specs=[HBM] * 4,
+        scratch_shapes=[pltpu.SemaphoreType.DMA((16,))],
+        name="pick",
+    )(cache)
 
 
 def attend_kernel(lengths_ref, place_ref, parts_ref, scale_ref, *refs):
     caches, out_ref, pair_ref = refs[:4], refs[4], refs[5]
     _, prompts, blocks, samples, _ = parts_ref.shape
-    _, _, heads, chunk, dim = caches[0].shape
+    _, heads, chunk, dim = caches[0].shape
     per_block = 512 // dim
     factor = dim**-0.5
     place = place_ref[0]
+    column = lax.broadcasted_iota(jnp.int32, (1, chunk), 1)
+    is_key = column % 2 == 0
+    positions = []
+    for k in range(len(caches)):
+        first = (place ^ k) * (chunk // 2)
+        positions.append(jnp.where(is_key, first + column // 2, 2**30))
     for p in range(prompts):
         length = lengths_ref[0, p]
         here = slice(p * samples, (p + 1) * samples)
@@ -73,11 +134,9 @@
             top = own
             for k in range(len(caches)):
                 block = lax.dot_general(
-                    query, caches[k][p, 0, g], (((1,), (1,)), ((), ())), preferred_element_type=F32
+                    query, caches[k][p, g], (((1,), (1,)), ((), ())), preferred_element_type=F32
                 )
-                first = lax.rem(place + len(caches) - k, len(caches)) * chunk
-                position = first + lax.broadcasted_iota(jnp.int32, block.shape, 1)
-                block = jnp.where(position < length, block * factor, FLOOR)
+                block = jnp.where(positions[k] < length, block * factor, FLOOR)
                 top = jnp.maximum(top, jnp.max(block, axis=1, keepdims=True))
                 scores.append(block)
             own_weight = jnp.exp(own - top)
@@ -86,9 +145,8 @@
             for k in range(len(caches)):
                 weight = jnp.exp(scores[k] - top)
                 weight_sum = weight_sum + jnp.sum(weight, axis=1, keepdims=True)
-                value = value + jnp.dot(
-                    weight.astype(BF), caches[k][p, 1, g], preferred_element_type=F32
-                )
+                weight = pltpu.roll(weight, 1, 1).astype(BF)
+                value = value + jnp.dot(weight, caches[k][p, g], preferred_element_type=F32)
             result = (value / weight_sum).astype(BF)
             for n, (j, h) in enumerate(names):
                 at = (j * per_block + h) * dim
@@ -117,25 +175,32 @@
     widened = hidden_in[0].astype(F32)
     sent = (widened * norm_gain[0][None, :]).astype(BF)
     local_squares = jnp.sum(widened * widened, axis=1)
-
-    ring = lax.all_gather(sent, "y")
-    theirs = lax.ppermute(sent, "xl", [(0, 1), (1, 0)])
-    direct = lax.all_to_all(jnp.broadcast_to(theirs[None], (8, rows, width)), "y", 0, 0)
-
-    prompts, chunk = kv_cache.shape[1], kv_cache.shape[2]
-    cache = kv_cache[0].reshape(prompts, chunk, 2, row_count, 2, HEAD_DIM).transpose(3, 0, 2, 4, 1, 5)
+    swap = [(0, 1), (1, 0)]
+
+    def spread(block):
+        return lax.all_to_all(jnp.broadcast_to(block[None], (8,) + block.shape), "y", 0, 0)
+
+    own = spread(sent[:, :FIRST])
+    rest = sent[:, FIRST:]
+    rest = jnp.concatenate([rest, lax.ppermute(rest, "xl", swap)], axis=1)
+    own, rest, pieces = lax.optimization_barrier((own, rest, pick(kv_cache[0])))
+    theirs = lax.ppermute(own, "xl", swap)
+    rest = spread(rest)
+
     caches = []
-    for k in range(row_count):
-        piece = lax.dynamic_index_in_dim(cache, (row_index + k) % row_count, 0, keepdims=False)
+    for k, piece in enumerate(pieces):
         if k:
-            piece = lax.ppermute(piece, ROW, [(i, (i + k) % row_count) for i in range(row_count)])
-        caches.append(piece)
-    ring, direct, caches = lax.optimization_barrier((ring, direct, caches))
-
-    partial = project(lax.axis_index("xl")[None], ring, direct, q_weight[0], kv_weight[0])
+            piece = lax.ppermute(piece, ROW, [(i, i ^ k) for i in range(row_count)])
+        caches.append(piece.reshape(piece.shape[0], 2, -1, HEAD_DIM))
+
+    place = lax.axis_index("xl")[None]
+    partial = project(place, own, theirs, rest, q_weight[0], kv_weight[0])
     partial = lax.all_to_all(partial, "co", 0, 0)
     both = (partial[0].astype(F32) + partial[1].astype(F32)).astype(BF)
+    both, local_squares, caches = lax.optimization_barrier((both, local_squares, caches))
     both = lax.all_to_all(both, COL, 0, 0)
+    squares = lax.psum(local_squares, ROW)
+    both, squares = lax.optimization_barrier((both, squares))
     samples = both.shape[1]
     query_blocks = both[:, :, :512].reshape(row_count, 4, samples, 512)
     pair_blocks = both[:, :, 512:].reshape(2, row_count, 2, samples, HEAD_DIM)
@@ -143,7 +208,6 @@
     parts = jnp.concatenate([query_blocks, pair_blocks], axis=3)
     parts = lax.all_to_all(parts, ROW, 0, 0).reshape((2, 2) + parts.shape[1:])
 
-    squares = lax.psum(local_squares, ROW)
     scale = lax.rsqrt(squares / (width * row_count) + EPSILON)[:, None]
     attended, pairs = attend(lengths, row_index[None], parts, scale, caches)
     count = 8

time: 129 us -> 176 us (1.36)
  Pallas kernels: 4.74 us -> 72.2 us
  blocking collectives: 38.3 us -> 20.2 us
  starting transfers between devices: 33.4 us -> 47 us
  between operations: 14.2 us -> 0.79 us
  local copies, waits for them, and re-layouts: 19.4 us -> 6.13 us
  waiting for transfers between devices: 15 us -> 26.1 us
    pallas_call x0 -> x1, Pallas kernels: none -> 64.8 us  [pick(): pl.pallas_call(pick_kernel, out_shape=[piece] * 4, in_specs=[HBM], out_sp...]
    all_to_all x1 -> x0, blocking collectives: 14.5 us -> none  [shards(): both = lax.all_to_all(both, COL, 0, 0)]
    all_to_all x1 -> x3, waiting for transfers between devices: 0.01 us -> 14.1 us  [the longest x2 10.5 us: spread(): lax.all_to_all(jnp.broadcast_to(block[None], (8,) + block.shape), 'y', 0, 0)]
    all_to_all x1 -> x3, starting transfers between devices: 7.61 us -> 21.1 us  [the longest x2 14.3 us: spread(): lax.all_to_all(jnp.broadcast_to(block[None], (8,) + block.shape), 'y', 0, 0)]
    unnamed x16 -> x9, local copies, waits for them, and re-layouts: 16 us -> 3.29 us
    ppermute x4 -> x5, waiting for transfers between devices: 14.4 us -> 3.85 us  [the longest x3 3.85 us: shards(): piece = lax.ppermute(piece, ROW, [(i, i ^ k) for i in range(row_count)])]
    all_to_all x1, waiting for transfers between devices: 0.01 us -> 7.28 us  [shards(): parts = lax.all_to_all(parts, ROW, 0, 0).reshape((2, 2) + parts.shape[1:])]
    ppermute x4 -> x5, starting transfers between devices: 16 us -> 18 us  [the longest x3 12.7 us: shards(): piece = lax.ppermute(piece, ROW, [(i, i ^ k) for i in range(row_count)])]
  transfers between devices with their start and end apart: 8 -> 10, of which waited for: 4 -> 5; matrix products, arithmetic and copies ran while one was open for 14% -> 1% of each run, Pallas kernels for 0% -> 39%
where the time goes in v3:
time: 176 us; the launch traced here: 175 us
  Pallas kernels  72.2 us (41%)
  starting transfers between devices  47 us (27%)
  waiting for transfers between devices  26.1 us (15%)
  blocking collectives  20.2 us (11%)
  local copies, waits for them, and re-layouts  6.13 us (3%)
  other arithmetic  2.62 us (1%)
    pallas_call x1, Pallas kernels, pick(): pl.pallas_call(pick_kernel, out_shape=[piece] * 4, in_specs=[HBM], out_sp...  64.8 us
    all_to_all x2, starting transfers between devices, spread(): lax.all_to_all(jnp.broadcast_to(block[None], (8,) + block.shape), 'y', 0, 0)  14.3 us
    ppermute x3, starting transfers between devices, shards(): piece = lax.ppermute(piece, ROW, [(i, i ^ k) for i in range(row_count)])  12.7 us
    all_to_all x2, waiting for transfers between devices, spread(): lax.all_to_all(jnp.broadcast_to(block[None], (8,) + block.shape), 'y', 0, 0)  10.5 us
    all_gather x1, blocking collectives, shards(): pairs = lax.all_gather(pairs, ROW)  7.92 us
    all_to_all x1, waiting for transfers between devices, shards(): parts = lax.all_to_all(parts, ROW, 0, 0).reshape((2, 2) + parts.shape[1:])  7.28 us
    psum x1, blocking collectives, shards(): squares = lax.psum(local_squares, ROW)  6.92 us
    all_to_all x1, starting transfers between devices, shards(): both = lax.all_to_all(both, COL, 0, 0)  6.78 us
  transfers between devices with their start and end apart: 10, of which 5 were waited for; matrix products, arithmetic and copies ran while one was open for 1% of the time, Pallas kernels for 39%

profile of v3, /device:TPU:1, one launch (start us, length us, event | category | flops | bytes accessed | tf_op | source)
XLA Modules:
  0.0 175.1 jit_solution(10708082759101613775)
XLA Ops:
  0.6 1.1 fusion.2
  1.7 0.9 broadcast_in_dim.26
  2.6 7.7 %all-to-all-start = ((bf16[8,32,1152]{2,1,0:T(8,128)(2,1)}), bf16[8,32,1152]{2,1,0:T(8,128)(2,1)S(1)}, u32[]{:S(2)}, u32[]{:S(2)}) async-start(bf16[8,32,1152]{2,1,0:T(8,128)(2,1)} %broadcast_in_dim.26), calls=%async_computation | async-start | bytes 1179648 | tf_op jit(solution)/shard_map/all_to_all | solution.py:181
  10.2 3.1 %collective-permute-start = (bf16[32,896]{1,0:T(8,128)(2,1)S(1)}, bf16[32,896]{1,0:T(8,128)(2,1)S(1)}, u32[]{:S(2)}, u32[]{:S(2)}) collective-permute-start(bf16[32,896]{1,0:T(8,128)(2,1)S(1)} %slice.25), channel_id=1, source_target_pairs={{0,8},{8,0},{1,9},{9,1},{2,10},{10,2},{3,11},{11,3},{4,12},{12,4},... | collective-permute-start | bytes 172040 | tf_op jit(solution)/shard_map/ppermute | solution.py:185
  13.3 64.8 %pick.1 = (bf16[2,2,256,2,128]{4,3,2,1,0:T(2,128)(2,1)}, bf16[2,2,256,2,128]{4,3,2,1,0:T(2,128)(2,1)}, bf16[2,2,256,2,128]{4,3,2,1,0:T(2,128)(2,1)}, bf16[2,2,256,2,128]{4,3,2,1,0:T(2,128)(2,1)}) custom-call(bf16[2,256,2,1024]{3,2,1,0:T(2,128)(2,1)} %bitcast.35), custom_call_target="tpu_custom_call" | custom-call | tf_op jit(solution)/shard_map/pick/pallas_call | solution.py:95
  78.1 0.0 collective-permute-done
  78.2 0.0 all-to-all-done.own_ref
  78.2 1.0 broadcast_in_dim.27
  79.2 6.6 %all-to-all-start.1 = ((bf16[8,32,1792]{2,1,0:T(8,128)(2,1)}), bf16[8,32,1792]{2,1,0:T(8,128)(2,1)S(1)}, u32[]{:S(2)}, u32[]{:S(2)}) async-start(bf16[8,32,1792]{2,1,0:T(8,128)(2,1)} %broadcast_in_dim.27), calls=%async_computation.1 | async-start | bytes 1835008 | tf_op jit(solution)/shard_map/all_to_all | solution.py:181
  85.8 2.2 %collective-permute-start.1 = (bf16[8,32,1152]{2,1,0:T(8,128)(2,1)S(1)}, bf16[8,32,1152]{2,1,0:T(8,128)(2,1)S(1)}, u32[]{:S(2)}, u32[]{:S(2)}) collective-permute-start(bf16[8,32,1152]{2,1,0:T(8,128)(2,1)S(1)} %all-to-all-done.own_ref), channel_id=1, source_target_pairs={{0,8},{8,0},{1,9},{9,1},{2,10},{10,2},{3,11},{11,3},{4,12},{12,4},... | collective-permute-start | bytes 1769480 | tf_op jit(solution)/shard_map/ppermute | solution.py:187
  88.0 5.7 %collective-permute-start.2 = (bf16[2,2,256,2,128]{4,3,2,1,0:T(2,128)(2,1)}, bf16[2,2,256,2,128]{4,3,2,1,0:T(2,128)(2,1)S(1)}, u32[]{:S(2)}, u32[]{:S(2)}) collective-permute-start(bf16[2,2,256,2,128]{4,3,2,1,0:T(2,128)(2,1)} %get-tuple-element.29), channel_id=1, source_target_pairs={{0,16},{16,0},{32,48},{48,32},{1,17},{17,1},{33,49},{49,33},{2,18}... | collective-permute-start | bytes 1572872 | tf_op jit(solution)/shard_map/ppermute | solution.py:193
  93.7 2.9 %collective-permute-start.3 = (bf16[2,2,256,2,128]{4,3,2,1,0:T(2,128)(2,1)}, bf16[2,2,256,2,128]{4,3,2,1,0:T(2,128)(2,1)S(1)}, u32[]{:S(2)}, u32[]{:S(2)}) collective-permute-start(bf16[2,2,256,2,128]{4,3,2,1,0:T(2,128)(2,1)} %get-tuple-element.30), channel_id=1, source_target_pairs={{0,32},{16,48},{32,0},{48,16},{1,33},{17,49},{33,1},{49,17},{2,34}... | collective-permute-start | bytes 1572872 | tf_op jit(solution)/shard_map/ppermute | solution.py:193
  96.6 4.0 %collective-permute-start.4 = (bf16[2,2,256,2,128]{4,3,2,1,0:T(2,128)(2,1)}, bf16[2,2,256,2,128]{4,3,2,1,0:T(2,128)(2,1)}, u32[]{:S(2)}, u32[]{:S(2)}) collective-permute-start(bf16[2,2,256,2,128]{4,3,2,1,0:T(2,128)(2,1)} %get-tuple-element.31), channel_id=1, source_target_pairs={{0,48},{16,32},{32,16},{48,0},{1,49},{17,33},{33,17},{49,1},{2,50}... | collective-permute-start | bytes 1572872 | tf_op jit(solution)/shard_map/ppermute | solution.py:193
  100.7 0.0 collective-permute-done.1.theirs_ref
  100.7 10.5 %all-to-all-done.1.rest_ref = bf16[8,32,1792]{2,1,0:T(8,128)(2,1)S(1)} async-done(((bf16[8,32,1792]{2,1,0:T(8,128)(2,1)}), bf16[8,32,1792]{2,1,0:T(8,128)(2,1)S(1)}, u32[]{:S(2)}, u32[]{:S(2)}) %all-to-all-start.1) | async-done | bytes 917536 | tf_op jit(solution)/shard_map/all_to_all | solution.py:181
  111.2 0.0 copy-start
  111.2 1.6 copy-done
  112.8 0.0 copy-start.2
  112.8 1.0 copy-done.2
  113.9 3.0 %project.1 = bf16[2,16,16,640]{3,2,1,0:T(8,128)(2,1)S(1)} custom-call(s32[1]{0:T(128)} %bitcast.1.place_ref, bf16[8,32,1152]{2,1,0:T(8,128)(2,1)S(1)} %all-to-all-done.own_ref, bf16[8,32,1152]{2,1,0:T(8,128)(2,1)S(1)} %collective-permute-done.1.theirs_ref, bf16[8,32,1792]{2,1,0:T(8,128)(2,1)S(1)} %all-to-all-done.1.rest_ref, bf16[2048,512]{1,0:T(8,128)(2,1)S(1)} %bitcast.28, ...), custom_call_target="tpu_custom_call" | custom-call | tf_op jit(solution)/shard_map/project/pallas_call | solution.py:60
  116.9 5.3 %all_to_all.25 = bf16[2,16,16,640]{3,2,1,0:T(8,128)(2,1)S(1)} all-to-all(bf16[2,16,16,640]{3,2,1,0:T(8,128)(2,1)S(1)} %project.1), channel_id=1, replica_groups=mesh['z'=8,'xh'=2,'co'=2,'xl'=2,'y'=8] {'co'}, dimensions={0} | all-to-all | bytes 1310720 | tf_op jit(solution)/shard_map/all_to_all | solution.py:198
  122.2 0.0 copy-start.1
  122.2 0.0 copy-start.3
  122.2 0.8 fusion
  123.0 0.0 collective-permute-done.2
  123.0 0.0 collective-permute-done.3
  123.0 3.8 %collective-permute-done.4 = bf16[2,2,256,2,128]{4,3,2,1,0:T(2,128)(2,1)} collective-permute-done((bf16[2,2,256,2,128]{4,3,2,1,0:T(2,128)(2,1)}, bf16[2,2,256,2,128]{4,3,2,1,0:T(2,128)(2,1)}, u32[]{:S(2)}, u32[]{:S(2)}) %collective-permute-start.4) | collective-permute-done | bytes 524320 | tf_op jit(solution)/shard_map/ppermute | solution.py:193
  126.9 6.8 %all-to-all-start.3 = ((bf16[16,16,640]{2,1,0:T(8,128)(2,1)}), bf16[16,16,640]{2,1,0:T(8,128)(2,1)S(1)}, u32[]{:S(2)}, u32[]{:S(2)}) async-start(bf16[16,16,640]{2,1,0:T(8,128)(2,1)} %fusion), calls=%async_computation.3 | async-start | bytes 655360 | tf_op jit(solution)/shard_map/all_to_all | solution.py:201
  133.7 6.9 %psum.7 = f32[32]{0:T(128)S(1)} all-reduce(f32[32]{0:T(128)S(1)} %get-tuple-element.33), channel_id=1, replica_groups=mesh['z'=8,'xh'=2,'co'=2,'xl'=2,'y'=8] {'xh','co'}, use_global_device_ids=true, to_apply=%region_1.0 | all-reduce | flops 32 | bytes 256 | tf_op jit(solution)/shard_map/psum | solution.py:202
  140.6 3.6 %all-to-all-done.3 = bf16[16,16,640]{2,1,0:T(8,128)(2,1)S(1)} async-done(((bf16[16,16,640]{2,1,0:T(8,128)(2,1)}), bf16[16,16,640]{2,1,0:T(8,128)(2,1)S(1)}, u32[]{:S(2)}, u32[]{:S(2)}) %all-to-all-start.3) | async-done | bytes 327712 | tf_op jit(solution)/shard_map/all_to_all | solution.py:201
  144.2 0.7 pad_maximum_fusion
  144.9 4.0 %all-to-all-start.4 = ((bf16[4,4,16,640]{3,2,1,0:T(8,128)(2,1)}), bf16[4,4,16,640]{3,2,1,0:T(8,128)(2,1)S(1)}, u32[]{:S(2)}, u32[]{:S(2)}) async-start(bf16[4,4,16,640]{3,2,1,0:T(8,128)(2,1)} %pad_maximum_fusion), calls=%async_computation.4 | async-start | bytes 655360 | tf_op jit(solution)/shard_map/all_to_all | solution.py:209
  148.9 0.1 copy.12.scale_ref
  149.0 7.3 %all-to-all-done.4 = bf16[4,4,16,640]{3,2,1,0:T(8,128)(2,1)S(1)} async-done(((bf16[4,4,16,640]{3,2,1,0:T(8,128)(2,1)}), bf16[4,4,16,640]{3,2,1,0:T(8,128)(2,1)S(1)}, u32[]{:S(2)}, u32[]{:S(2)}) %all-to-all-start.4) | async-done | bytes 327712 | tf_op jit(solution)/shard_map/all_to_all | solution.py:209
  156.3 0.0 copy-done.1
  156.3 0.0 copy-done.3
  156.3 4.4 %attend.1 = (bf16[32,2048]{1,0:T(8,128)(2,1)S(1)}, bf16[4,32,128]{2,1,0:T(8,128)(2,1)S(1)}) custom-call(s32[1,2]{1,0:T(1,128)S(1)} %copy-done.3, s32[1]{0:T(128)} %bitcast.place_ref, bf16[2,2,4,16,640]{4,3,2,1,0:T(8,128)(2,1)S(1)} %bitcast.29, f32[32,1]{1,0:T(8,128)S(1)} %copy.12.scale_ref, bf16[2,2,512,128]{3,2,1,0:T(8,128)(2,1)S(1)} %bitcast.30, ...), custom_call_target="tpu_custom_call" | custom-call | tf_op jit(solution)/shard_map/attend/pallas_call | solution.py:158
  160.8 4.0 %collective-permute-start.5 = (bf16[1,32,2048]{2,1,0:T(8,128)(2,1)S(1)}, bf16[1,32,2048]{2,1,0:T(8,128)(2,1)S(1)}, u32[]{:S(2)}, u32[]{:S(2)}) collective-permute-start(bf16[1,32,2048]{2,1,0:T(8,128)(2,1)S(1)} %bitcast.34), channel_id=1, source_target_pairs={{448,0},{0,64},{64,128},{128,192},{192,256},{256,320},{320,384},{3... | collective-permute-start | bytes 393224 | tf_op jit(solution)/shard_map/ppermute | solution.py:214
  164.7 7.9 %all-gather = bf16[16,32,128]{2,1,0:T(8,128)(2,1)S(1)} all-gather(bf16[4,32,128]{2,1,0:T(8,128)(2,1)S(1)} %get-tuple-element.41), channel_id=2, replica_groups=mesh['z'=8,'xh'=2,'co'=2,'xl'=2,'y'=8] {'xh','co'}, dimensions={0}, use_global_device_ids=true | all-gather | bytes 163840 | tf_op jit(solution)/shard_map/all_gather | solution.py:215
  172.7 0.1 copy.13
  172.8 0.7 reshape.51
  173.5 0.9 collective-permute-done.5
  174.4 0.7 copy.15
  (7 shorter events, 0.1 us)
Async XLA Ops:
  2.6 75.6 %all-to-all-start = ((bf16[8,32,1152]{2,1,0:T(8,128)(2,1)}), bf16[8,32,1152]{2,1,0:T(8,128)(2,1)S(1)}, u32[]{:S(2)}, u32[]{:S(2)}) async-start(bf16[8,32,1152]{2,1,0:T(8,128)(2,1)} %broadcast_in_dim.26), calls=%async_computation | async-start | bytes 1179648 | tf_op jit(solution)/shard_map/all_to_all | solution.py:181
  10.2 67.9 %collective-permute-start = (bf16[32,896]{1,0:T(8,128)(2,1)S(1)}, bf16[32,896]{1,0:T(8,128)(2,1)S(1)}, u32[]{:S(2)}, u32[]{:S(2)}) collective-permute-start(bf16[32,896]{1,0:T(8,128)(2,1)S(1)} %slice.25), channel_id=1, source_target_pairs={{0,8},{8,0},{1,9},{9,1},{2,10},{10,2},{3,11},{11,3},{4,12},{12,4},... | collective-permute-start | bytes 172040 | tf_op jit(solution)/shard_map/ppermute | solution.py:185
  79.2 32.1 %all-to-all-start.1 = ((bf16[8,32,1792]{2,1,0:T(8,128)(2,1)}), bf16[8,32,1792]{2,1,0:T(8,128)(2,1)S(1)}, u32[]{:S(2)}, u32[]{:S(2)}) async-start(bf16[8,32,1792]{2,1,0:T(8,128)(2,1)} %broadcast_in_dim.27), calls=%async_computation.1 | async-start | bytes 1835008 | tf_op jit(solution)/shard_map/all_to_all | solution.py:181
  85.8 14.9 %collective-permute-start.1 = (bf16[8,32,1152]{2,1,0:T(8,128)(2,1)S(1)}, bf16[8,32,1152]{2,1,0:T(8,128)(2,1)S(1)}, u32[]{:S(2)}, u32[]{:S(2)}) collective-permute-start(bf16[8,32,1152]{2,1,0:T(8,128)(2,1)S(1)} %all-to-all-done.own_ref), channel_id=1, source_target_pairs={{0,8},{8,0},{1,9},{9,1},{2,10},{10,2},{3,11},{11,3},{4,12},{12,4},... | collective-permute-start | bytes 1769480 | tf_op jit(solution)/shard_map/ppermute | solution.py:187
  88.0 35.0 %collective-permute-start.2 = (bf16[2,2,256,2,128]{4,3,2,1,0:T(2,128)(2,1)}, bf16[2,2,256,2,128]{4,3,2,1,0:T(2,128)(2,1)S(1)}, u32[]{:S(2)}, u32[]{:S(2)}) collective-permute-start(bf16[2,2,256,2,128]{4,3,2,1,0:T(2,128)(2,1)} %get-tuple-element.29), channel_id=1, source_target_pairs={{0,16},{16,0},{32,48},{48,32},{1,17},{17,1},{33,49},{49,33},{2,18}... | collective-permute-start | bytes 1572872 | tf_op jit(solution)/shard_map/ppermute | solution.py:193
  93.7 29.3 %collective-permute-start.3 = (bf16[2,2,256,2,128]{4,3,2,1,0:T(2,128)(2,1)}, bf16[2,2,256,2,128]{4,3,2,1,0:T(2,128)(2,1)S(1)}, u32[]{:S(2)}, u32[]{:S(2)}) collective-permute-start(bf16[2,2,256,2,128]{4,3,2,1,0:T(2,128)(2,1)} %get-tuple-element.30), channel_id=1, source_target_pairs={{0,32},{16,48},{32,0},{48,16},{1,33},{17,49},{33,1},{49,17},{2,34}... | collective-permute-start | bytes 1572872 | tf_op jit(solution)/shard_map/ppermute | solution.py:193
  96.6 30.2 %collective-permute-start.4 = (bf16[2,2,256,2,128]{4,3,2,1,0:T(2,128)(2,1)}, bf16[2,2,256,2,128]{4,3,2,1,0:T(2,128)(2,1)}, u32[]{:S(2)}, u32[]{:S(2)}) collective-permute-start(bf16[2,2,256,2,128]{4,3,2,1,0:T(2,128)(2,1)} %get-tuple-element.31), channel_id=1, source_target_pairs={{0,48},{16,32},{32,16},{48,0},{1,49},{17,33},{33,17},{49,1},{2,50}... | collective-permute-start | bytes 1572872 | tf_op jit(solution)/shard_map/ppermute | solution.py:193
  111.2 1.6 copy-start
  112.8 1.0 copy-start.2
  122.2 34.1 %copy-start.1 = (bf16[2,2,256,2,128]{4,3,2,1,0:T(2,128)(2,1)S(1)}, bf16[2,2,256,2,128]{4,3,2,1,0:T(2,128)(2,1)}, u32[]{:S(2)}) copy-start(bf16[2,2,256,2,128]{4,3,2,1,0:T(2,128)(2,1)} %get-tuple-element.28) | copy-start | bytes 1572868
  122.2 34.1 %copy-start.3 = (s32[1,2]{1,0:T(1,128)S(1)}, s32[1,2]{1,0:T(1,128)}, u32[]{:S(2)}) copy-start(s32[1,2]{1,0:T(1,128)} %lengths_ref.1) | copy-start | bytes 28
  126.9 17.3 %all-to-all-start.3 = ((bf16[16,16,640]{2,1,0:T(8,128)(2,1)}), bf16[16,16,640]{2,1,0:T(8,128)(2,1)S(1)}, u32[]{:S(2)}, u32[]{:S(2)}) async-start(bf16[16,16,640]{2,1,0:T(8,128)(2,1)} %fusion), calls=%async_computation.3 | async-start | bytes 655360 | tf_op jit(solution)/shard_map/all_to_all | solution.py:201
  144.9 11.4 %all-to-all-start.4 = ((bf16[4,4,16,640]{3,2,1,0:T(8,128)(2,1)}), bf16[4,4,16,640]{3,2,1,0:T(8,128)(2,1)S(1)}, u32[]{:S(2)}, u32[]{:S(2)}) async-start(bf16[4,4,16,640]{3,2,1,0:T(8,128)(2,1)} %pad_maximum_fusion), calls=%async_computation.4 | async-start | bytes 655360 | tf_op jit(solution)/shard_map/all_to_all | solution.py:209
  160.8 13.7 %collective-permute-start.5 = (bf16[1,32,2048]{2,1,0:T(8,128)(2,1)S(1)}, bf16[1,32,2048]{2,1,0:T(8,128)(2,1)S(1)}, u32[]{:S(2)}, u32[]{:S(2)}) collective-permute-start(bf16[1,32,2048]{2,1,0:T(8,128)(2,1)S(1)} %bitcast.34), channel_id=1, source_target_pairs={{448,0},{0,64},{64,128},{128,192},{192,256},{256,320},{320,384},{3... | collective-permute-start | bytes 393224 | tf_op jit(solution)/shard_map/ppermute | solution.py:214

commit v4 on v3

v4 whole, which is shorter than its diff:
```python
import jax
import jax.numpy as jnp
from jax import lax
from jax.experimental import pallas as pl
from jax.experimental.pallas import tpu as pltpu
from jax.sharding import Mesh
from jax.sharding import PartitionSpec as P

HEAD_DIM = 128
EPSILON = 1e-05
FLOOR = -1e30
ROW = ("xh", "co")
COL = ("xl", "y")
BF = jnp.bfloat16
F32 = jnp.float32
FIRST = 1280
VMEM = pl.BlockSpec(memory_space=pltpu.VMEM)
HBM = pl.BlockSpec(memory_space=pltpu.HBM)
SMEM = pl.BlockSpec(memory_space=pltpu.SMEM)
PARAMS = pltpu.CompilerParams(vmem_limit_bytes=32 * 1024 * 1024)
FULL = pltpu.CompilerParams(vmem_limit_bytes=56 * 1024 * 1024)


def project_kernel(place_ref, own_ref, theirs_ref, rest_ref, query_ref, pair_ref, out_ref, query, pair, sems):
    count, rows, first = own_ref.shape
    remainder = rest_ref.shape[2] // 2
    half = rows // 2
    mine = place_ref[0] * count
    other = (1 - place_ref[0]) * count
    copies = []
    for lines in (pl.ds(0, first), pl.ds(first, remainder)):
        for source, target in ((query_ref, query), (pair_ref, pair)):
            n = len(copies)
            copies.append(pltpu.make_async_copy(source.at[lines], target.at[lines], sems.at[n]))
    for copy in copies:
        copy.start()

    def flat(block):
        return block.reshape(count * rows, block.shape[2])

    def times(block, lines):
        return [
            jnp.dot(block, weight[lines], preferred_element_type=F32) for weight in (query, pair)
        ]

    copies[0].wait()
    copies[1].wait()
    former = [times(flat(ref[...]), slice(0, first)) for ref in (own_ref, theirs_ref)]
    copies[2].wait()
    copies[3].wait()
    for n, start in enumerate((mine, other)):
        block = flat(rest_ref[:, :, n * remainder : (n + 1) * remainder])
        latter = times(block, slice(first, first + remainder))
        for part, more, lanes in zip(former[n], latter, (slice(0, 512), slice(512, 640))):
            part = (part + more).astype(BF).reshape(count, 2, half, part.shape[1])
            for h in range(2):
                out_ref[h, pl.ds(start, count), :, lanes] = part[:, h]


def project(place, own, theirs, rest, query_weight, pair_weight):
    return pl.pallas_call(
        project_kernel,
        out_shape=jax.ShapeDtypeStruct((2, 16, 16, 640), BF),
        in_specs=[SMEM, VMEM, VMEM, VMEM, HBM, HBM],
        out_specs=VMEM,
        scratch_shapes=[
            pltpu.VMEM(query_weight.shape, BF),
            pltpu.VMEM(pair_weight.shape, BF),
            pltpu.SemaphoreType.DMA((4,)),
        ],
        compiler_params=FULL,
        name="project",
    )(place, own, theirs, rest, query_weight, pair_weight)


def pick_kernel(place_ref, cache_ref, *pieces):
    for k, piece_ref in enumerate(pieces):
        for g in range(2):
            at = pl.multiple_of((place_ref[0] ^ k) * 256 + g * HEAD_DIM, HEAD_DIM)
            block = cache_ref[0, :, :, pl.ds(at, HEAD_DIM)]
            for v in range(2):
                piece_ref[0, v, g] = block[:, v, :]


def pick(place, cache):
    prompts, chunk = cache.shape[:2]
    return pl.pallas_call(
        pick_kernel,
        grid=(prompts,),
        out_shape=[jax.ShapeDtypeStruct((prompts, 2, 2, chunk, HEAD_DIM), BF)] * 4,
        in_specs=[SMEM, pl.BlockSpec((1,) + cache.shape[1:], lambda p: (p, 0, 0, 0))],
        out_specs=[pl.BlockSpec((1, 2, 2, chunk, HEAD_DIM), lambda p: (p, 0, 0, 0, 0))] * 4,
        compiler_params=PARAMS,
        name="pick",
    )(place, cache)


def arrange_kernel(both_ref, parts_ref):
    for j in range(4):
        for a in range(4):
            parts_ref[a, j, :, :512] = both_ref[4 * a + j, :, :512]
        pairs = [both_ref[4 * j + i, :, 512:] for i in range(4)]
        pairs = jnp.concatenate(pairs, axis=1)
        for a in range(4):
            parts_ref[a, j, :, 512:] = pairs


def arrange(both):
    return pl.pallas_call(
        arrange_kernel,
        out_shape=jax.ShapeDtypeStruct((4, 4, both.shape[1], 1024), BF),
        in_specs=[VMEM],
        out_specs=VMEM,
        compiler_params=PARAMS,
        name="arrange",
    )(both)


def attend_kernel(lengths_ref, place_ref, parts_ref, scale_ref, *refs):
    caches, out_ref, pair_ref = refs[:4], refs[4], refs[5]
    _, prompts, blocks, samples, _ = parts_ref.shape
    _, _, heads, chunk, dim = caches[0].shape
    per_block = 512 // dim
    factor = dim**-0.5
    place = place_ref[0]
    column = lax.broadcasted_iota(jnp.int32, (1, chunk), 1)
    positions = [(place ^ k) * chunk + column for k in range(len(caches))]
    for p in range(prompts):
        length = lengths_ref[0, p]
        here = slice(p * samples, (p + 1) * samples)
        scale = scale_ref[here]

        def total(block, lanes):
            part = parts_ref[0, p, block, :, lanes].astype(F32)
            part = part + parts_ref[1, p, block, :, lanes].astype(F32)
            return (part * scale).astype(BF)

        for j in range(blocks):
            pair_ref[here, j * 512 : (j + 1) * 512] = total(j, slice(512, 1024))
        for g in range(heads):
            head = place * heads + g
            lanes = pl.ds(pl.multiple_of(512 + lax.rem(head, 4) * dim, dim), dim)
            new_key = total(head // 4, lanes).astype(F32)
            new_value = total(2 + head // 4, lanes).astype(F32)
            names = [(j, h) for j in (2 * g, 2 * g + 1) for h in range(per_block)]
            queries = [total(j, slice(0, 512)) for j in (2 * g, 2 * g + 1)]
            query = [q[:, h * dim : (h + 1) * dim] for q in queries for h in range(per_block)]
            query = jnp.concatenate(query, axis=0)
            new_key = jnp.concatenate([new_key] * len(names), axis=0)
            new_value = jnp.concatenate([new_value] * len(names), axis=0)
            own = jnp.sum(query.astype(F32) * new_key, axis=1, keepdims=True) * factor
            scores = []
            top = own
            for k in range(len(caches)):
                block = lax.dot_general(
                    query, caches[k][p, 0, g], (((1,), (1,)), ((), ())), preferred_element_type=F32
                )
                block = jnp.where(positions[k] < length, block * factor, FLOOR)
                top = jnp.maximum(top, jnp.max(block, axis=1, keepdims=True))
                scores.append(block)
            own_weight = jnp.exp(own - top)
            weight_sum = own_weight
            value = own_weight.astype(BF).astype(F32) * new_value
            for k in range(len(caches)):
                weight = jnp.exp(scores[k] - top)
                weight_sum = weight_sum + jnp.sum(weight, axis=1, keepdims=True)
                value = value + jnp.dot(
                    weight.astype(BF), caches[k][p, 1, g], preferred_element_type=F32
                )
            result = (value / weight_sum).astype(BF)
            for n, (j, h) in enumerate(names):
                at = (j * per_block + h) * dim
                out_ref[here, at : at + dim] = result[n * samples : (n + 1) * samples]


def attend(lengths, place, parts, scale, caches):
    rows = parts.shape[1] * parts.shape[3]
    return pl.pallas_call(
        attend_kernel,
        out_shape=[jax.ShapeDtypeStruct((rows, 2048), BF)] * 2,
        in_specs=[SMEM, SMEM] + [VMEM] * 6,
        out_specs=(VMEM, VMEM),
        compiler_params=PARAMS,
        name="attend",
    )(lengths, place, parts, scale, *caches)


def shards(hidden_in, norm_gain, q_weight, kv_weight, kv_cache, lengths):
    rows, width = hidden_in.shape[1:]
    row_count = 4
    row_index = lax.axis_index(ROW)
    widened = hidden_in[0].astype(F32)
    sent = (widened * norm_gain[0][None, :]).astype(BF)
    local_squares = jnp.sum(widened * widened, axis=1)
    swap = [(0, 1), (1, 0)]

    def spread(block):
        return lax.all_to_all(jnp.broadcast_to(block[None], (8,) + block.shape), "y", 0, 0)

    own = spread(sent[:, :FIRST])
    rest = sent[:, FIRST:]
    rest = jnp.concatenate([rest, lax.ppermute(rest, "xl", swap)], axis=1)
    squares = lax.psum(local_squares, ROW)
    own, rest, pieces, squares = lax.optimization_barrier(
        (own, rest, pick(row_index[None], kv_cache[0]), squares)
    )
    theirs = lax.ppermute(own, "xl", swap)
    rest = spread(rest)

    caches = []
    for k, piece in enumerate(pieces):
        if k:
            piece = lax.ppermute(piece, ROW, [(i, i ^ k) for i in range(row_count)])
        caches.append(piece)

    place = lax.axis_index("xl")[None]
    partial = project(place, own, theirs, rest, q_weight[0], kv_weight[0])
    partial = lax.all_to_all(partial, "co", 0, 0)
    both = (partial[0].astype(F32) + partial[1].astype(F32)).astype(BF)
    both, caches = lax.optimization_barrier((both, caches))
    both = lax.all_to_all(both, COL, 0, 0)
    parts = lax.all_to_all(arrange(both), ROW, 0, 0)
    parts = parts.reshape((2, 2) + parts.shape[1:])

    scale = lax.rsqrt(squares / (width * row_count) + EPSILON)[:, None]
    attended, new_kv = attend(lengths, row_index[None], parts, scale, caches)
    count = 8
    handed = lax.ppermute(attended[None], "z", [((i - 1) % count, i) for i in range(count)])
    return (handed, new_kv[None])


def solution(mesh):
    fine = Mesh(mesh.devices.reshape(8, 2, 2, 2, 8), ("z", "xh", "co", "xl", "y"))
    return jax.shard_map(
        shards,
        mesh=fine,
        in_specs=(
            P("z", COL, ROW),
            P("z", ROW),
            P("z", ROW, COL),
            P("z", ROW, COL),
            P("z", COL, ROW, None, None),
            P("z", COL),
        ),
        out_specs=(P("z", COL, ROW), P("z", COL, None)),
        check_vma=False,
    )
```

time: 176 us -> 130 us (0.74)
  Pallas kernels: 72.2 us -> 13.9 us
  blocking collectives: 20.2 us -> 33.3 us
  waiting for transfers between devices: 26.1 us -> 36.2 us
  starting transfers between devices: 47 us -> 39.4 us
  local copies, waits for them, and re-layouts: 6.13 us -> 3.45 us
    pallas_call x2 -> x3, Pallas kernels: 69.2 us -> 8.02 us  [the longest x1 5.05 us: pick(): pl.pallas_call(pick_kernel, grid=(prompts,), out_shape=[jax.ShapeDtypeStr...]
    all_to_all x0 -> x1, blocking collectives: none -> 17.8 us  [shards(): both = lax.all_to_all(both, COL, 0, 0)]
    ppermute x1, waiting for transfers between devices: 0.9 us -> 9.65 us  [shards(): lax.ppermute(attended[None], 'z', [((i - 1) % count, i) for i in range(co...]
    all_gather x1 -> x0, blocking collectives: 7.92 us -> none  [shards(): pairs = lax.all_gather(pairs, ROW)]
    all_to_all x2 -> x1, starting transfers between devices: 10.8 us -> 4.03 us  [shards(): parts = lax.all_to_all(arrange(both), ROW, 0, 0)]
    all_to_all x2, waiting for transfers between devices: 10.5 us -> 5.3 us  [spread(): lax.all_to_all(jnp.broadcast_to(block[None], (8,) + block.shape), 'y', 0, 0)]
    ppermute x3, waiting for transfers between devices: 3.85 us -> 8.47 us  [shards(): piece = lax.ppermute(piece, ROW, [(i, i ^ k) for i in range(row_count)])]
    ppermute x1, waiting for transfers between devices: 0.01 us -> 3.38 us  [shards(): theirs = lax.ppermute(own, 'xl', swap)]
  transfers between devices with their start and end apart: 10 -> 9, of which waited for: 5 -> 5; matrix products, arithmetic and copies ran while one was open for 1% -> 0% of each run, Pallas kernels for 39% -> 9%
where the time goes in v4:
time: 130 us; the launch traced here: 128 us
  starting transfers between devices  39.4 us (30%)
  waiting for transfers between devices  36.2 us (28%)
  blocking collectives  33.3 us (26%)
  Pallas kernels  13.9 us (11%)
  local copies, waits for them, and re-layouts  3.45 us (3%)
    all_to_all x1, blocking collectives, shards(): both = lax.all_to_all(both, COL, 0, 0)  17.8 us
    all_to_all x2, starting transfers between devices, spread(): lax.all_to_all(jnp.broadcast_to(block[None], (8,) + block.shape), 'y', 0, 0)  14.5 us
    ppermute x3, starting transfers between devices, shards(): piece = lax.ppermute(piece, ROW, [(i, i ^ k) for i in range(row_count)])  10.2 us
    ppermute x1, waiting for transfers between devices, shards(): lax.ppermute(attended[None], 'z', [((i - 1) % count, i) for i in range(co...  9.65 us
    all_to_all x1, waiting for transfers between devices, shards(): parts = lax.all_to_all(arrange(both), ROW, 0, 0)  9.39 us
    psum x1, blocking collectives, shards(): squares = lax.psum(local_squares, ROW)  8.86 us
    ppermute x3, waiting for transfers between devices, shards(): piece = lax.ppermute(piece, ROW, [(i, i ^ k) for i in range(row_count)])  8.47 us
    all_to_all x1, blocking collectives, shards(): partial = lax.all_to_all(partial, 'co', 0, 0)  6.61 us
  transfers between devices with their start and end apart: 9, of which 5 were waited for; matrix products, arithmetic and copies ran while one was open for 0% of the time, Pallas kernels for 9%

profile of v4, /device:TPU:1, one launch (start us, length us, event | category | flops | bytes accessed | tf_op | source)
XLA Modules:
  0.0 128.3 jit_solution(14673921173130144348)
XLA Ops:
  0.6 0.0 copy-start
  0.6 1.2 fusion.2
  1.9 0.9 broadcast_in_dim.30
  2.7 7.7 %all-to-all-start = ((bf16[8,32,1280]{2,1,0:T(8,128)(2,1)}), bf16[8,32,1280]{2,1,0:T(8,128)(2,1)}, u32[]{:S(2)}, u32[]{:S(2)}) async-start(bf16[8,32,1280]{2,1,0:T(8,128)(2,1)} %broadcast_in_dim.30), calls=%async_computation | async-start | bytes 1310720 | tf_op jit(solution)/shard_map/all_to_all | solution.py:198
  10.4 3.1 %collective-permute-start = (bf16[32,768]{1,0:T(8,128)(2,1)S(1)}, bf16[32,768]{1,0:T(8,128)(2,1)S(1)}, u32[]{:S(2)}, u32[]{:S(2)}) collective-permute-start(bf16[32,768]{1,0:T(8,128)(2,1)S(1)} %slice.17), channel_id=1, source_target_pairs={{0,8},{8,0},{1,9},{9,1},{2,10},{10,2},{3,11},{11,3},{4,12},{12,4},... | collective-permute-start | bytes 147464 | tf_op jit(solution)/shard_map/ppermute | solution.py:202
  13.5 0.0 copy-done
  13.6 5.1 %pick.1 = (bf16[2,2,2,256,128]{4,3,2,1,0:T(8,128)(2,1)S(1)}, bf16[2,2,2,256,128]{4,3,2,1,0:T(8,128)(2,1)}, bf16[2,2,2,256,128]{4,3,2,1,0:T(8,128)(2,1)S(1)}, bf16[2,2,2,256,128]{4,3,2,1,0:T(8,128)(2,1)S(1)}) custom-call(s32[1]{0:T(128)} %bitcast.place_ref, bf16[2,256,2,1024]{3,2,1,0:T(2,128)(2,1)S(1)} %bitcast.18), custom_call_target="tpu_custom_call" | custom-call | tf_op jit(solution)/shard_map/pick/pallas_call | solution.py:87
  18.6 0.0 copy-start.2
  18.6 0.8 copy-done.2
  19.4 0.0 copy-start.3
  19.4 8.9 %psum.7 = f32[32]{0:T(128)S(1)} all-reduce(f32[32]{0:T(128)S(1)} %get-tuple-element.38), channel_id=1, replica_groups=mesh['z'=8,'xh'=2,'co'=2,'xl'=2,'y'=8] {'xh','co'}, use_global_device_ids=true, to_apply=%region_1.0 | all-reduce | flops 32 | bytes 256 | tf_op jit(solution)/shard_map/psum | solution.py:203
  28.3 0.0 collective-permute-done
  28.3 0.0 all-to-all-done.own_ref
  28.3 1.0 broadcast_in_dim.31
  29.3 6.8 %all-to-all-start.1 = ((bf16[8,32,1536]{2,1,0:T(8,128)(2,1)}), bf16[8,32,1536]{2,1,0:T(8,128)(2,1)}, u32[]{:S(2)}, u32[]{:S(2)}) async-start(bf16[8,32,1536]{2,1,0:T(8,128)(2,1)} %broadcast_in_dim.31), calls=%async_computation.1 | async-start | bytes 1572864 | tf_op jit(solution)/shard_map/all_to_all | solution.py:198
  36.1 3.6 %collective-permute-start.1 = (bf16[8,32,1280]{2,1,0:T(8,128)(2,1)}, bf16[8,32,1280]{2,1,0:T(8,128)(2,1)}, u32[]{:S(2)}, u32[]{:S(2)}) collective-permute-start(bf16[8,32,1280]{2,1,0:T(8,128)(2,1)} %all-to-all-done.own_ref), channel_id=1, source_target_pairs={{0,8},{8,0},{1,9},{9,1},{2,10},{10,2},{3,11},{11,3},{4,12},{12,4},... | collective-permute-start | bytes 1966088 | tf_op jit(solution)/shard_map/ppermute | solution.py:207
  39.7 3.2 %collective-permute-start.2 = (bf16[2,2,2,256,128]{4,3,2,1,0:T(8,128)(2,1)}, bf16[2,2,2,256,128]{4,3,2,1,0:T(8,128)(2,1)S(1)}, u32[]{:S(2)}, u32[]{:S(2)}) collective-permute-start(bf16[2,2,2,256,128]{4,3,2,1,0:T(8,128)(2,1)} %get-tuple-element.27), channel_id=1, source_target_pairs={{0,16},{16,0},{32,48},{48,32},{1,17},{17,1},{33,49},{49,33},{2,18}... | collective-permute-start | bytes 1572872 | tf_op jit(solution)/shard_map/ppermute | solution.py:213
  43.0 0.0 copy-done.3
  43.0 3.7 %collective-permute-start.3 = (bf16[2,2,2,256,128]{4,3,2,1,0:T(8,128)(2,1)S(1)}, bf16[2,2,2,256,128]{4,3,2,1,0:T(8,128)(2,1)S(1)}, u32[]{:S(2)}, u32[]{:S(2)}) collective-permute-start(bf16[2,2,2,256,128]{4,3,2,1,0:T(8,128)(2,1)S(1)} %copy-done.3), channel_id=1, source_target_pairs={{0,32},{16,48},{32,0},{48,16},{1,33},{17,49},{33,1},{49,17},{2,34}... | collective-permute-start | bytes 1572872 | tf_op jit(solution)/shard_map/ppermute | solution.py:213
  46.7 3.3 %collective-permute-start.4 = (bf16[2,2,2,256,128]{4,3,2,1,0:T(8,128)(2,1)S(1)}, bf16[2,2,2,256,128]{4,3,2,1,0:T(8,128)(2,1)S(1)}, u32[]{:S(2)}, u32[]{:S(2)}) collective-permute-start(bf16[2,2,2,256,128]{4,3,2,1,0:T(8,128)(2,1)S(1)} %get-tuple-element.29), channel_id=1, source_target_pairs={{0,48},{16,32},{32,16},{48,0},{1,49},{17,33},{33,17},{49,1},{2,50}... | collective-permute-start | bytes 1572872 | tf_op jit(solution)/shard_map/ppermute | solution.py:213
  49.9 3.4 %collective-permute-done.1.theirs_ref = bf16[8,32,1280]{2,1,0:T(8,128)(2,1)} collective-permute-done((bf16[8,32,1280]{2,1,0:T(8,128)(2,1)}, bf16[8,32,1280]{2,1,0:T(8,128)(2,1)}, u32[]{:S(2)}, u32[]{:S(2)}) %collective-permute-start.1) | collective-permute-done | bytes 655392 | tf_op jit(solution)/shard_map/ppermute | solution.py:207
  53.3 5.3 %all-to-all-done.1.rest_ref = bf16[8,32,1536]{2,1,0:T(8,128)(2,1)} async-done(((bf16[8,32,1536]{2,1,0:T(8,128)(2,1)}), bf16[8,32,1536]{2,1,0:T(8,128)(2,1)}, u32[]{:S(2)}, u32[]{:S(2)}) %all-to-all-start.1) | async-done | bytes 786464 | tf_op jit(solution)/shard_map/all_to_all | solution.py:198
  58.6 5.9 %project.1 = bf16[2,16,16,640]{3,2,1,0:T(8,128)(2,1)} custom-call(s32[1]{0:T(128)} %bitcast.1.place_ref, bf16[8,32,1280]{2,1,0:T(8,128)(2,1)} %all-to-all-done.own_ref, bf16[8,32,1280]{2,1,0:T(8,128)(2,1)} %collective-permute-done.1.theirs_ref, bf16[8,32,1536]{2,1,0:T(8,128)(2,1)} %all-to-all-done.1.rest_ref, bf16[2048,512]{1,0:T(8,128)(2,1)} %bitcast.20, ...), custom_call_target="tpu_custom_call" | custom-call | tf_op jit(solution)/shard_map/project/pallas_call | solution.py:61
  64.5 6.6 %all_to_all.25 = bf16[2,16,16,640]{3,2,1,0:T(8,128)(2,1)S(1)} all-to-all(bf16[2,16,16,640]{3,2,1,0:T(8,128)(2,1)} %project.1), channel_id=1, replica_groups=mesh['z'=8,'xh'=2,'co'=2,'xl'=2,'y'=8] {'co'}, dimensions={0} | all-to-all | bytes 1310720 | tf_op jit(solution)/shard_map/all_to_all | solution.py:218
  71.1 0.0 copy-start.1
  71.1 0.1 fusion
  71.2 0.0 collective-permute-done.2.refs_1_
  71.2 0.0 collective-permute-done.3.refs_2_
  71.2 8.5 %collective-permute-done.4.refs_3_ = bf16[2,2,2,256,128]{4,3,2,1,0:T(8,128)(2,1)S(1)} collective-permute-done((bf16[2,2,2,256,128]{4,3,2,1,0:T(8,128)(2,1)S(1)}, bf16[2,2,2,256,128]{4,3,2,1,0:T(8,128)(2,1)S(1)}, u32[]{:S(2)}, u32[]{:S(2)}) %collective-permute-start.4) | collective-permute-done | bytes 524320 | tf_op jit(solution)/shard_map/ppermute | solution.py:213
  79.7 17.8 %all_to_all.26.both_ref = bf16[16,16,640]{2,1,0:T(8,128)(2,1)S(1)} all-to-all(bf16[16,16,640]{2,1,0:T(8,128)(2,1)S(1)} %fusion), channel_id=1, replica_groups=mesh['z'=8,'xh'=2,'co'=2,'xl'=2,'y'=8] {'xl','y'}, dimensions={0} | all-to-all | bytes 655360 | tf_op jit(solution)/shard_map/all_to_all | solution.py:221
  97.5 0.8 arrange.1
  98.3 4.0 %all-to-all-start.4 = ((bf16[4,4,16,1024]{3,2,1,0:T(8,128)(2,1)}), bf16[4,4,16,1024]{3,2,1,0:T(8,128)(2,1)S(1)}, u32[]{:S(2)}, u32[]{:S(2)}) async-start(bf16[4,4,16,1024]{3,2,1,0:T(8,128)(2,1)} %arrange.1), calls=%async_computation.4 | async-start | bytes 1048576 | tf_op jit(solution)/shard_map/all_to_all | solution.py:222
  102.4 0.1 copy.8.scale_ref
  102.5 9.4 %all-to-all-done.4 = bf16[4,4,16,1024]{3,2,1,0:T(8,128)(2,1)S(1)} async-done(((bf16[4,4,16,1024]{3,2,1,0:T(8,128)(2,1)}), bf16[4,4,16,1024]{3,2,1,0:T(8,128)(2,1)S(1)}, u32[]{:S(2)}, u32[]{:S(2)}) %all-to-all-start.4) | async-done | bytes 524320 | tf_op jit(solution)/shard_map/all_to_all | solution.py:222
  111.9 0.0 copy-done.1
  111.9 2.1 %attend.1 = (bf16[32,2048]{1,0:T(8,128)(2,1)S(1)}, bf16[32,2048]{1,0:T(8,128)(2,1)}) custom-call(s32[1,2]{1,0:T(1,128)S(1)} %copy-done.1, s32[1]{0:T(128)} %bitcast.place_ref, bf16[2,2,4,16,1024]{4,3,2,1,0:T(8,128)(2,1)S(1)} %bitcast.17, f32[32,1]{1,0:T(8,128)S(1)} %copy.8.scale_ref, bf16[2,2,2,256,128]{4,3,2,1,0:T(8,128)(2,1)S(1)} %get-tuple-element.32.refs_0_, ...), custom_call_target="tpu_custom_call" | custom-call | tf_op jit(solution)/shard_map/attend/pallas_call | solution.py:178
  114.0 4.0 %collective-permute-start.5 = (bf16[1,32,2048]{2,1,0:T(8,128)(2,1)S(1)}, bf16[1,32,2048]{2,1,0:T(8,128)(2,1)S(1)}, u32[]{:S(2)}, u32[]{:S(2)}) collective-permute-start(bf16[1,32,2048]{2,1,0:T(8,128)(2,1)S(1)} %bitcast.19), channel_id=1, source_target_pairs={{448,0},{0,64},{64,128},{128,192},{192,256},{256,320},{320,384},{3... | collective-permute-start | bytes 393224 | tf_op jit(solution)/shard_map/ppermute | solution.py:228
  118.0 9.6 %collective-permute-done.5 = bf16[1,32,2048]{2,1,0:T(8,128)(2,1)S(1)} collective-permute-done((bf16[1,32,2048]{2,1,0:T(8,128)(2,1)S(1)}, bf16[1,32,2048]{2,1,0:T(8,128)(2,1)S(1)}, u32[]{:S(2)}, u32[]{:S(2)}) %collective-permute-start.5) | collective-permute-done | bytes 131104 | tf_op jit(solution)/shard_map/ppermute | solution.py:228
  127.6 0.7 copy.10
  (4 shorter events, 0.0 us)
Async XLA Ops:
  0.6 12.9 %copy-start = (bf16[1,2,256,2,1024]{4,3,2,1,0:T(2,128)(2,1)S(1)}, bf16[1,2,256,2,1024]{4,3,2,1,0:T(2,128)(2,1)}, u32[]{:S(2)}) copy-start(bf16[1,2,256,2,1024]{4,3,2,1,0:T(2,128)(2,1)} %param.10) | copy-start | bytes 6291460
  2.7 25.5 %all-to-all-start = ((bf16[8,32,1280]{2,1,0:T(8,128)(2,1)}), bf16[8,32,1280]{2,1,0:T(8,128)(2,1)}, u32[]{:S(2)}, u32[]{:S(2)}) async-start(bf16[8,32,1280]{2,1,0:T(8,128)(2,1)} %broadcast_in_dim.30), calls=%async_computation | async-start | bytes 1310720 | tf_op jit(solution)/shard_map/all_to_all | solution.py:198
  10.4 17.9 %collective-permute-start = (bf16[32,768]{1,0:T(8,128)(2,1)S(1)}, bf16[32,768]{1,0:T(8,128)(2,1)S(1)}, u32[]{:S(2)}, u32[]{:S(2)}) collective-permute-start(bf16[32,768]{1,0:T(8,128)(2,1)S(1)} %slice.17), channel_id=1, source_target_pairs={{0,8},{8,0},{1,9},{9,1},{2,10},{10,2},{3,11},{11,3},{4,12},{12,4},... | collective-permute-start | bytes 147464 | tf_op jit(solution)/shard_map/ppermute | solution.py:202
  18.6 0.8 copy-start.2
  19.4 23.5 %copy-start.3 = (bf16[2,2,2,256,128]{4,3,2,1,0:T(8,128)(2,1)S(1)}, bf16[2,2,2,256,128]{4,3,2,1,0:T(8,128)(2,1)}, u32[]{:S(2)}) copy-start(bf16[2,2,2,256,128]{4,3,2,1,0:T(8,128)(2,1)} %copy-done.2) | copy-start | bytes 1572868
  29.3 29.3 %all-to-all-start.1 = ((bf16[8,32,1536]{2,1,0:T(8,128)(2,1)}), bf16[8,32,1536]{2,1,0:T(8,128)(2,1)}, u32[]{:S(2)}, u32[]{:S(2)}) async-start(bf16[8,32,1536]{2,1,0:T(8,128)(2,1)} %broadcast_in_dim.31), calls=%async_computation.1 | async-start | bytes 1572864 | tf_op jit(solution)/shard_map/all_to_all | solution.py:198
  36.1 17.2 %collective-permute-start.1 = (bf16[8,32,1280]{2,1,0:T(8,128)(2,1)}, bf16[8,32,1280]{2,1,0:T(8,128)(2,1)}, u32[]{:S(2)}, u32[]{:S(2)}) collective-permute-start(bf16[8,32,1280]{2,1,0:T(8,128)(2,1)} %all-to-all-done.own_ref), channel_id=1, source_target_pairs={{0,8},{8,0},{1,9},{9,1},{2,10},{10,2},{3,11},{11,3},{4,12},{12,4},... | collective-permute-start | bytes 1966088 | tf_op jit(solution)/shard_map/ppermute | solution.py:207
  39.7 31.5 %collective-permute-start.2 = (bf16[2,2,2,256,128]{4,3,2,1,0:T(8,128)(2,1)}, bf16[2,2,2,256,128]{4,3,2,1,0:T(8,128)(2,1)S(1)}, u32[]{:S(2)}, u32[]{:S(2)}) collective-permute-start(bf16[2,2,2,256,128]{4,3,2,1,0:T(8,128)(2,1)} %get-tuple-element.27), channel_id=1, source_target_pairs={{0,16},{16,0},{32,48},{48,32},{1,17},{17,1},{33,49},{49,33},{2,18}... | collective-permute-start | bytes 1572872 | tf_op jit(solution)/shard_map/ppermute | solution.py:213
  43.0 28.3 %collective-permute-start.3 = (bf16[2,2,2,256,128]{4,3,2,1,0:T(8,128)(2,1)S(1)}, bf16[2,2,2,256,128]{4,3,2,1,0:T(8,128)(2,1)S(1)}, u32[]{:S(2)}, u32[]{:S(2)}) collective-permute-start(bf16[2,2,2,256,128]{4,3,2,1,0:T(8,128)(2,1)S(1)} %copy-done.3), channel_id=1, source_target_pairs={{0,32},{16,48},{32,0},{48,16},{1,33},{17,49},{33,1},{49,17},{2,34}... | collective-permute-start | bytes 1572872 | tf_op jit(solution)/shard_map/ppermute | solution.py:213
  46.7 33.0 %collective-permute-start.4 = (bf16[2,2,2,256,128]{4,3,2,1,0:T(8,128)(2,1)S(1)}, bf16[2,2,2,256,128]{4,3,2,1,0:T(8,128)(2,1)S(1)}, u32[]{:S(2)}, u32[]{:S(2)}) collective-permute-start(bf16[2,2,2,256,128]{4,3,2,1,0:T(8,128)(2,1)S(1)} %get-tuple-element.29), channel_id=1, source_target_pairs={{0,48},{16,32},{32,16},{48,0},{1,49},{17,33},{33,17},{49,1},{2,50}... | collective-permute-start | bytes 1572872 | tf_op jit(solution)/shard_map/ppermute | solution.py:213
  71.1 40.7 %copy-start.1 = (s32[1,2]{1,0:T(1,128)S(1)}, s32[1,2]{1,0:T(1,128)}, u32[]{:S(2)}) copy-start(s32[1,2]{1,0:T(1,128)} %lengths_ref.1) | copy-start | bytes 28
  98.3 13.5 %all-to-all-start.4 = ((bf16[4,4,16,1024]{3,2,1,0:T(8,128)(2,1)}), bf16[4,4,16,1024]{3,2,1,0:T(8,128)(2,1)S(1)}, u32[]{:S(2)}, u32[]{:S(2)}) async-start(bf16[4,4,16,1024]{3,2,1,0:T(8,128)(2,1)} %arrange.1), calls=%async_computation.4 | async-start | bytes 1048576 | tf_op jit(solution)/shard_map/all_to_all | solution.py:222
  114.0 13.6 %collective-permute-start.5 = (bf16[1,32,2048]{2,1,0:T(8,128)(2,1)S(1)}, bf16[1,32,2048]{2,1,0:T(8,128)(2,1)S(1)}, u32[]{:S(2)}, u32[]{:S(2)}) collective-permute-start(bf16[1,32,2048]{2,1,0:T(8,128)(2,1)S(1)} %bitcast.19), channel_id=1, source_target_pairs={{448,0},{0,64},{64,128},{128,192},{192,256},{256,320},{320,384},{3... | collective-permute-start | bytes 393224 | tf_op jit(solution)/shard_map/ppermute | solution.py:228

commit v5 on v4

--- a/solution.py
+++ b/solution.py
@@ -13,7 +13,7 @@
 COL = ("xl", "y")
 BF = jnp.bfloat16
 F32 = jnp.float32
-FIRST = 1280
+FIRST = 1152
 VMEM = pl.BlockSpec(memory_space=pltpu.VMEM)
 HBM = pl.BlockSpec(memory_space=pltpu.HBM)
 SMEM = pl.BlockSpec(memory_space=pltpu.SMEM)
@@ -21,35 +21,42 @@
 FULL = pltpu.CompilerParams(vmem_limit_bytes=56 * 1024 * 1024)
 
 
-def project_kernel(place_ref, own_ref, theirs_ref, rest_ref, query_ref, pair_ref, out_ref, query, pair, sems):
+def project_kernel(place_ref, own_ref, theirs_ref, rest_ref, query_ref, pair_ref, out_ref, *scratch):
+    own, theirs, rest, query, pair, sems = scratch
     count, rows, first = own_ref.shape
     remainder = rest_ref.shape[2] // 2
     half = rows // 2
     mine = place_ref[0] * count
     other = (1 - place_ref[0]) * count
-    copies = []
-    for lines in (pl.ds(0, first), pl.ds(first, remainder)):
-        for source, target in ((query_ref, query), (pair_ref, pair)):
-            n = len(copies)
-            copies.append(pltpu.make_async_copy(source.at[lines], target.at[lines], sems.at[n]))
+    former_lines, latter_lines = pl.ds(0, first), pl.ds(first, remainder)
+    moves = (
+        (own_ref, own),
+        (query_ref.at[former_lines], query.at[former_lines]),
+        (pair_ref.at[former_lines], pair.at[former_lines]),
+        (theirs_ref, theirs),
+        (rest_ref, rest),
+        (query_ref.at[latter_lines], query.at[latter_lines]),
+        (pair_ref.at[latter_lines], pair.at[latter_lines]),
+    )
+    copies = [pltpu.make_async_copy(a, b, sems.at[n]) for n, (a, b) in enumerate(moves)]
     for copy in copies:
         copy.start()
 
-    def flat(block):
-        return block.reshape(count * rows, block.shape[2])
-
     def times(block, lines):
+        block = block.reshape(count * rows, block.shape[2])
         return [
             jnp.dot(block, weight[lines], preferred_element_type=F32) for weight in (query, pair)
         ]
 
-    copies[0].wait()
-    copies[1].wait()
-    former = [times(flat(ref[...]), slice(0, first)) for ref in (own_ref, theirs_ref)]
-    copies[2].wait()
+    for copy in copies[:3]:
+        copy.wait()
+    former = [times(own[...], slice(0, first))]
     copies[3].wait()
+    former.append(times(theirs[...], slice(0, first)))
+    for copy in copies[4:]:
+        copy.wait()
     for n, start in enumerate((mine, other)):
-        block = flat(rest_ref[:, :, n * remainder : (n + 1) * remainder])
+        block = rest[:, :, n * remainder : (n + 1) * remainder]
         latter = times(block, slice(first, first + remainder))
         for part, more, lanes in zip(former[n], latter, (slice(0, 512), slice(512, 640))):
             part = (part + more).astype(BF).reshape(count, 2, half, part.shape[1])
@@ -57,39 +64,36 @@
                 out_ref[h, pl.ds(start, count), :, lanes] = part[:, h]
 
 
-def project(place, own, theirs, rest, query_weight, pair_weight):
+def project(place, *operands):
     return pl.pallas_call(
         project_kernel,
         out_shape=jax.ShapeDtypeStruct((2, 16, 16, 640), BF),
-        in_specs=[SMEM, VMEM, VMEM, VMEM, HBM, HBM],
+        in_specs=[SMEM] + [HBM] * 5,
         out_specs=VMEM,
-        scratch_shapes=[
-            pltpu.VMEM(query_weight.shape, BF),
-            pltpu.VMEM(pair_weight.shape, BF),
-            pltpu.SemaphoreType.DMA((4,)),
-        ],
+        scratch_shapes=[pltpu.VMEM(x.shape, BF) for x in operands] + [pltpu.SemaphoreType.DMA((7,))],
         compiler_params=FULL,
         name="project",
-    )(place, own, theirs, rest, query_weight, pair_weight)
-
-
-def pick_kernel(place_ref, cache_ref, *pieces):
-    for k, piece_ref in enumerate(pieces):
-        for g in range(2):
-            at = pl.multiple_of((place_ref[0] ^ k) * 256 + g * HEAD_DIM, HEAD_DIM)
-            block = cache_ref[0, :, :, pl.ds(at, HEAD_DIM)]
-            for v in range(2):
-                piece_ref[0, v, g] = block[:, v, :]
-
-
-def pick(place, cache):
+    )(place, *operands)
+
+
+def pick(places, place, cache):
     prompts, chunk = cache.shape[:2]
+
+    def pick_kernel(place_ref, cache_ref, *pieces):
+        for k, piece_ref in zip(places, pieces):
+            for g in range(2):
+                at = pl.multiple_of((place_ref[0] ^ k) * 256 + g * HEAD_DIM, HEAD_DIM)
+                block = cache_ref[0, :, :, pl.ds(at, HEAD_DIM)]
+                for v in range(2):
+                    piece_ref[0, v, g] = block[:, v, :]
+
+    block = pl.BlockSpec((1, 2, 2, chunk, HEAD_DIM), lambda p: (p, 0, 0, 0, 0))
     return pl.pallas_call(
         pick_kernel,
         grid=(prompts,),
-        out_shape=[jax.ShapeDtypeStruct((prompts, 2, 2, chunk, HEAD_DIM), BF)] * 4,
+        out_shape=[jax.ShapeDtypeStruct((prompts, 2, 2, chunk, HEAD_DIM), BF)] * len(places),
         in_specs=[SMEM, pl.BlockSpec((1,) + cache.shape[1:], lambda p: (p, 0, 0, 0))],
-        out_specs=[pl.BlockSpec((1, 2, 2, chunk, HEAD_DIM), lambda p: (p, 0, 0, 0, 0))] * 4,
+        out_specs=[block] * len(places),
         compiler_params=PARAMS,
         name="pick",
     )(place, cache)
@@ -197,21 +201,22 @@
     def spread(block):
         return lax.all_to_all(jnp.broadcast_to(block[None], (8,) + block.shape), "y", 0, 0)
 
+    def exchanged(piece, k):
+        return lax.ppermute(piece, ROW, [(i, i ^ k) for i in range(row_count)])
+
     own = spread(sent[:, :FIRST])
+    across = exchanged(pick((2,), row_index[None], kv_cache[0])[0], 2)
     rest = sent[:, FIRST:]
     rest = jnp.concatenate([rest, lax.ppermute(rest, "xl", swap)], axis=1)
-    squares = lax.psum(local_squares, ROW)
-    own, rest, pieces, squares = lax.optimization_barrier(
-        (own, rest, pick(row_index[None], kv_cache[0]), squares)
+    pieces = pick((0, 1, 3), row_index[None], kv_cache[0])
+    own, rest, pieces, across, local_squares = lax.optimization_barrier(
+        (own, rest, pieces, across, local_squares)
     )
     theirs = lax.ppermute(own, "xl", swap)
     rest = spread(rest)
-
-    caches = []
-    for k, piece in enumerate(pieces):
-        if k:
-            piece = lax.ppermute(piece, ROW, [(i, i ^ k) for i in range(row_count)])
-        caches.append(piece)
+    caches = [pieces[0], exchanged(pieces[1], 1), across, exchanged(pieces[2], 3)]
+    squares = lax.psum(local_squares, ROW)
+    theirs, rest, squares = lax.optimization_barrier((theirs, rest, squares))
 
     place = lax.axis_index("xl")[None]
     partial = project(place, own, theirs, rest, q_weight[0], kv_weight[0])

time: 130 us -> 130 us (level)
  waiting for transfers between devices: 36.2 us -> 24.9 us
  blocking collectives: 33.3 us -> 43.3 us
  starting transfers between devices: 39.4 us -> 41.6 us
    psum x1, blocking collectives: 8.86 us -> 19.1 us  [shards(): squares = lax.psum(local_squares, ROW)]
    ppermute x3, waiting for transfers between devices: 8.47 us -> 0.01 us  [exchanged(): return lax.ppermute(piece, ROW, [(i, i ^ k) for i in range(row_count)])]
    ppermute x1, waiting for transfers between devices: 0.01 us -> 5.89 us  [shards(): rest = jnp.concatenate([rest, lax.ppermute(rest, 'xl', swap)], axis=1)]
    all_to_all x2, waiting for transfers between devices: 5.3 us -> 0.01 us  [spread(): lax.all_to_all(jnp.broadcast_to(block[None], (8,) + block.shape), 'y', 0, 0)]
    ppermute x1, waiting for transfers between devices: 3.38 us -> 0.01 us  [shards(): theirs = lax.ppermute(own, 'xl', swap)]
    ppermute x3, starting transfers between devices: 10.2 us -> 12.9 us  [exchanged(): return lax.ppermute(piece, ROW, [(i, i ^ k) for i in range(row_count)])]
    all_to_all x1, starting transfers between devices: 4.03 us -> 5.56 us  [shards(): parts = lax.all_to_all(arrange(both), ROW, 0, 0)]
    pallas_call x1 -> x2, Pallas kernels: 5.05 us -> 4.95 us  [pick(): pl.pallas_call(pick_kernel, grid=(prompts,), out_shape=[jax.ShapeDtypeStr...]
  transfers between devices with their start and end apart: 9 -> 9, of which waited for: 5 -> 3; matrix products, arithmetic and copies ran while one was open for 0% -> 0% of each run, Pallas kernels for 9% -> 8%
where the time goes in v5:
time: 130 us; the launch traced here: 129 us
  blocking collectives  43.3 us (33%)
  starting transfers between devices  41.6 us (32%)
  waiting for transfers between devices  24.9 us (19%)
  Pallas kernels  13.1 us (10%)
  local copies, waits for them, and re-layouts  4.34 us (3%)
  other arithmetic  1.3 us (1%)
    psum x1, blocking collectives, shards(): squares = lax.psum(local_squares, ROW)  19.1 us
    all_to_all x1, blocking collectives, shards(): both = lax.all_to_all(both, COL, 0, 0)  16.8 us
    all_to_all x2, starting transfers between devices, spread(): lax.all_to_all(jnp.broadcast_to(block[None], (8,) + block.shape), 'y', 0, 0)  13.9 us
    ppermute x3, starting transfers between devices, exchanged(): return lax.ppermute(piece, ROW, [(i, i ^ k) for i in range(row_count)])  12.9 us
    ppermute x1, waiting for transfers between devices, shards(): lax.ppermute(attended[None], 'z', [((i - 1) % count, i) for i in range(co...  9.65 us
    all_to_all x1, waiting for transfers between devices, shards(): parts = lax.all_to_all(arrange(both), ROW, 0, 0)  9.39 us
    all_to_all x1, blocking collectives, shards(): partial = lax.all_to_all(partial, 'co', 0, 0)  7.45 us
    ppermute x1, waiting for transfers between devices, shards(): rest = jnp.concatenate([rest, lax.ppermute(rest, 'xl', swap)], axis=1)  5.89 us
  transfers between devices with their start and end apart: 9, of which 3 were waited for; matrix products, arithmetic and copies ran while one was open for 0% of the time, Pallas kernels for 8%

profile of v5, /device:TPU:1, one launch (start us, length us, event | category | flops | bytes accessed | tf_op | source)
XLA Modules:
  0.0 129.3 jit_solution(13456705755755034270)
XLA Ops:
  0.6 0.0 copy-start
  0.6 1.2 fusion.2
  1.9 0.9 broadcast_in_dim.31
  2.7 7.7 %all-to-all-start = ((bf16[8,32,1152]{2,1,0:T(8,128)(2,1)}), bf16[8,32,1152]{2,1,0:T(8,128)(2,1)}, u32[]{:S(2)}, u32[]{:S(2)}) async-start(bf16[8,32,1152]{2,1,0:T(8,128)(2,1)} %broadcast_in_dim.31), calls=%async_computation | async-start | bytes 1179648 | tf_op jit(solution)/shard_map/all_to_all | solution.py:202
  10.4 0.0 copy-done
  10.4 1.2 pick.3
  11.6 4.7 %collective-permute-start.1 = (bf16[2,2,2,256,128]{4,3,2,1,0:T(8,128)(2,1)S(1)}, bf16[2,2,2,256,128]{4,3,2,1,0:T(8,128)(2,1)S(1)}, u32[]{:S(2)}, u32[]{:S(2)}) collective-permute-start(bf16[2,2,2,256,128]{4,3,2,1,0:T(8,128)(2,1)S(1)} %pick.3), channel_id=1, source_target_pairs={{0,32},{16,48},{32,0},{48,16},{1,33},{17,49},{33,1},{49,17},{2,34}... | collective-permute-start | bytes 1572872 | tf_op jit(solution)/shard_map/ppermute | solution.py:205
  16.3 2.2 %collective-permute-start = (bf16[32,896]{1,0:T(8,128)(2,1)S(1)}, bf16[32,896]{1,0:T(8,128)(2,1)S(1)}, u32[]{:S(2)}, u32[]{:S(2)}) collective-permute-start(bf16[32,896]{1,0:T(8,128)(2,1)S(1)} %slice.17), channel_id=1, source_target_pairs={{0,8},{8,0},{1,9},{9,1},{2,10},{10,2},{3,11},{11,3},{4,12},{12,4},... | collective-permute-start | bytes 172040 | tf_op jit(solution)/shard_map/ppermute | solution.py:210
  18.5 3.7 %pick.2 = (bf16[2,2,2,256,128]{4,3,2,1,0:T(8,128)(2,1)S(1)}, bf16[2,2,2,256,128]{4,3,2,1,0:T(8,128)(2,1)}, bf16[2,2,2,256,128]{4,3,2,1,0:T(8,128)(2,1)S(1)}) custom-call(s32[1]{0:T(128)} %bitcast.place_ref, bf16[2,256,2,1024]{3,2,1,0:T(2,128)(2,1)S(1)} %bitcast.18), custom_call_target="tpu_custom_call" | custom-call | tf_op jit(solution)/shard_map/pick/pallas_call | solution.py:91
  22.2 0.0 copy-start.2
  22.2 0.8 copy-done.2
  23.0 5.9 %collective-permute-done = bf16[32,896]{1,0:T(8,128)(2,1)S(1)} collective-permute-done((bf16[32,896]{1,0:T(8,128)(2,1)S(1)}, bf16[32,896]{1,0:T(8,128)(2,1)S(1)}, u32[]{:S(2)}, u32[]{:S(2)}) %collective-permute-start) | collective-permute-done | bytes 57376 | tf_op jit(solution)/shard_map/ppermute | solution.py:210
  28.9 0.0 copy-start.3
  28.9 0.0 collective-permute-done.1.refs_2_
  29.0 0.0 all-to-all-done.own_ref
  29.0 1.1 broadcast_in_dim.32
  30.0 6.2 %all-to-all-start.1 = ((bf16[8,32,1792]{2,1,0:T(8,128)(2,1)}), bf16[8,32,1792]{2,1,0:T(8,128)(2,1)}, u32[]{:S(2)}, u32[]{:S(2)}) async-start(bf16[8,32,1792]{2,1,0:T(8,128)(2,1)} %broadcast_in_dim.32), calls=%async_computation.1 | async-start | bytes 1835008 | tf_op jit(solution)/shard_map/all_to_all | solution.py:202
  36.3 3.0 %collective-permute-start.2 = (bf16[8,32,1152]{2,1,0:T(8,128)(2,1)}, bf16[8,32,1152]{2,1,0:T(8,128)(2,1)S(1)}, u32[]{:S(2)}, u32[]{:S(2)}) collective-permute-start(bf16[8,32,1152]{2,1,0:T(8,128)(2,1)} %all-to-all-done.own_ref), channel_id=1, source_target_pairs={{0,8},{8,0},{1,9},{9,1},{2,10},{10,2},{3,11},{11,3},{4,12},{12,4},... | collective-permute-start | bytes 1769480 | tf_op jit(solution)/shard_map/ppermute | solution.py:215
  39.3 4.6 %collective-permute-start.3 = (bf16[2,2,2,256,128]{4,3,2,1,0:T(8,128)(2,1)}, bf16[2,2,2,256,128]{4,3,2,1,0:T(8,128)(2,1)S(1)}, u32[]{:S(2)}, u32[]{:S(2)}) collective-permute-start(bf16[2,2,2,256,128]{4,3,2,1,0:T(8,128)(2,1)} %get-tuple-element.31), channel_id=1, source_target_pairs={{0,16},{16,0},{32,48},{48,32},{1,17},{17,1},{33,49},{49,33},{2,18}... | collective-permute-start | bytes 1572872 | tf_op jit(solution)/shard_map/ppermute | solution.py:205
  44.0 0.0 copy-done.3
  44.0 3.6 %collective-permute-start.4 = (bf16[2,2,2,256,128]{4,3,2,1,0:T(8,128)(2,1)S(1)}, bf16[2,2,2,256,128]{4,3,2,1,0:T(8,128)(2,1)S(1)}, u32[]{:S(2)}, u32[]{:S(2)}) collective-permute-start(bf16[2,2,2,256,128]{4,3,2,1,0:T(8,128)(2,1)S(1)} %copy-done.3), channel_id=1, source_target_pairs={{0,48},{16,32},{32,16},{48,0},{1,49},{17,33},{33,17},{49,1},{2,50}... | collective-permute-start | bytes 1572872 | tf_op jit(solution)/shard_map/ppermute | solution.py:205
  47.6 19.1 %psum.7 = f32[32]{0:T(128)S(1)} all-reduce(f32[32]{0:T(128)S(1)} %get-tuple-element.27), channel_id=1, replica_groups=mesh['z'=8,'xh'=2,'co'=2,'xl'=2,'y'=8] {'xh','co'}, use_global_device_ids=true, to_apply=%region_1.0 | all-reduce | flops 32 | bytes 256 | tf_op jit(solution)/shard_map/psum | solution.py:218
  66.6 0.0 collective-permute-done.2.theirs_ref
  66.6 0.0 copy-start.4
  66.6 0.0 all-to-all-done.1.rest_ref
  66.6 0.8 copy-done.4
  67.4 5.2 %project.1 = bf16[2,16,16,640]{3,2,1,0:T(8,128)(2,1)} custom-call(s32[1]{0:T(128)} %bitcast.1.place_ref, bf16[8,32,1152]{2,1,0:T(8,128)(2,1)} %all-to-all-done.own_ref, bf16[8,32,1152]{2,1,0:T(8,128)(2,1)} %copy-done.4, bf16[8,32,1792]{2,1,0:T(8,128)(2,1)} %all-to-all-done.1.rest_ref, bf16[2048,512]{1,0:T(8,128)(2,1)} %bitcast.21, bf16[2048,128]{1,0:T(8,128)(2,1)} %bitcast.22), custom_call_target="tpu_custom_call" | custom-call | tf_op jit(solution)/shard_map/project/pallas_call | solution.py:68
  72.6 7.5 %all_to_all.25 = bf16[2,16,16,640]{3,2,1,0:T(8,128)(2,1)S(1)} all-to-all(bf16[2,16,16,640]{3,2,1,0:T(8,128)(2,1)} %project.1), channel_id=1, replica_groups=mesh['z'=8,'xh'=2,'co'=2,'xl'=2,'y'=8] {'co'}, dimensions={0} | all-to-all | bytes 1310720 | tf_op jit(solution)/shard_map/all_to_all | solution.py:223
  80.1 0.0 copy-start.1
  80.1 0.1 fusion
  80.2 0.0 collective-permute-done.3.refs_1_
  80.2 0.0 collective-permute-done.4.refs_3_
  80.2 16.8 %all_to_all.26.both_ref = bf16[16,16,640]{2,1,0:T(8,128)(2,1)S(1)} all-to-all(bf16[16,16,640]{2,1,0:T(8,128)(2,1)S(1)} %fusion), channel_id=1, replica_groups=mesh['z'=8,'xh'=2,'co'=2,'xl'=2,'y'=8] {'xl','y'}, dimensions={0} | all-to-all | bytes 655360 | tf_op jit(solution)/shard_map/all_to_all | solution.py:226
  97.0 0.8 arrange.1
  97.8 5.6 %all-to-all-start.4 = ((bf16[4,4,16,1024]{3,2,1,0:T(8,128)(2,1)}), bf16[4,4,16,1024]{3,2,1,0:T(8,128)(2,1)S(1)}, u32[]{:S(2)}, u32[]{:S(2)}) async-start(bf16[4,4,16,1024]{3,2,1,0:T(8,128)(2,1)} %arrange.1), calls=%async_computation.4 | async-start | bytes 1048576 | tf_op jit(solution)/shard_map/all_to_all | solution.py:227
  103.3 0.1 copy.8.scale_ref
  103.4 9.4 %all-to-all-done.4 = bf16[4,4,16,1024]{3,2,1,0:T(8,128)(2,1)S(1)} async-done(((bf16[4,4,16,1024]{3,2,1,0:T(8,128)(2,1)}), bf16[4,4,16,1024]{3,2,1,0:T(8,128)(2,1)S(1)}, u32[]{:S(2)}, u32[]{:S(2)}) %all-to-all-start.4) | async-done | bytes 524320 | tf_op jit(solution)/shard_map/all_to_all | solution.py:227
  112.8 0.0 copy-done.1
  112.8 2.1 %attend.1 = (bf16[32,2048]{1,0:T(8,128)(2,1)S(1)}, bf16[32,2048]{1,0:T(8,128)(2,1)}) custom-call(s32[1,2]{1,0:T(1,128)S(1)} %copy-done.1, s32[1]{0:T(128)} %bitcast.place_ref, bf16[2,2,4,16,1024]{4,3,2,1,0:T(8,128)(2,1)S(1)} %bitcast.19, f32[32,1]{1,0:T(8,128)S(1)} %copy.8.scale_ref, bf16[2,2,2,256,128]{4,3,2,1,0:T(8,128)(2,1)S(1)} %get-tuple-element.36.refs_0_, ...), custom_call_target="tpu_custom_call" | custom-call | tf_op jit(solution)/shard_map/attend/pallas_call | solution.py:182
  115.0 4.0 %collective-permute-start.5 = (bf16[1,32,2048]{2,1,0:T(8,128)(2,1)S(1)}, bf16[1,32,2048]{2,1,0:T(8,128)(2,1)S(1)}, u32[]{:S(2)}, u32[]{:S(2)}) collective-permute-start(bf16[1,32,2048]{2,1,0:T(8,128)(2,1)S(1)} %bitcast.20), channel_id=1, source_target_pairs={{448,0},{0,64},{64,128},{128,192},{192,256},{256,320},{320,384},{3... | collective-permute-start | bytes 393224 | tf_op jit(solution)/shard_map/ppermute | solution.py:233
  119.0 9.7 %collective-permute-done.5 = bf16[1,32,2048]{2,1,0:T(8,128)(2,1)S(1)} collective-permute-done((bf16[1,32,2048]{2,1,0:T(8,128)(2,1)S(1)}, bf16[1,32,2048]{2,1,0:T(8,128)(2,1)S(1)}, u32[]{:S(2)}, u32[]{:S(2)}) %collective-permute-start.5) | collective-permute-done | bytes 131104 | tf_op jit(solution)/shard_map/ppermute | solution.py:233
  128.6 0.7 copy.10
  (4 shorter events, 0.0 us)
Async XLA Ops:
  0.6 9.7 %copy-start = (bf16[1,2,256,2,1024]{4,3,2,1,0:T(2,128)(2,1)S(1)}, bf16[1,2,256,2,1024]{4,3,2,1,0:T(2,128)(2,1)}, u32[]{:S(2)}) copy-start(bf16[1,2,256,2,1024]{4,3,2,1,0:T(2,128)(2,1)} %param.10) | copy-start | bytes 6291460
  2.7 26.2 %all-to-all-start = ((bf16[8,32,1152]{2,1,0:T(8,128)(2,1)}), bf16[8,32,1152]{2,1,0:T(8,128)(2,1)}, u32[]{:S(2)}, u32[]{:S(2)}) async-start(bf16[8,32,1152]{2,1,0:T(8,128)(2,1)} %broadcast_in_dim.31), calls=%async_computation | async-start | bytes 1179648 | tf_op jit(solution)/shard_map/all_to_all | solution.py:202
  11.6 17.3 %collective-permute-start.1 = (bf16[2,2,2,256,128]{4,3,2,1,0:T(8,128)(2,1)S(1)}, bf16[2,2,2,256,128]{4,3,2,1,0:T(8,128)(2,1)S(1)}, u32[]{:S(2)}, u32[]{:S(2)}) collective-permute-start(bf16[2,2,2,256,128]{4,3,2,1,0:T(8,128)(2,1)S(1)} %pick.3), channel_id=1, source_target_pairs={{0,32},{16,48},{32,0},{48,16},{1,33},{17,49},{33,1},{49,17},{2,34}... | collective-permute-start | bytes 1572872 | tf_op jit(solution)/shard_map/ppermute | solution.py:205
  16.3 12.6 %collective-permute-start = (bf16[32,896]{1,0:T(8,128)(2,1)S(1)}, bf16[32,896]{1,0:T(8,128)(2,1)S(1)}, u32[]{:S(2)}, u32[]{:S(2)}) collective-permute-start(bf16[32,896]{1,0:T(8,128)(2,1)S(1)} %slice.17), channel_id=1, source_target_pairs={{0,8},{8,0},{1,9},{9,1},{2,10},{10,2},{3,11},{11,3},{4,12},{12,4},... | collective-permute-start | bytes 172040 | tf_op jit(solution)/shard_map/ppermute | solution.py:210
  22.2 0.8 copy-start.2
  28.9 15.0 %copy-start.3 = (bf16[2,2,2,256,128]{4,3,2,1,0:T(8,128)(2,1)S(1)}, bf16[2,2,2,256,128]{4,3,2,1,0:T(8,128)(2,1)}, u32[]{:S(2)}) copy-start(bf16[2,2,2,256,128]{4,3,2,1,0:T(8,128)(2,1)} %copy-done.2) | copy-start | bytes 1572868
  30.0 36.6 %all-to-all-start.1 = ((bf16[8,32,1792]{2,1,0:T(8,128)(2,1)}), bf16[8,32,1792]{2,1,0:T(8,128)(2,1)}, u32[]{:S(2)}, u32[]{:S(2)}) async-start(bf16[8,32,1792]{2,1,0:T(8,128)(2,1)} %broadcast_in_dim.32), calls=%async_computation.1 | async-start | bytes 1835008 | tf_op jit(solution)/shard_map/all_to_all | solution.py:202
  36.3 30.4 %collective-permute-start.2 = (bf16[8,32,1152]{2,1,0:T(8,128)(2,1)}, bf16[8,32,1152]{2,1,0:T(8,128)(2,1)S(1)}, u32[]{:S(2)}, u32[]{:S(2)}) collective-permute-start(bf16[8,32,1152]{2,1,0:T(8,128)(2,1)} %all-to-all-done.own_ref), channel_id=1, source_target_pairs={{0,8},{8,0},{1,9},{9,1},{2,10},{10,2},{3,11},{11,3},{4,12},{12,4},... | collective-permute-start | bytes 1769480 | tf_op jit(solution)/shard_map/ppermute | solution.py:215
  39.3 40.9 %collective-permute-start.3 = (bf16[2,2,2,256,128]{4,3,2,1,0:T(8,128)(2,1)}, bf16[2,2,2,256,128]{4,3,2,1,0:T(8,128)(2,1)S(1)}, u32[]{:S(2)}, u32[]{:S(2)}) collective-permute-start(bf16[2,2,2,256,128]{4,3,2,1,0:T(8,128)(2,1)} %get-tuple-element.31), channel_id=1, source_target_pairs={{0,16},{16,0},{32,48},{48,32},{1,17},{17,1},{33,49},{49,33},{2,18}... | collective-permute-start | bytes 1572872 | tf_op jit(solution)/shard_map/ppermute | solution.py:205
  44.0 36.2 %collective-permute-start.4 = (bf16[2,2,2,256,128]{4,3,2,1,0:T(8,128)(2,1)S(1)}, bf16[2,2,2,256,128]{4,3,2,1,0:T(8,128)(2,1)S(1)}, u32[]{:S(2)}, u32[]{:S(2)}) collective-permute-start(bf16[2,2,2,256,128]{4,3,2,1,0:T(8,128)(2,1)S(1)} %copy-done.3), channel_id=1, source_target_pairs={{0,48},{16,32},{32,16},{48,0},{1,49},{17,33},{33,17},{49,1},{2,50}... | collective-permute-start | bytes 1572872 | tf_op jit(solution)/shard_map/ppermute | solution.py:205
  66.6 0.8 copy-start.4
  80.1 32.7 %copy-start.1 = (s32[1,2]{1,0:T(1,128)S(1)}, s32[1,2]{1,0:T(1,128)}, u32[]{:S(2)}) copy-start(s32[1,2]{1,0:T(1,128)} %lengths_ref.1) | copy-start | bytes 28
  97.8 15.0 %all-to-all-start.4 = ((bf16[4,4,16,1024]{3,2,1,0:T(8,128)(2,1)}), bf16[4,4,16,1024]{3,2,1,0:T(8,128)(2,1)S(1)}, u32[]{:S(2)}, u32[]{:S(2)}) async-start(bf16[4,4,16,1024]{3,2,1,0:T(8,128)(2,1)} %arrange.1), calls=%async_computation.4 | async-start | bytes 1048576 | tf_op jit(solution)/shard_map/all_to_all | solution.py:227
  115.0 13.7 %collective-permute-start.5 = (bf16[1,32,2048]{2,1,0:T(8,128)(2,1)S(1)}, bf16[1,32,2048]{2,1,0:T(8,128)(2,1)S(1)}, u32[]{:S(2)}, u32[]{:S(2)}) collective-permute-start(bf16[1,32,2048]{2,1,0:T(8,128)(2,1)S(1)} %bitcast.20), channel_id=1, source_target_pairs={{448,0},{0,64},{64,128},{128,192},{192,256},{256,320},{320,384},{3... | collective-permute-start | bytes 393224 | tf_op jit(solution)/shard_map/ppermute | solution.py:233

commit v6 on v5

--- a/solution.py
+++ b/solution.py
@@ -13,7 +13,7 @@
 COL = ("xl", "y")
 BF = jnp.bfloat16
 F32 = jnp.float32
-FIRST = 1152
+FIRST = 1024
 VMEM = pl.BlockSpec(memory_space=pltpu.VMEM)
 HBM = pl.BlockSpec(memory_space=pltpu.HBM)
 SMEM = pl.BlockSpec(memory_space=pltpu.SMEM)
@@ -21,7 +21,7 @@
 FULL = pltpu.CompilerParams(vmem_limit_bytes=56 * 1024 * 1024)
 
 
-def project_kernel(place_ref, own_ref, theirs_ref, rest_ref, query_ref, pair_ref, out_ref, *scratch):
+def project_kernel(place_ref, own_ref, theirs_ref, rest_ref, query_ref, pair_ref, keep_ref, send_ref, *scratch):
     own, theirs, rest, query, pair, sems = scratch
     count, rows, first = own_ref.shape
     remainder = rest_ref.shape[2] // 2
@@ -60,16 +60,20 @@
         latter = times(block, slice(first, first + remainder))
         for part, more, lanes in zip(former[n], latter, (slice(0, 512), slice(512, 640))):
             part = (part + more).astype(BF).reshape(count, 2, half, part.shape[1])
-            for h in range(2):
-                out_ref[h, pl.ds(start, count), :, lanes] = part[:, h]
+            for core in range(2):
+
+                @pl.when(place_ref[1] == core)
+                def _():
+                    keep_ref[pl.ds(start, count), :, lanes] = part[:, core]
+                    send_ref[pl.ds(start, count), :, lanes] = part[:, 1 - core]
 
 
 def project(place, *operands):
     return pl.pallas_call(
         project_kernel,
-        out_shape=jax.ShapeDtypeStruct((2, 16, 16, 640), BF),
+        out_shape=[jax.ShapeDtypeStruct((16, 16, 640), BF)] * 2,
         in_specs=[SMEM] + [HBM] * 5,
-        out_specs=VMEM,
+        out_specs=[VMEM] * 2,
         scratch_shapes=[pltpu.VMEM(x.shape, BF) for x in operands] + [pltpu.SemaphoreType.DMA((7,))],
         compiler_params=FULL,
         name="project",
@@ -209,21 +213,19 @@
     rest = sent[:, FIRST:]
     rest = jnp.concatenate([rest, lax.ppermute(rest, "xl", swap)], axis=1)
     pieces = pick((0, 1, 3), row_index[None], kv_cache[0])
-    own, rest, pieces, across, local_squares = lax.optimization_barrier(
-        (own, rest, pieces, across, local_squares)
-    )
+    rest, own, pieces, across = lax.optimization_barrier((rest, own, pieces, across))
     theirs = lax.ppermute(own, "xl", swap)
     rest = spread(rest)
     caches = [pieces[0], exchanged(pieces[1], 1), across, exchanged(pieces[2], 3)]
+
+    place = jnp.stack([lax.axis_index("xl"), lax.axis_index("co")])
+    keep, send = project(place, own, theirs, rest, q_weight[0], kv_weight[0])
+    send, caches = lax.optimization_barrier((send, caches))
+    both = (keep.astype(F32) + lax.ppermute(send, "co", swap).astype(F32)).astype(BF)
+    both, local_squares = lax.optimization_barrier((both, local_squares))
+    both = lax.all_to_all(both, COL, 0, 0)
     squares = lax.psum(local_squares, ROW)
-    theirs, rest, squares = lax.optimization_barrier((theirs, rest, squares))
-
-    place = lax.axis_index("xl")[None]
-    partial = project(place, own, theirs, rest, q_weight[0], kv_weight[0])
-    partial = lax.all_to_all(partial, "co", 0, 0)
-    both = (partial[0].astype(F32) + partial[1].astype(F32)).astype(BF)
-    both, caches = lax.optimization_barrier((both, caches))
-    both = lax.all_to_all(both, COL, 0, 0)
+    both, squares = lax.optimization_barrier((both, squares))
     parts = lax.all_to_all(arrange(both), ROW, 0, 0)
     parts = parts.reshape((2, 2) + parts.shape[1:])
 

time: 130 us -> 125 us (0.962)
  blocking collectives: 43.3 us -> 6.95 us
  waiting for transfers between devices: 24.9 us -> 45.5 us
  starting transfers between devices: 41.6 us -> 49 us
  other arithmetic: 1.3 us -> 3.64 us
    all_to_all x2 -> x0, blocking collectives: 24.2 us -> none  [the longest x1 16.8 us: shards(): both = lax.all_to_all(both, COL, 0, 0)]
    all_to_all x2, waiting for transfers between devices: 0.01 us -> 14.4 us  [spread(): lax.all_to_all(jnp.broadcast_to(block[None], (8,) + block.shape), 'y', 0, 0)]
    psum x1, blocking collectives: 19.1 us -> 6.95 us  [shards(): squares = lax.psum(local_squares, ROW)]
    ppermute x0 -> x1, starting transfers between devices: none -> 4.13 us  [shards(): lax.ppermute(send, 'co', swap).astype(F32)]
    all_to_all x0 -> x1, starting transfers between devices: none -> 3.54 us  [shards(): both = lax.all_to_all(both, COL, 0, 0)]
    all_to_all x0 -> x1, waiting for transfers between devices: none -> 3.28 us  [shards(): both = lax.all_to_all(both, COL, 0, 0)]
    convert_element_type x1, other arithmetic: 0.08 us -> 1.79 us  [shards(): (keep.astype(F32) + lax.ppermute(send, 'co', swap).astype(F32)).astype(BF)]
    ppermute x0 -> x1, waiting for transfers between devices: none -> 1.44 us  [shards(): lax.ppermute(send, 'co', swap).astype(F32)]
  transfers between devices with their start and end apart: 9 -> 11, of which waited for: 3 -> 7; matrix products, arithmetic and copies ran while one was open for 0% -> 1% of each run, Pallas kernels for 8% -> 9%
where the time goes in v6:
time: 125 us; the launch traced here: 124 us
  starting transfers between devices  49 us (39%)
  waiting for transfers between devices  45.5 us (36%)
  Pallas kernels  14.1 us (11%)
  blocking collectives  6.95 us (6%)
  other arithmetic  3.64 us (3%)
  local copies, waits for them, and re-layouts  3.53 us (3%)
    all_to_all x2, waiting for transfers between devices, spread(): lax.all_to_all(jnp.broadcast_to(block[None], (8,) + block.shape), 'y', 0, 0)  14.4 us
    all_to_all x2, starting transfers between devices, spread(): lax.all_to_all(jnp.broadcast_to(block[None], (8,) + block.shape), 'y', 0, 0)  14 us
    ppermute x3, starting transfers between devices, exchanged(): return lax.ppermute(piece, ROW, [(i, i ^ k) for i in range(row_count)])  12.8 us
    ppermute x1, waiting for transfers between devices, shards(): lax.ppermute(attended[None], 'z', [((i - 1) % count, i) for i in range(co...  9.65 us
    all_to_all x1, waiting for transfers between devices, shards(): parts = lax.all_to_all(arrange(both), ROW, 0, 0)  9.39 us
    psum x1, blocking collectives, shards(): squares = lax.psum(local_squares, ROW)  6.95 us
    pallas_call x1, Pallas kernels, project(): pl.pallas_call(project_kernel, out_shape=[jax.ShapeDtypeStruct((16, 16, 6...  6.22 us
    ppermute x1, waiting for transfers between devices, shards(): rest = jnp.concatenate([rest, lax.ppermute(rest, 'xl', swap)], axis=1)  5.97 us
  transfers between devices with their start and end apart: 11, of which 7 were waited for; matrix products, arithmetic and copies ran while one was open for 1% of the time, Pallas kernels for 9%

profile of v6, /device:TPU:1, one launch (start us, length us, event | category | flops | bytes accessed | tf_op | source)
XLA Modules:
  0.0 123.5 jit_solution(18264695122626000334)
XLA Ops:
  0.6 0.0 copy-start
  0.6 1.2 fusion.1
  1.9 0.9 broadcast_in_dim.13
  2.7 7.7 %all-to-all-start = ((bf16[8,32,1024]{2,1,0:T(8,128)(2,1)}), bf16[8,32,1024]{2,1,0:T(8,128)(2,1)}, u32[]{:S(2)}, u32[]{:S(2)}) async-start(bf16[8,32,1024]{2,1,0:T(8,128)(2,1)} %broadcast_in_dim.13), calls=%async_computation | async-start | bytes 1048576 | tf_op jit(solution)/shard_map/all_to_all | solution.py:206
  10.4 0.0 copy-done
  10.4 1.2 %pick.3 = bf16[2,2,2,256,128]{4,3,2,1,0:T(8,128)(2,1)S(1)} custom-call(s32[1]{0:T(128)} %bitcast.place_ref, bf16[2,256,2,1024]{3,2,1,0:T(2,128)(2,1)S(1)} %bitcast.16), custom_call_target="tpu_custom_call" | custom-call | tf_op jit(solution)/shard_map/pick/pallas_call | solution.py:95
  11.6 4.7 %collective-permute-start.1 = (bf16[2,2,2,256,128]{4,3,2,1,0:T(8,128)(2,1)S(1)}, bf16[2,2,2,256,128]{4,3,2,1,0:T(8,128)(2,1)S(1)}, u32[]{:S(2)}, u32[]{:S(2)}) collective-permute-start(bf16[2,2,2,256,128]{4,3,2,1,0:T(8,128)(2,1)S(1)} %pick.3), channel_id=1, source_target_pairs={{0,32},{16,48},{32,0},{48,16},{1,33},{17,49},{33,1},{49,17},{2,34}... | collective-permute-start | bytes 1572872 | tf_op jit(solution)/shard_map/ppermute | solution.py:209
  16.3 2.2 %collective-permute-start = (bf16[32,1024]{1,0:T(8,128)(2,1)S(1)}, bf16[32,1024]{1,0:T(8,128)(2,1)S(1)}, u32[]{:S(2)}, u32[]{:S(2)}) collective-permute-start(bf16[32,1024]{1,0:T(8,128)(2,1)S(1)} %get-tuple-element.49), channel_id=1, source_target_pairs={{0,8},{8,0},{1,9},{9,1},{2,10},{10,2},{3,11},{11,3},{4,12},{12,4},... | collective-permute-start | bytes 196616 | tf_op jit(solution)/shard_map/ppermute | solution.py:214
  18.5 3.7 %pick.2 = (bf16[2,2,2,256,128]{4,3,2,1,0:T(8,128)(2,1)S(1)}, bf16[2,2,2,256,128]{4,3,2,1,0:T(8,128)(2,1)}, bf16[2,2,2,256,128]{4,3,2,1,0:T(8,128)(2,1)S(1)}) custom-call(s32[1]{0:T(128)} %bitcast.place_ref, bf16[2,256,2,1024]{3,2,1,0:T(2,128)(2,1)S(1)} %bitcast.17), custom_call_target="tpu_custom_call" | custom-call | tf_op jit(solution)/shard_map/pick/pallas_call | solution.py:95
  22.2 0.0 copy-start.2
  22.2 0.8 copy-done.2
  23.0 6.0 %collective-permute-done = bf16[32,1024]{1,0:T(8,128)(2,1)S(1)} collective-permute-done((bf16[32,1024]{1,0:T(8,128)(2,1)S(1)}, bf16[32,1024]{1,0:T(8,128)(2,1)S(1)}, u32[]{:S(2)}, u32[]{:S(2)}) %collective-permute-start) | collective-permute-done | bytes 65568 | tf_op jit(solution)/shard_map/ppermute | solution.py:214
  29.0 0.0 copy-start.3
  29.0 0.0 collective-permute-done.1.refs_2_
  29.0 0.0 all-to-all-done.own_ref
  29.0 1.1 broadcast_in_dim.28
  30.1 6.3 %all-to-all-start.1 = ((bf16[8,32,2048]{2,1,0:T(8,128)(2,1)}), bf16[8,32,2048]{2,1,0:T(8,128)(2,1)}, u32[]{:S(2)}, u32[]{:S(2)}) async-start(bf16[8,32,2048]{2,1,0:T(8,128)(2,1)} %broadcast_in_dim.28), calls=%async_computation.1 | async-start | bytes 2097152 | tf_op jit(solution)/shard_map/all_to_all | solution.py:206
  36.5 3.0 %collective-permute-start.2 = (bf16[8,32,1024]{2,1,0:T(8,128)(2,1)}, bf16[8,32,1024]{2,1,0:T(8,128)(2,1)S(1)}, u32[]{:S(2)}, u32[]{:S(2)}) collective-permute-start(bf16[8,32,1024]{2,1,0:T(8,128)(2,1)} %all-to-all-done.own_ref), channel_id=1, source_target_pairs={{0,8},{8,0},{1,9},{9,1},{2,10},{10,2},{3,11},{11,3},{4,12},{12,4},... | collective-permute-start | bytes 1572872 | tf_op jit(solution)/shard_map/ppermute | solution.py:217
  39.5 4.6 %collective-permute-start.3 = (bf16[2,2,2,256,128]{4,3,2,1,0:T(8,128)(2,1)}, bf16[2,2,2,256,128]{4,3,2,1,0:T(8,128)(2,1)S(1)}, u32[]{:S(2)}, u32[]{:S(2)}) collective-permute-start(bf16[2,2,2,256,128]{4,3,2,1,0:T(8,128)(2,1)} %get-tuple-element.32), channel_id=1, source_target_pairs={{0,16},{16,0},{32,48},{48,32},{1,17},{17,1},{33,49},{49,33},{2,18}... | collective-permute-start | bytes 1572872 | tf_op jit(solution)/shard_map/ppermute | solution.py:209
  44.2 0.0 copy-done.3
  44.2 3.5 %collective-permute-start.4 = (bf16[2,2,2,256,128]{4,3,2,1,0:T(8,128)(2,1)S(1)}, bf16[2,2,2,256,128]{4,3,2,1,0:T(8,128)(2,1)S(1)}, u32[]{:S(2)}, u32[]{:S(2)}) collective-permute-start(bf16[2,2,2,256,128]{4,3,2,1,0:T(8,128)(2,1)S(1)} %copy-done.3), channel_id=1, source_target_pairs={{0,48},{16,32},{32,16},{48,0},{1,49},{17,33},{33,17},{49,1},{2,50}... | collective-permute-start | bytes 1572872 | tf_op jit(solution)/shard_map/ppermute | solution.py:209
  47.7 0.6 pad_add_fusion.place_ref
  48.3 1.3 %collective-permute-done.2.theirs_ref = bf16[8,32,1024]{2,1,0:T(8,128)(2,1)S(1)} collective-permute-done((bf16[8,32,1024]{2,1,0:T(8,128)(2,1)}, bf16[8,32,1024]{2,1,0:T(8,128)(2,1)S(1)}, u32[]{:S(2)}, u32[]{:S(2)}) %collective-permute-start.2) | collective-permute-done | bytes 524320 | tf_op jit(solution)/shard_map/ppermute | solution.py:217
  49.6 0.0 copy-start.4
  49.6 14.4 %all-to-all-done.1.rest_ref = bf16[8,32,2048]{2,1,0:T(8,128)(2,1)} async-done(((bf16[8,32,2048]{2,1,0:T(8,128)(2,1)}), bf16[8,32,2048]{2,1,0:T(8,128)(2,1)}, u32[]{:S(2)}, u32[]{:S(2)}) %all-to-all-start.1) | async-done | bytes 1048608 | tf_op jit(solution)/shard_map/all_to_all | solution.py:206
  64.0 0.0 copy-done.4
  64.0 6.2 %project.1 = (bf16[16,16,640]{2,1,0:T(8,128)(2,1)}, bf16[16,16,640]{2,1,0:T(8,128)(2,1)}) custom-call(s32[2]{0:T(128)} %pad_add_fusion.place_ref, bf16[8,32,1024]{2,1,0:T(8,128)(2,1)} %all-to-all-done.own_ref, bf16[8,32,1024]{2,1,0:T(8,128)(2,1)} %copy-done.4, bf16[8,32,2048]{2,1,0:T(8,128)(2,1)} %all-to-all-done.1.rest_ref, bf16[2048,512]{1,0:T(8,128)(2,1)} %bitcast.20, ...), custom_call_target="tpu_custom_call" | custom-call | tf_op jit(solution)/shard_map/project/pallas_call | solution.py:72
  70.3 0.0 copy-start.1
  70.3 0.0 collective-permute-done.3.refs_1_
  70.3 0.0 collective-permute-done.4.refs_3_
  70.3 4.1 %collective-permute-start.5 = (bf16[16,16,640]{2,1,0:T(8,128)(2,1)}, bf16[16,16,640]{2,1,0:T(8,128)(2,1)S(1)}, u32[]{:S(2)}, u32[]{:S(2)}) collective-permute-start(bf16[16,16,640]{2,1,0:T(8,128)(2,1)} %get-tuple-element.35), channel_id=1, source_target_pairs={{0,16},{16,0},{1,17},{17,1},{2,18},{18,2},{3,19},{19,3},{4,20},{20... | collective-permute-start | bytes 983048 | tf_op jit(solution)/shard_map/ppermute | solution.py:224
  74.4 1.4 %collective-permute-done.5 = bf16[16,16,640]{2,1,0:T(8,128)(2,1)S(1)} collective-permute-done((bf16[16,16,640]{2,1,0:T(8,128)(2,1)}, bf16[16,16,640]{2,1,0:T(8,128)(2,1)S(1)}, u32[]{:S(2)}, u32[]{:S(2)}) %collective-permute-start.5) | collective-permute-done | bytes 327712 | tf_op jit(solution)/shard_map/ppermute | solution.py:224
  75.9 1.8 %add_convert_fusion = bf16[16,16,640]{2,1,0:T(8,128)(2,1)} fusion(bf16[16,16,640]{2,1,0:T(8,128)(2,1)S(1)} %collective-permute-done.5, bf16[16,16,640]{2,1,0:T(8,128)(2,1)} %get-tuple-element.29), kind=kLoop, calls=%fused_computation | loop fusion | flops 655360 | bytes 983040 | tf_op jit(solution)/shard_map/convert_element_type | solution.py:224
  77.7 3.5 %all-to-all-start.2 = ((bf16[16,16,640]{2,1,0:T(8,128)(2,1)}), bf16[16,16,640]{2,1,0:T(8,128)(2,1)S(1)}, u32[]{:S(2)}, u32[]{:S(2)}) async-start(bf16[16,16,640]{2,1,0:T(8,128)(2,1)} %add_convert_fusion), calls=%async_computation.2 | async-start | bytes 655360 | tf_op jit(solution)/shard_map/all_to_all | solution.py:226
  81.2 7.0 %psum.7 = f32[32]{0:T(128)S(1)} all-reduce(f32[32]{0:T(128)S(1)} %get-tuple-element.37), channel_id=1, replica_groups=mesh['z'=8,'xh'=2,'co'=2,'xl'=2,'y'=8] {'xh','co'}, use_global_device_ids=true, to_apply=%region_1.0 | all-reduce | flops 32 | bytes 256 | tf_op jit(solution)/shard_map/psum | solution.py:227
  88.2 3.3 %all-to-all-done.2.both_ref = bf16[16,16,640]{2,1,0:T(8,128)(2,1)S(1)} async-done(((bf16[16,16,640]{2,1,0:T(8,128)(2,1)}), bf16[16,16,640]{2,1,0:T(8,128)(2,1)S(1)}, u32[]{:S(2)}, u32[]{:S(2)}) %all-to-all-start.2) | async-done | bytes 327712 | tf_op jit(solution)/shard_map/all_to_all | solution.py:226
  91.4 0.8 arrange.1
  92.3 5.3 %all-to-all-start.3 = ((bf16[4,4,16,1024]{3,2,1,0:T(8,128)(2,1)}), bf16[4,4,16,1024]{3,2,1,0:T(8,128)(2,1)S(1)}, u32[]{:S(2)}, u32[]{:S(2)}) async-start(bf16[4,4,16,1024]{3,2,1,0:T(8,128)(2,1)} %arrange.1), calls=%async_computation.3 | async-start | bytes 1048576 | tf_op jit(solution)/shard_map/all_to_all | solution.py:229
  97.6 0.1 copy.8.scale_ref
  97.7 9.4 %all-to-all-done.3 = bf16[4,4,16,1024]{3,2,1,0:T(8,128)(2,1)S(1)} async-done(((bf16[4,4,16,1024]{3,2,1,0:T(8,128)(2,1)}), bf16[4,4,16,1024]{3,2,1,0:T(8,128)(2,1)S(1)}, u32[]{:S(2)}, u32[]{:S(2)}) %all-to-all-start.3) | async-done | bytes 524320 | tf_op jit(solution)/shard_map/all_to_all | solution.py:229
  107.1 0.0 copy-done.1
  107.1 2.1 %attend.1 = (bf16[32,2048]{1,0:T(8,128)(2,1)S(1)}, bf16[32,2048]{1,0:T(8,128)(2,1)}) custom-call(s32[1,2]{1,0:T(1,128)S(1)} %copy-done.1, s32[1]{0:T(128)} %bitcast.place_ref, bf16[2,2,4,16,1024]{4,3,2,1,0:T(8,128)(2,1)S(1)} %bitcast.18, f32[32,1]{1,0:T(8,128)S(1)} %copy.8.scale_ref, bf16[2,2,2,256,128]{4,3,2,1,0:T(8,128)(2,1)S(1)} %get-tuple-element.40.refs_0_, ...), custom_call_target="tpu_custom_call" | custom-call | tf_op jit(solution)/shard_map/attend/pallas_call | solution.py:186
  109.2 4.0 %collective-permute-start.6 = (bf16[1,32,2048]{2,1,0:T(8,128)(2,1)S(1)}, bf16[1,32,2048]{2,1,0:T(8,128)(2,1)S(1)}, u32[]{:S(2)}, u32[]{:S(2)}) collective-permute-start(bf16[1,32,2048]{2,1,0:T(8,128)(2,1)S(1)} %bitcast.19), channel_id=1, source_target_pairs={{448,0},{0,64},{64,128},{128,192},{192,256},{256,320},{320,384},{3... | collective-permute-start | bytes 393224 | tf_op jit(solution)/shard_map/ppermute | solution.py:235
  113.2 9.7 %collective-permute-done.6 = bf16[1,32,2048]{2,1,0:T(8,128)(2,1)S(1)} collective-permute-done((bf16[1,32,2048]{2,1,0:T(8,128)(2,1)S(1)}, bf16[1,32,2048]{2,1,0:T(8,128)(2,1)S(1)}, u32[]{:S(2)}, u32[]{:S(2)}) %collective-permute-start.6) | collective-permute-done | bytes 131104 | tf_op jit(solution)/shard_map/ppermute | solution.py:235
  122.9 0.7 copy.10
  (3 shorter events, 0.0 us)
Async XLA Ops:
  0.6 9.7 %copy-start = (bf16[1,2,256,2,1024]{4,3,2,1,0:T(2,128)(2,1)S(1)}, bf16[1,2,256,2,1024]{4,3,2,1,0:T(2,128)(2,1)}, u32[]{:S(2)}) copy-start(bf16[1,2,256,2,1024]{4,3,2,1,0:T(2,128)(2,1)} %param.10) | copy-start | bytes 6291460
  2.7 26.3 %all-to-all-start = ((bf16[8,32,1024]{2,1,0:T(8,128)(2,1)}), bf16[8,32,1024]{2,1,0:T(8,128)(2,1)}, u32[]{:S(2)}, u32[]{:S(2)}) async-start(bf16[8,32,1024]{2,1,0:T(8,128)(2,1)} %broadcast_in_dim.13), calls=%async_computation | async-start | bytes 1048576 | tf_op jit(solution)/shard_map/all_to_all | solution.py:206
  11.6 17.4 %collective-permute-start.1 = (bf16[2,2,2,256,128]{4,3,2,1,0:T(8,128)(2,1)S(1)}, bf16[2,2,2,256,128]{4,3,2,1,0:T(8,128)(2,1)S(1)}, u32[]{:S(2)}, u32[]{:S(2)}) collective-permute-start(bf16[2,2,2,256,128]{4,3,2,1,0:T(8,128)(2,1)S(1)} %pick.3), channel_id=1, source_target_pairs={{0,32},{16,48},{32,0},{48,16},{1,33},{17,49},{33,1},{49,17},{2,34}... | collective-permute-start | bytes 1572872 | tf_op jit(solution)/shard_map/ppermute | solution.py:209
  16.3 12.7 %collective-permute-start = (bf16[32,1024]{1,0:T(8,128)(2,1)S(1)}, bf16[32,1024]{1,0:T(8,128)(2,1)S(1)}, u32[]{:S(2)}, u32[]{:S(2)}) collective-permute-start(bf16[32,1024]{1,0:T(8,128)(2,1)S(1)} %get-tuple-element.49), channel_id=1, source_target_pairs={{0,8},{8,0},{1,9},{9,1},{2,10},{10,2},{3,11},{11,3},{4,12},{12,4},... | collective-permute-start | bytes 196616 | tf_op jit(solution)/shard_map/ppermute | solution.py:214
  22.2 0.8 copy-start.2
  29.0 15.2 %copy-start.3 = (bf16[2,2,2,256,128]{4,3,2,1,0:T(8,128)(2,1)S(1)}, bf16[2,2,2,256,128]{4,3,2,1,0:T(8,128)(2,1)}, u32[]{:S(2)}) copy-start(bf16[2,2,2,256,128]{4,3,2,1,0:T(8,128)(2,1)} %copy-done.2) | copy-start | bytes 1572868
  30.1 33.9 %all-to-all-start.1 = ((bf16[8,32,2048]{2,1,0:T(8,128)(2,1)}), bf16[8,32,2048]{2,1,0:T(8,128)(2,1)}, u32[]{:S(2)}, u32[]{:S(2)}) async-start(bf16[8,32,2048]{2,1,0:T(8,128)(2,1)} %broadcast_in_dim.28), calls=%async_computation.1 | async-start | bytes 2097152 | tf_op jit(solution)/shard_map/all_to_all | solution.py:206
  36.5 13.2 %collective-permute-start.2 = (bf16[8,32,1024]{2,1,0:T(8,128)(2,1)}, bf16[8,32,1024]{2,1,0:T(8,128)(2,1)S(1)}, u32[]{:S(2)}, u32[]{:S(2)}) collective-permute-start(bf16[8,32,1024]{2,1,0:T(8,128)(2,1)} %all-to-all-done.own_ref), channel_id=1, source_target_pairs={{0,8},{8,0},{1,9},{9,1},{2,10},{10,2},{3,11},{11,3},{4,12},{12,4},... | collective-permute-start | bytes 1572872 | tf_op jit(solution)/shard_map/ppermute | solution.py:217
  39.5 30.8 %collective-permute-start.3 = (bf16[2,2,2,256,128]{4,3,2,1,0:T(8,128)(2,1)}, bf16[2,2,2,256,128]{4,3,2,1,0:T(8,128)(2,1)S(1)}, u32[]{:S(2)}, u32[]{:S(2)}) collective-permute-start(bf16[2,2,2,256,128]{4,3,2,1,0:T(8,128)(2,1)} %get-tuple-element.32), channel_id=1, source_target_pairs={{0,16},{16,0},{32,48},{48,32},{1,17},{17,1},{33,49},{49,33},{2,18}... | collective-permute-start | bytes 1572872 | tf_op jit(solution)/shard_map/ppermute | solution.py:209
  44.2 26.1 %collective-permute-start.4 = (bf16[2,2,2,256,128]{4,3,2,1,0:T(8,128)(2,1)S(1)}, bf16[2,2,2,256,128]{4,3,2,1,0:T(8,128)(2,1)S(1)}, u32[]{:S(2)}, u32[]{:S(2)}) collective-permute-start(bf16[2,2,2,256,128]{4,3,2,1,0:T(8,128)(2,1)S(1)} %copy-done.3), channel_id=1, source_target_pairs={{0,48},{16,32},{32,16},{48,0},{1,49},{17,33},{33,17},{49,1},{2,50}... | collective-permute-start | bytes 1572872 | tf_op jit(solution)/shard_map/ppermute | solution.py:209
  49.6 14.4 %copy-start.4 = (bf16[8,32,1024]{2,1,0:T(8,128)(2,1)}, bf16[8,32,1024]{2,1,0:T(8,128)(2,1)S(1)}, u32[]{:S(2)}) copy-start(bf16[8,32,1024]{2,1,0:T(8,128)(2,1)S(1)} %collective-permute-done.2.theirs_ref) | copy-start | bytes 1572868
  70.3 36.8 %copy-start.1 = (s32[1,2]{1,0:T(1,128)S(1)}, s32[1,2]{1,0:T(1,128)}, u32[]{:S(2)}) copy-start(s32[1,2]{1,0:T(1,128)} %lengths_ref.1) | copy-start | bytes 28
  70.3 5.6 %collective-permute-start.5 = (bf16[16,16,640]{2,1,0:T(8,128)(2,1)}, bf16[16,16,640]{2,1,0:T(8,128)(2,1)S(1)}, u32[]{:S(2)}, u32[]{:S(2)}) collective-permute-start(bf16[16,16,640]{2,1,0:T(8,128)(2,1)} %get-tuple-element.35), channel_id=1, source_target_pairs={{0,16},{16,0},{1,17},{17,1},{2,18},{18,2},{3,19},{19,3},{4,20},{20... | collective-permute-start | bytes 983048 | tf_op jit(solution)/shard_map/ppermute | solution.py:224
  77.7 13.8 %all-to-all-start.2 = ((bf16[16,16,640]{2,1,0:T(8,128)(2,1)}), bf16[16,16,640]{2,1,0:T(8,128)(2,1)S(1)}, u32[]{:S(2)}, u32[]{:S(2)}) async-start(bf16[16,16,640]{2,1,0:T(8,128)(2,1)} %add_convert_fusion), calls=%async_computation.2 | async-start | bytes 655360 | tf_op jit(solution)/shard_map/all_to_all | solution.py:226
  92.3 14.8 %all-to-all-start.3 = ((bf16[4,4,16,1024]{3,2,1,0:T(8,128)(2,1)}), bf16[4,4,16,1024]{3,2,1,0:T(8,128)(2,1)S(1)}, u32[]{:S(2)}, u32[]{:S(2)}) async-start(bf16[4,4,16,1024]{3,2,1,0:T(8,128)(2,1)} %arrange.1), calls=%async_computation.3 | async-start | bytes 1048576 | tf_op jit(solution)/shard_map/all_to_all | solution.py:229
  109.2 13.7 %collective-permute-start.6 = (bf16[1,32,2048]{2,1,0:T(8,128)(2,1)S(1)}, bf16[1,32,2048]{2,1,0:T(8,128)(2,1)S(1)}, u32[]{:S(2)}, u32[]{:S(2)}) collective-permute-start(bf16[1,32,2048]{2,1,0:T(8,128)(2,1)S(1)} %bitcast.19), channel_id=1, source_target_pairs={{448,0},{0,64},{64,128},{128,192},{192,256},{256,320},{320,384},{3... | collective-permute-start | bytes 393224 | tf_op jit(solution)/shard_map/ppermute | solution.py:235

commit v7 on v6

--- a/solution.py
+++ b/solution.py
@@ -13,7 +13,6 @@
 COL = ("xl", "y")
 BF = jnp.bfloat16
 F32 = jnp.float32
-FIRST = 1024
 VMEM = pl.BlockSpec(memory_space=pltpu.VMEM)
 HBM = pl.BlockSpec(memory_space=pltpu.HBM)
 SMEM = pl.BlockSpec(memory_space=pltpu.SMEM)
@@ -21,60 +20,41 @@
 FULL = pltpu.CompilerParams(vmem_limit_bytes=56 * 1024 * 1024)
 
 
-def project_kernel(place_ref, own_ref, theirs_ref, rest_ref, query_ref, pair_ref, keep_ref, send_ref, *scratch):
-    own, theirs, rest, query, pair, sems = scratch
-    count, rows, first = own_ref.shape
-    remainder = rest_ref.shape[2] // 2
+def project_kernel(place_ref, gathered_ref, query_ref, pair_ref, keep_ref, send_ref, *scratch):
+    gathered, query, pair, sems = scratch
+    count, rows, width = gathered_ref.shape
     half = rows // 2
-    mine = place_ref[0] * count
-    other = (1 - place_ref[0]) * count
-    former_lines, latter_lines = pl.ds(0, first), pl.ds(first, remainder)
-    moves = (
-        (own_ref, own),
-        (query_ref.at[former_lines], query.at[former_lines]),
-        (pair_ref.at[former_lines], pair.at[former_lines]),
-        (theirs_ref, theirs),
-        (rest_ref, rest),
-        (query_ref.at[latter_lines], query.at[latter_lines]),
-        (pair_ref.at[latter_lines], pair.at[latter_lines]),
-    )
+    step = count // 4
+    moves = [(query_ref, query), (pair_ref, pair)]
+    for n in range(4):
+        part = pl.ds(n * step, step)
+        moves.append((gathered_ref.at[part], gathered.at[part]))
     copies = [pltpu.make_async_copy(a, b, sems.at[n]) for n, (a, b) in enumerate(moves)]
     for copy in copies:
         copy.start()
-
-    def times(block, lines):
-        block = block.reshape(count * rows, block.shape[2])
-        return [
-            jnp.dot(block, weight[lines], preferred_element_type=F32) for weight in (query, pair)
-        ]
-
-    for copy in copies[:3]:
-        copy.wait()
-    former = [times(own[...], slice(0, first))]
-    copies[3].wait()
-    former.append(times(theirs[...], slice(0, first)))
-    for copy in copies[4:]:
-        copy.wait()
-    for n, start in enumerate((mine, other)):
-        block = rest[:, :, n * remainder : (n + 1) * remainder]
-        latter = times(block, slice(first, first + remainder))
-        for part, more, lanes in zip(former[n], latter, (slice(0, 512), slice(512, 640))):
-            part = (part + more).astype(BF).reshape(count, 2, half, part.shape[1])
+    copies[0].wait()
+    copies[1].wait()
+    for n in range(4):
+        copies[2 + n].wait()
+        block = gathered[n * step : (n + 1) * step].reshape(step * rows, width)
+        for weight, lanes in ((query, slice(0, 512)), (pair, slice(512, 640))):
+            part = jnp.dot(block, weight[...], preferred_element_type=F32)
+            part = part.astype(BF).reshape(step, 2, half, part.shape[1])
             for core in range(2):
 
-                @pl.when(place_ref[1] == core)
+                @pl.when(place_ref[0] == core)
                 def _():
-                    keep_ref[pl.ds(start, count), :, lanes] = part[:, core]
-                    send_ref[pl.ds(start, count), :, lanes] = part[:, 1 - core]
+                    keep_ref[n * step : (n + 1) * step, :, lanes] = part[:, core]
+                    send_ref[n * step : (n + 1) * step, :, lanes] = part[:, 1 - core]
 
 
 def project(place, *operands):
     return pl.pallas_call(
         project_kernel,
         out_shape=[jax.ShapeDtypeStruct((16, 16, 640), BF)] * 2,
-        in_specs=[SMEM] + [HBM] * 5,
+        in_specs=[SMEM] + [HBM] * 3,
         out_specs=[VMEM] * 2,
-        scratch_shapes=[pltpu.VMEM(x.shape, BF) for x in operands] + [pltpu.SemaphoreType.DMA((7,))],
+        scratch_shapes=[pltpu.VMEM(x.shape, BF) for x in operands] + [pltpu.SemaphoreType.DMA((6,))],
         compiler_params=FULL,
         name="project",
     )(place, *operands)
@@ -202,24 +182,12 @@
     local_squares = jnp.sum(widened * widened, axis=1)
     swap = [(0, 1), (1, 0)]
 
-    def spread(block):
-        return lax.all_to_all(jnp.broadcast_to(block[None], (8,) + block.shape), "y", 0, 0)
-
-    def exchanged(piece, k):
-        return lax.ppermute(piece, ROW, [(i, i ^ k) for i in range(row_count)])
-
-    own = spread(sent[:, :FIRST])
-    across = exchanged(pick((2,), row_index[None], kv_cache[0])[0], 2)
-    rest = sent[:, FIRST:]
-    rest = jnp.concatenate([rest, lax.ppermute(rest, "xl", swap)], axis=1)
-    pieces = pick((0, 1, 3), row_index[None], kv_cache[0])
-    rest, own, pieces, across = lax.optimization_barrier((rest, own, pieces, across))
-    theirs = lax.ppermute(own, "xl", swap)
-    rest = spread(rest)
-    caches = [pieces[0], exchanged(pieces[1], 1), across, exchanged(pieces[2], 3)]
-
-    place = jnp.stack([lax.axis_index("xl"), lax.axis_index("co")])
-    keep, send = project(place, own, theirs, rest, q_weight[0], kv_weight[0])
+    count = 16
+    gathered = lax.all_to_all(jnp.broadcast_to(sent[None], (count, rows, width)), COL, 0, 0)
+    caches = list(pick((0, 1, 2, 3), row_index[None], kv_cache[0]))
+    for k in range(1, row_count):
+        caches[k] = lax.ppermute(caches[k], ROW, [(i, i ^ k) for i in range(row_count)])
+    keep, send = project(lax.axis_index("co")[None], gathered, q_weight[0], kv_weight[0])
     send, caches = lax.optimization_barrier((send, caches))
     both = (keep.astype(F32) + lax.ppermute(send, "co", swap).astype(F32)).astype(BF)
     both, local_squares = lax.optimization_barrier((both, local_squares))

time: 125 us -> 122 us (0.976)
  waiting for transfers between devices: 45.5 us -> 54.4 us
  starting transfers between devices: 49 us -> 40.3 us
    all_to_all x2 -> x1, waiting for transfers between devices: 14.4 us -> 30.9 us  [shards(): lax.all_to_all(jnp.broadcast_to(sent[None], (count, rows, width)), COL, 0...]
    ppermute x5 -> x3, waiting for transfers between devices: 7.3 us -> 0.01 us  [shards(): lax.ppermute(caches[k], ROW, [(i, i ^ k) for i in range(row_count)])]
    ppermute x5 -> x3, starting transfers between devices: 18 us -> 11.4 us  [shards(): lax.ppermute(caches[k], ROW, [(i, i ^ k) for i in range(row_count)])]
    all_to_all x2 -> x1, starting transfers between devices: 14 us -> 8.86 us  [shards(): lax.all_to_all(jnp.broadcast_to(sent[None], (count, rows, width)), COL, 0...]
    pallas_call x2 -> x1, Pallas kernels: 4.96 us -> 5.06 us  [pick(): pl.pallas_call(pick_kernel, grid=(prompts,), out_shape=[jax.ShapeDtypeStr...]
  transfers between devices with their start and end apart: 11 -> 8, of which waited for: 7 -> 5; matrix products, arithmetic and copies ran while one was open for 1% -> 0% of each run, Pallas kernels for 9% -> 9%
where the time goes in v7:
time: 122 us; the launch traced here: 121 us
  waiting for transfers between devices  54.4 us (45%)
  starting transfers between devices  40.3 us (33%)
  Pallas kernels  13.8 us (11%)
  blocking collectives  7.18 us (6%)
  other arithmetic  2.84 us (2%)
  local copies, waits for them, and re-layouts  2.34 us (2%)
    all_to_all x1, waiting for transfers between devices, shards(): lax.all_to_all(jnp.broadcast_to(sent[None], (count, rows, width)), COL, 0...  30.9 us
    ppermute x3, starting transfers between devices, shards(): lax.ppermute(caches[k], ROW, [(i, i ^ k) for i in range(row_count)])  11.4 us
    ppermute x1, waiting for transfers between devices, shards(): lax.ppermute(attended[None], 'z', [((i - 1) % count, i) for i in range(co...  9.64 us
    all_to_all x1, waiting for transfers between devices, shards(): parts = lax.all_to_all(arrange(both), ROW, 0, 0)  9.39 us
    all_to_all x1, starting transfers between devices, shards(): lax.all_to_all(jnp.broadcast_to(sent[None], (count, rows, width)), COL, 0...  8.86 us
    psum x1, blocking collectives, shards(): squares = lax.psum(local_squares, ROW)  7.18 us
    all_to_all x1, starting transfers between devices, shards(): parts = lax.all_to_all(arrange(both), ROW, 0, 0)  6.36 us
    pallas_call x1, Pallas kernels, project(): pl.pallas_call(project_kernel, out_shape=[jax.ShapeDtypeStruct((16, 16, 6...  5.73 us
  transfers between devices with their start and end apart: 8, of which 5 were waited for; matrix products, arithmetic and copies ran while one was open for 0% of the time, Pallas kernels for 9%

profile of v7, /device:TPU:1, one launch (start us, length us, event | category | flops | bytes accessed | tf_op | source)
XLA Modules:
  0.0 121.5 jit_solution(3075659144271574177)
XLA Ops:
  0.6 1.1 fusion.1
  1.7 1.6 %broadcast_in_dim.27 = bf16[16,32,2048]{2,1,0:T(8,128)(2,1)} broadcast(bf16[32,2048]{1,0:T(8,128)(2,1)S(1)} %get-tuple-element.37), dimensions={1,2} | broadcast | bytes 2228224 | tf_op jit(solution)/shard_map/broadcast_in_dim | solution.py:186
  3.3 0.0 copy-start
  3.3 8.9 %all-to-all-start = ((bf16[16,32,2048]{2,1,0:T(8,128)(2,1)}), bf16[16,32,2048]{2,1,0:T(8,128)(2,1)}, u32[]{:S(2)}, u32[]{:S(2)}) async-start(bf16[16,32,2048]{2,1,0:T(8,128)(2,1)} %broadcast_in_dim.27), calls=%async_computation | async-start | bytes 4194304 | tf_op jit(solution)/shard_map/all_to_all | solution.py:186
  12.1 0.0 copy-done
  12.2 5.1 %pick.1 = (bf16[2,2,2,256,128]{4,3,2,1,0:T(8,128)(2,1)S(1)}, bf16[2,2,2,256,128]{4,3,2,1,0:T(8,128)(2,1)}, bf16[2,2,2,256,128]{4,3,2,1,0:T(8,128)(2,1)}, bf16[2,2,2,256,128]{4,3,2,1,0:T(8,128)(2,1)S(1)}) custom-call(s32[1]{0:T(128)} %bitcast.place_ref, bf16[2,256,2,1024]{3,2,1,0:T(2,128)(2,1)S(1)} %bitcast.14), custom_call_target="tpu_custom_call" | custom-call | tf_op jit(solution)/shard_map/pick/pallas_call | solution.py:75
  17.2 4.5 %collective-permute-start = (bf16[2,2,2,256,128]{4,3,2,1,0:T(8,128)(2,1)}, bf16[2,2,2,256,128]{4,3,2,1,0:T(8,128)(2,1)S(1)}, u32[]{:S(2)}, u32[]{:S(2)}) collective-permute-start(bf16[2,2,2,256,128]{4,3,2,1,0:T(8,128)(2,1)} %get-tuple-element.22), channel_id=1, source_target_pairs={{0,16},{16,0},{32,48},{48,32},{1,17},{17,1},{33,49},{49,33},{2,18}... | collective-permute-start | bytes 1572872 | tf_op jit(solution)/shard_map/ppermute | solution.py:189
  21.7 2.7 %collective-permute-start.1 = (bf16[2,2,2,256,128]{4,3,2,1,0:T(8,128)(2,1)}, bf16[2,2,2,256,128]{4,3,2,1,0:T(8,128)(2,1)S(1)}, u32[]{:S(2)}, u32[]{:S(2)}) collective-permute-start(bf16[2,2,2,256,128]{4,3,2,1,0:T(8,128)(2,1)} %get-tuple-element.23), channel_id=1, source_target_pairs={{0,32},{16,48},{32,0},{48,16},{1,33},{17,49},{33,1},{49,17},{2,34}... | collective-permute-start | bytes 1572872 | tf_op jit(solution)/shard_map/ppermute | solution.py:189
  24.4 4.2 %collective-permute-start.2 = (bf16[2,2,2,256,128]{4,3,2,1,0:T(8,128)(2,1)S(1)}, bf16[2,2,2,256,128]{4,3,2,1,0:T(8,128)(2,1)S(1)}, u32[]{:S(2)}, u32[]{:S(2)}) collective-permute-start(bf16[2,2,2,256,128]{4,3,2,1,0:T(8,128)(2,1)S(1)} %get-tuple-element.24), channel_id=1, source_target_pairs={{0,48},{16,32},{32,16},{48,0},{1,49},{17,33},{33,17},{49,1},{2,50}... | collective-permute-start | bytes 1572872 | tf_op jit(solution)/shard_map/ppermute | solution.py:189
  28.7 30.9 %all-to-all-done.gathered_ref = bf16[16,32,2048]{2,1,0:T(8,128)(2,1)} async-done(((bf16[16,32,2048]{2,1,0:T(8,128)(2,1)}), bf16[16,32,2048]{2,1,0:T(8,128)(2,1)}, u32[]{:S(2)}, u32[]{:S(2)}) %all-to-all-start) | async-done | bytes 2097184 | tf_op jit(solution)/shard_map/all_to_all | solution.py:186
  59.5 5.7 %project.1 = (bf16[16,16,640]{2,1,0:T(8,128)(2,1)}, bf16[16,16,640]{2,1,0:T(8,128)(2,1)}) custom-call(s32[1]{0:T(128)} %bitcast.1.place_ref, bf16[16,32,2048]{2,1,0:T(8,128)(2,1)} %all-to-all-done.gathered_ref, bf16[2048,512]{1,0:T(8,128)(2,1)} %bitcast.16, bf16[2048,128]{1,0:T(8,128)(2,1)} %bitcast.17), custom_call_target="tpu_custom_call" | custom-call | tf_op jit(solution)/shard_map/project/pallas_call | solution.py:52
  65.3 0.0 copy-start.1
  65.3 0.0 collective-permute-done.refs_1_
  65.3 0.0 collective-permute-done.1.refs_2_
  65.3 0.0 collective-permute-done.2.refs_3_
  65.3 5.0 %collective-permute-start.3 = (bf16[16,16,640]{2,1,0:T(8,128)(2,1)}, bf16[16,16,640]{2,1,0:T(8,128)(2,1)S(1)}, u32[]{:S(2)}, u32[]{:S(2)}) collective-permute-start(bf16[16,16,640]{2,1,0:T(8,128)(2,1)} %get-tuple-element.25), channel_id=1, source_target_pairs={{0,16},{16,0},{1,17},{17,1},{2,18},{18,2},{3,19},{19,3},{4,20},{20... | collective-permute-start | bytes 983048 | tf_op jit(solution)/shard_map/ppermute | solution.py:192
  70.3 1.4 %collective-permute-done.3 = bf16[16,16,640]{2,1,0:T(8,128)(2,1)S(1)} collective-permute-done((bf16[16,16,640]{2,1,0:T(8,128)(2,1)}, bf16[16,16,640]{2,1,0:T(8,128)(2,1)S(1)}, u32[]{:S(2)}, u32[]{:S(2)}) %collective-permute-start.3) | collective-permute-done | bytes 327712 | tf_op jit(solution)/shard_map/ppermute | solution.py:192
  71.7 1.8 %add_convert_fusion = bf16[16,16,640]{2,1,0:T(8,128)(2,1)} fusion(bf16[16,16,640]{2,1,0:T(8,128)(2,1)S(1)} %collective-permute-done.3, bf16[16,16,640]{2,1,0:T(8,128)(2,1)} %get-tuple-element.19), kind=kLoop, calls=%fused_computation | loop fusion | flops 655360 | bytes 983040 | tf_op jit(solution)/shard_map/convert_element_type | solution.py:192
  73.5 4.6 %all-to-all-start.1 = ((bf16[16,16,640]{2,1,0:T(8,128)(2,1)}), bf16[16,16,640]{2,1,0:T(8,128)(2,1)S(1)}, u32[]{:S(2)}, u32[]{:S(2)}) async-start(bf16[16,16,640]{2,1,0:T(8,128)(2,1)} %add_convert_fusion), calls=%async_computation.1 | async-start | bytes 655360 | tf_op jit(solution)/shard_map/all_to_all | solution.py:194
  78.2 7.2 %psum.7 = f32[32]{0:T(128)S(1)} all-reduce(f32[32]{0:T(128)S(1)} %get-tuple-element.27), channel_id=1, replica_groups=mesh['z'=8,'xh'=2,'co'=2,'xl'=2,'y'=8] {'xh','co'}, use_global_device_ids=true, to_apply=%region_1.0 | all-reduce | flops 32 | bytes 256 | tf_op jit(solution)/shard_map/psum | solution.py:195
  85.4 3.0 %all-to-all-done.1.both_ref = bf16[16,16,640]{2,1,0:T(8,128)(2,1)S(1)} async-done(((bf16[16,16,640]{2,1,0:T(8,128)(2,1)}), bf16[16,16,640]{2,1,0:T(8,128)(2,1)S(1)}, u32[]{:S(2)}, u32[]{:S(2)}) %all-to-all-start.1) | async-done | bytes 327712 | tf_op jit(solution)/shard_map/all_to_all | solution.py:194
  88.4 0.8 arrange.1
  89.2 6.4 %all-to-all-start.2 = ((bf16[4,4,16,1024]{3,2,1,0:T(8,128)(2,1)}), bf16[4,4,16,1024]{3,2,1,0:T(8,128)(2,1)S(1)}, u32[]{:S(2)}, u32[]{:S(2)}) async-start(bf16[4,4,16,1024]{3,2,1,0:T(8,128)(2,1)} %arrange.1), calls=%async_computation.2 | async-start | bytes 1048576 | tf_op jit(solution)/shard_map/all_to_all | solution.py:197
  95.6 0.1 copy.8.scale_ref
  95.7 9.4 %all-to-all-done.2 = bf16[4,4,16,1024]{3,2,1,0:T(8,128)(2,1)S(1)} async-done(((bf16[4,4,16,1024]{3,2,1,0:T(8,128)(2,1)}), bf16[4,4,16,1024]{3,2,1,0:T(8,128)(2,1)S(1)}, u32[]{:S(2)}, u32[]{:S(2)}) %all-to-all-start.2) | async-done | bytes 524320 | tf_op jit(solution)/shard_map/all_to_all | solution.py:197
  105.0 0.0 copy-done.1
  105.0 2.1 %attend.1 = (bf16[32,2048]{1,0:T(8,128)(2,1)S(1)}, bf16[32,2048]{1,0:T(8,128)(2,1)}) custom-call(s32[1,2]{1,0:T(1,128)S(1)} %copy-done.1, s32[1]{0:T(128)} %bitcast.place_ref, bf16[2,2,4,16,1024]{4,3,2,1,0:T(8,128)(2,1)S(1)} %bitcast.13, f32[32,1]{1,0:T(8,128)S(1)} %copy.8.scale_ref, bf16[2,2,2,256,128]{4,3,2,1,0:T(8,128)(2,1)S(1)} %get-tuple-element.30.refs_0_, ...), custom_call_target="tpu_custom_call" | custom-call | tf_op jit(solution)/shard_map/attend/pallas_call | solution.py:166
  107.2 4.0 %collective-permute-start.4 = (bf16[1,32,2048]{2,1,0:T(8,128)(2,1)S(1)}, bf16[1,32,2048]{2,1,0:T(8,128)(2,1)S(1)}, u32[]{:S(2)}, u32[]{:S(2)}) collective-permute-start(bf16[1,32,2048]{2,1,0:T(8,128)(2,1)S(1)} %bitcast.15), channel_id=1, source_target_pairs={{448,0},{0,64},{64,128},{128,192},{192,256},{256,320},{320,384},{3... | collective-permute-start | bytes 393224 | tf_op jit(solution)/shard_map/ppermute | solution.py:203
  111.2 9.6 %collective-permute-done.4 = bf16[1,32,2048]{2,1,0:T(8,128)(2,1)S(1)} collective-permute-done((bf16[1,32,2048]{2,1,0:T(8,128)(2,1)S(1)}, bf16[1,32,2048]{2,1,0:T(8,128)(2,1)S(1)}, u32[]{:S(2)}, u32[]{:S(2)}) %collective-permute-start.4) | collective-permute-done | bytes 131104 | tf_op jit(solution)/shard_map/ppermute | solution.py:203
  120.8 0.7 copy.10
  (1 shorter events, 0.0 us)
Async XLA Ops:
  3.3 8.9 %copy-start = (bf16[1,2,256,2,1024]{4,3,2,1,0:T(2,128)(2,1)S(1)}, bf16[1,2,256,2,1024]{4,3,2,1,0:T(2,128)(2,1)}, u32[]{:S(2)}) copy-start(bf16[1,2,256,2,1024]{4,3,2,1,0:T(2,128)(2,1)} %param.10) | copy-start | bytes 6291460
  3.3 56.3 %all-to-all-start = ((bf16[16,32,2048]{2,1,0:T(8,128)(2,1)}), bf16[16,32,2048]{2,1,0:T(8,128)(2,1)}, u32[]{:S(2)}, u32[]{:S(2)}) async-start(bf16[16,32,2048]{2,1,0:T(8,128)(2,1)} %broadcast_in_dim.27), calls=%async_computation | async-start | bytes 4194304 | tf_op jit(solution)/shard_map/all_to_all | solution.py:186
  17.2 48.1 %collective-permute-start = (bf16[2,2,2,256,128]{4,3,2,1,0:T(8,128)(2,1)}, bf16[2,2,2,256,128]{4,3,2,1,0:T(8,128)(2,1)S(1)}, u32[]{:S(2)}, u32[]{:S(2)}) collective-permute-start(bf16[2,2,2,256,128]{4,3,2,1,0:T(8,128)(2,1)} %get-tuple-element.22), channel_id=1, source_target_pairs={{0,16},{16,0},{32,48},{48,32},{1,17},{17,1},{33,49},{49,33},{2,18}... | collective-permute-start | bytes 1572872 | tf_op jit(solution)/shard_map/ppermute | solution.py:189
  21.7 43.6 %collective-permute-start.1 = (bf16[2,2,2,256,128]{4,3,2,1,0:T(8,128)(2,1)}, bf16[2,2,2,256,128]{4,3,2,1,0:T(8,128)(2,1)S(1)}, u32[]{:S(2)}, u32[]{:S(2)}) collective-permute-start(bf16[2,2,2,256,128]{4,3,2,1,0:T(8,128)(2,1)} %get-tuple-element.23), channel_id=1, source_target_pairs={{0,32},{16,48},{32,0},{48,16},{1,33},{17,49},{33,1},{49,17},{2,34}... | collective-permute-start | bytes 1572872 | tf_op jit(solution)/shard_map/ppermute | solution.py:189
  24.4 40.9 %collective-permute-start.2 = (bf16[2,2,2,256,128]{4,3,2,1,0:T(8,128)(2,1)S(1)}, bf16[2,2,2,256,128]{4,3,2,1,0:T(8,128)(2,1)S(1)}, u32[]{:S(2)}, u32[]{:S(2)}) collective-permute-start(bf16[2,2,2,256,128]{4,3,2,1,0:T(8,128)(2,1)S(1)} %get-tuple-element.24), channel_id=1, source_target_pairs={{0,48},{16,32},{32,16},{48,0},{1,49},{17,33},{33,17},{49,1},{2,50}... | collective-permute-start | bytes 1572872 | tf_op jit(solution)/shard_map/ppermute | solution.py:189
  65.3 39.8 %copy-start.1 = (s32[1,2]{1,0:T(1,128)S(1)}, s32[1,2]{1,0:T(1,128)}, u32[]{:S(2)}) copy-start(s32[1,2]{1,0:T(1,128)} %lengths_ref.1) | copy-start | bytes 28
  65.3 6.4 %collective-permute-start.3 = (bf16[16,16,640]{2,1,0:T(8,128)(2,1)}, bf16[16,16,640]{2,1,0:T(8,128)(2,1)S(1)}, u32[]{:S(2)}, u32[]{:S(2)}) collective-permute-start(bf16[16,16,640]{2,1,0:T(8,128)(2,1)} %get-tuple-element.25), channel_id=1, source_target_pairs={{0,16},{16,0},{1,17},{17,1},{2,18},{18,2},{3,19},{19,3},{4,20},{20... | collective-permute-start | bytes 983048 | tf_op jit(solution)/shard_map/ppermute | solution.py:192
  73.5 14.8 %all-to-all-start.1 = ((bf16[16,16,640]{2,1,0:T(8,128)(2,1)}), bf16[16,16,640]{2,1,0:T(8,128)(2,1)S(1)}, u32[]{:S(2)}, u32[]{:S(2)}) async-start(bf16[16,16,640]{2,1,0:T(8,128)(2,1)} %add_convert_fusion), calls=%async_computation.1 | async-start | bytes 655360 | tf_op jit(solution)/shard_map/all_to_all | solution.py:194
  89.2 15.8 %all-to-all-start.2 = ((bf16[4,4,16,1024]{3,2,1,0:T(8,128)(2,1)}), bf16[4,4,16,1024]{3,2,1,0:T(8,128)(2,1)S(1)}, u32[]{:S(2)}, u32[]{:S(2)}) async-start(bf16[4,4,16,1024]{3,2,1,0:T(8,128)(2,1)} %arrange.1), calls=%async_computation.2 | async-start | bytes 1048576 | tf_op jit(solution)/shard_map/all_to_all | solution.py:197
  107.2 13.6 %collective-permute-start.4 = (bf16[1,32,2048]{2,1,0:T(8,128)(2,1)S(1)}, bf16[1,32,2048]{2,1,0:T(8,128)(2,1)S(1)}, u32[]{:S(2)}, u32[]{:S(2)}) collective-permute-start(bf16[1,32,2048]{2,1,0:T(8,128)(2,1)S(1)} %bitcast.15), channel_id=1, source_target_pairs={{448,0},{0,64},{64,128},{128,192},{192,256},{256,320},{320,384},{3... | collective-permute-start | bytes 393224 | tf_op jit(solution)/shard_map/ppermute | solution.py:203

commit v8 on v7

--- a/solution.py
+++ b/solution.py
@@ -17,35 +17,79 @@
 HBM = pl.BlockSpec(memory_space=pltpu.HBM)
 SMEM = pl.BlockSpec(memory_space=pltpu.SMEM)
 PARAMS = pltpu.CompilerParams(vmem_limit_bytes=32 * 1024 * 1024)
+MOST = pltpu.CompilerParams(vmem_limit_bytes=59 * 1024 * 1024)
 FULL = pltpu.CompilerParams(vmem_limit_bytes=56 * 1024 * 1024)
+
+
+def spread_kernel(hidden_ref, gain_ref, copies_ref, squares_ref, sent, sems):
+    widened = hidden_ref[...].astype(F32)
+    sent[...] = (widened * gain_ref[...]).astype(BF)
+    copies = [
+        pltpu.make_async_copy(sent, copies_ref.at[n], sems.at[n]) for n in range(copies_ref.shape[0])
+    ]
+    for copy in copies:
+        copy.start()
+    squares_ref[...] = jnp.sum(widened * widened, axis=1, keepdims=True)
+    for copy in copies:
+        copy.wait()
+
+
+def spread(hidden, gain, count):
+    rows = hidden.shape[0]
+    return pl.pallas_call(
+        spread_kernel,
+        out_shape=[
+            jax.ShapeDtypeStruct((count,) + hidden.shape, BF),
+            jax.ShapeDtypeStruct((rows, 1), F32),
+        ],
+        in_specs=[VMEM, VMEM],
+        out_specs=[HBM, VMEM],
+        scratch_shapes=[pltpu.VMEM(hidden.shape, BF), pltpu.SemaphoreType.DMA((count,))],
+        compiler_params=MOST,
+        name="spread",
+    )(hidden, gain)
+
+
+def join_kernel(keep_ref, other_ref, out_ref):
+    out_ref[...] = (keep_ref[...].astype(F32) + other_ref[...].astype(F32)).astype(BF)
+
+
+def join(keep, other):
+    return pl.pallas_call(
+        join_kernel,
+        out_shape=jax.ShapeDtypeStruct(keep.shape, BF),
+        in_specs=[VMEM, VMEM],
+        out_specs=VMEM,
+        compiler_params=PARAMS,
+        name="join",
+    )(keep, other)
 
 
 def project_kernel(place_ref, gathered_ref, query_ref, pair_ref, keep_ref, send_ref, *scratch):
     gathered, query, pair, sems = scratch
     count, rows, width = gathered_ref.shape
     half = rows // 2
-    step = count // 4
-    moves = [(query_ref, query), (pair_ref, pair)]
-    for n in range(4):
-        part = pl.ds(n * step, step)
-        moves.append((gathered_ref.at[part], gathered.at[part]))
+    block = 256
+    moves = [(gathered_ref, gathered), (query_ref.at[:, pl.ds(0, block)], query.at[:, pl.ds(0, block)])]
+    moves.append((query_ref.at[:, pl.ds(block, block)], query.at[:, pl.ds(block, block)]))
+    moves.append((pair_ref, pair))
     copies = [pltpu.make_async_copy(a, b, sems.at[n]) for n, (a, b) in enumerate(moves)]
     for copy in copies:
         copy.start()
     copies[0].wait()
-    copies[1].wait()
-    for n in range(4):
-        copies[2 + n].wait()
-        block = gathered[n * step : (n + 1) * step].reshape(step * rows, width)
-        for weight, lanes in ((query, slice(0, 512)), (pair, slice(512, 640))):
-            part = jnp.dot(block, weight[...], preferred_element_type=F32)
-            part = part.astype(BF).reshape(step, 2, half, part.shape[1])
-            for core in range(2):
-
-                @pl.when(place_ref[0] == core)
-                def _():
-                    keep_ref[n * step : (n + 1) * step, :, lanes] = part[:, core]
-                    send_ref[n * step : (n + 1) * step, :, lanes] = part[:, 1 - core]
+    flat = gathered[...].reshape(count * rows, width)
+    for n in range(3):
+        copies[1 + n].wait()
+        weight = query[:, n * block : (n + 1) * block] if n < 2 else pair[...]
+        lanes = slice(n * block, n * block + weight.shape[1])
+        part = jnp.dot(flat, weight, preferred_element_type=F32)
+        part = part.astype(BF).reshape(count, 2, half, part.shape[1])
+        for core in range(2):
+
+            @pl.when(place_ref[0] == core)
+            def _():
+                keep_ref[:, :, lanes] = part[:, core]
+                send_ref[:, :, lanes] = part[:, 1 - core]
 
 
 def project(place, *operands):
@@ -54,7 +98,7 @@
         out_shape=[jax.ShapeDtypeStruct((16, 16, 640), BF)] * 2,
         in_specs=[SMEM] + [HBM] * 3,
         out_specs=[VMEM] * 2,
-        scratch_shapes=[pltpu.VMEM(x.shape, BF) for x in operands] + [pltpu.SemaphoreType.DMA((6,))],
+        scratch_shapes=[pltpu.VMEM(x.shape, BF) for x in operands] + [pltpu.SemaphoreType.DMA((4,))],
         compiler_params=FULL,
         name="project",
     )(place, *operands)
@@ -177,19 +221,15 @@
     rows, width = hidden_in.shape[1:]
     row_count = 4
     row_index = lax.axis_index(ROW)
-    widened = hidden_in[0].astype(F32)
-    sent = (widened * norm_gain[0][None, :]).astype(BF)
-    local_squares = jnp.sum(widened * widened, axis=1)
     swap = [(0, 1), (1, 0)]
-
-    count = 16
-    gathered = lax.all_to_all(jnp.broadcast_to(sent[None], (count, rows, width)), COL, 0, 0)
+    copies, local_squares = spread(hidden_in[0], norm_gain, 16)
+    gathered = lax.all_to_all(copies, COL, 0, 0)
     caches = list(pick((0, 1, 2, 3), row_index[None], kv_cache[0]))
     for k in range(1, row_count):
         caches[k] = lax.ppermute(caches[k], ROW, [(i, i ^ k) for i in range(row_count)])
     keep, send = project(lax.axis_index("co")[None], gathered, q_weight[0], kv_weight[0])
     send, caches = lax.optimization_barrier((send, caches))
-    both = (keep.astype(F32) + lax.ppermute(send, "co", swap).astype(F32)).astype(BF)
+    both = join(keep, lax.ppermute(send, "co", swap))
     both, local_squares = lax.optimization_barrier((both, local_squares))
     both = lax.all_to_all(both, COL, 0, 0)
     squares = lax.psum(local_squares, ROW)
@@ -197,7 +237,7 @@
     parts = lax.all_to_all(arrange(both), ROW, 0, 0)
     parts = parts.reshape((2, 2) + parts.shape[1:])
 
-    scale = lax.rsqrt(squares / (width * row_count) + EPSILON)[:, None]
+    scale = lax.rsqrt(squares / (width * row_count) + EPSILON)
     attended, new_kv = attend(lengths, row_index[None], parts, scale, caches)
     count = 8
     handed = lax.ppermute(attended[None], "z", [((i - 1) % count, i) for i in range(count)])

time: 122 us -> 126 us (1.033)
  blocking collectives: 7.18 us -> 13 us
  Pallas kernels: 13.8 us -> 17.8 us
  waiting for transfers between devices: 54.4 us -> 51.5 us
  other arithmetic: 2.84 us -> 0.01 us
    psum x1, blocking collectives: 7.18 us -> 13 us  [shards(): squares = lax.psum(local_squares, ROW)]
    pallas_call x0 -> x2, Pallas kernels: none -> 3.82 us  [the longest x1 3.02 us: spread(): pl.pallas_call(spread_kernel, out_shape=[jax.ShapeDtypeStruct((count,) +...]
    all_to_all x1, waiting for transfers between devices: 3.01 us -> 0.01 us  [shards(): both = lax.all_to_all(both, COL, 0, 0)]
    convert_element_type x1 -> x0, other arithmetic: 1.79 us -> none  [shards(): (keep.astype(F32) + lax.ppermute(send, 'co', swap).astype(F32)).astype(BF)]
    broadcast_in_dim x2 -> x0, local copies, waits for them, and re-layouts: 1.67 us -> none  [the longest x1 1.58 us: shards(): jnp.broadcast_to(sent[None], (count, rows, width))]
  transfers between devices with their start and end apart: 8 -> 8, of which waited for: 5 -> 4; matrix products, arithmetic and copies ran while one was open for 0% -> 0% of each run, Pallas kernels for 9% -> 9%
where the time goes in v8:
time: 126 us; the launch traced here: 125 us
  waiting for transfers between devices  51.5 us (41%)
  starting transfers between devices  40.7 us (32%)
  Pallas kernels  17.8 us (14%)
  blocking collectives  13 us (10%)
  local copies, waits for them, and re-layouts  1.64 us (1%)
    all_to_all x1, waiting for transfers between devices, shards(): gathered = lax.all_to_all(copies, COL, 0, 0)  30.9 us
    psum x1, blocking collectives, shards(): squares = lax.psum(local_squares, ROW)  13 us
    ppermute x3, starting transfers between devices, shards(): lax.ppermute(caches[k], ROW, [(i, i ^ k) for i in range(row_count)])  11.4 us
    ppermute x1, waiting for transfers between devices, shards(): lax.ppermute(attended[None], 'z', [((i - 1) % count, i) for i in range(co...  9.65 us
    all_to_all x1, waiting for transfers between devices, shards(): parts = lax.all_to_all(arrange(both), ROW, 0, 0)  9.47 us
    all_to_all x1, starting transfers between devices, shards(): gathered = lax.all_to_all(copies, COL, 0, 0)  8.88 us
    all_to_all x1, starting transfers between devices, shards(): parts = lax.all_to_all(arrange(both), ROW, 0, 0)  7.27 us
    pallas_call x1, Pallas kernels, project(): pl.pallas_call(project_kernel, out_shape=[jax.ShapeDtypeStruct((16, 16, 6...  5.97 us
  transfers between devices with their start and end apart: 8, of which 4 were waited for; matrix products, arithmetic and copies ran while one was open for 0% of the time, Pallas kernels for 9%

profile of v8, /device:TPU:1, one launch (start us, length us, event | category | flops | bytes accessed | tf_op | source)
XLA Modules:
  0.0 125.4 jit_solution(15769123390752760439)
XLA Ops:
  0.6 3.0 %spread.1 = (bf16[16,32,2048]{2,1,0:T(8,128)(2,1)}, f32[32,1]{1,0:T(8,128)}) custom-call(bf16[32,2048]{1,0:T(8,128)(2,1)} %bitcast.14, f32[1,2048]{1,0:T(1,128)} %gain_ref.1), custom_call_target="tpu_custom_call" | custom-call | tf_op jit(solution)/shard_map/spread/pallas_call | solution.py:39
  3.7 0.0 copy-start
  3.7 8.9 %all-to-all-start = ((bf16[16,32,2048]{2,1,0:T(8,128)(2,1)}), bf16[16,32,2048]{2,1,0:T(8,128)(2,1)}, u32[]{:S(2)}, u32[]{:S(2)}) async-start(bf16[16,32,2048]{2,1,0:T(8,128)(2,1)} %get-tuple-element.21), calls=%async_computation | async-start | bytes 4194304 | tf_op jit(solution)/shard_map/all_to_all | solution.py:226
  12.6 0.0 copy-done
  12.6 5.1 %pick.1 = (bf16[2,2,2,256,128]{4,3,2,1,0:T(8,128)(2,1)S(1)}, bf16[2,2,2,256,128]{4,3,2,1,0:T(8,128)(2,1)}, bf16[2,2,2,256,128]{4,3,2,1,0:T(8,128)(2,1)}, bf16[2,2,2,256,128]{4,3,2,1,0:T(8,128)(2,1)S(1)}) custom-call(s32[1]{0:T(128)} %bitcast.place_ref, bf16[2,256,2,1024]{3,2,1,0:T(2,128)(2,1)S(1)} %bitcast.10), custom_call_target="tpu_custom_call" | custom-call | tf_op jit(solution)/shard_map/pick/pallas_call | solution.py:119
  17.6 4.5 %collective-permute-start = (bf16[2,2,2,256,128]{4,3,2,1,0:T(8,128)(2,1)}, bf16[2,2,2,256,128]{4,3,2,1,0:T(8,128)(2,1)S(1)}, u32[]{:S(2)}, u32[]{:S(2)}) collective-permute-start(bf16[2,2,2,256,128]{4,3,2,1,0:T(8,128)(2,1)} %get-tuple-element.25), channel_id=1, source_target_pairs={{0,16},{16,0},{32,48},{48,32},{1,17},{17,1},{33,49},{49,33},{2,18}... | collective-permute-start | bytes 1572872 | tf_op jit(solution)/shard_map/ppermute | solution.py:229
  22.1 2.7 %collective-permute-start.1 = (bf16[2,2,2,256,128]{4,3,2,1,0:T(8,128)(2,1)}, bf16[2,2,2,256,128]{4,3,2,1,0:T(8,128)(2,1)S(1)}, u32[]{:S(2)}, u32[]{:S(2)}) collective-permute-start(bf16[2,2,2,256,128]{4,3,2,1,0:T(8,128)(2,1)} %get-tuple-element.26), channel_id=1, source_target_pairs={{0,32},{16,48},{32,0},{48,16},{1,33},{17,49},{33,1},{49,17},{2,34}... | collective-permute-start | bytes 1572872 | tf_op jit(solution)/shard_map/ppermute | solution.py:229
  24.9 4.2 %collective-permute-start.2 = (bf16[2,2,2,256,128]{4,3,2,1,0:T(8,128)(2,1)S(1)}, bf16[2,2,2,256,128]{4,3,2,1,0:T(8,128)(2,1)S(1)}, u32[]{:S(2)}, u32[]{:S(2)}) collective-permute-start(bf16[2,2,2,256,128]{4,3,2,1,0:T(8,128)(2,1)S(1)} %get-tuple-element.27), channel_id=1, source_target_pairs={{0,48},{16,32},{32,16},{48,0},{1,49},{17,33},{33,17},{49,1},{2,50}... | collective-permute-start | bytes 1572872 | tf_op jit(solution)/shard_map/ppermute | solution.py:229
  29.1 30.9 %all-to-all-done.gathered_ref = bf16[16,32,2048]{2,1,0:T(8,128)(2,1)} async-done(((bf16[16,32,2048]{2,1,0:T(8,128)(2,1)}), bf16[16,32,2048]{2,1,0:T(8,128)(2,1)}, u32[]{:S(2)}, u32[]{:S(2)}) %all-to-all-start) | async-done | bytes 2097184 | tf_op jit(solution)/shard_map/all_to_all | solution.py:226
  60.0 0.0 copy-start.3
  60.0 6.0 %project.1 = (bf16[16,16,640]{2,1,0:T(8,128)(2,1)}, bf16[16,16,640]{2,1,0:T(8,128)(2,1)}) custom-call(s32[1]{0:T(128)} %bitcast.1.place_ref, bf16[16,32,2048]{2,1,0:T(8,128)(2,1)} %all-to-all-done.gathered_ref, bf16[2048,512]{1,0:T(8,128)(2,1)} %bitcast.12, bf16[2048,128]{1,0:T(8,128)(2,1)} %bitcast.13), custom_call_target="tpu_custom_call" | custom-call | tf_op jit(solution)/shard_map/project/pallas_call | solution.py:96
  66.0 0.0 copy-start.2
  66.0 0.0 collective-permute-done.refs_1_
  66.0 0.0 collective-permute-done.1.refs_2_
  66.0 0.0 collective-permute-done.2.refs_3_
  66.0 4.9 %collective-permute-start.3 = (bf16[16,16,640]{2,1,0:T(8,128)(2,1)}, bf16[16,16,640]{2,1,0:T(8,128)(2,1)S(1)}, u32[]{:S(2)}, u32[]{:S(2)}) collective-permute-start(bf16[16,16,640]{2,1,0:T(8,128)(2,1)} %get-tuple-element.28), channel_id=1, source_target_pairs={{0,16},{16,0},{1,17},{17,1},{2,18},{18,2},{3,19},{19,3},{4,20},{20... | collective-permute-start | bytes 983048 | tf_op jit(solution)/shard_map/ppermute | solution.py:232
  70.9 1.4 %collective-permute-done.3.other_ref = bf16[16,16,640]{2,1,0:T(8,128)(2,1)S(1)} collective-permute-done((bf16[16,16,640]{2,1,0:T(8,128)(2,1)}, bf16[16,16,640]{2,1,0:T(8,128)(2,1)S(1)}, u32[]{:S(2)}, u32[]{:S(2)}) %collective-permute-start.3) | collective-permute-done | bytes 327712 | tf_op jit(solution)/shard_map/ppermute | solution.py:232
  72.4 0.0 copy-start.1
  72.4 1.0 copy-done.1
  73.3 0.8 join.1
  74.1 4.5 %all-to-all-start.1 = ((bf16[16,16,640]{2,1,0:T(8,128)(2,1)}), bf16[16,16,640]{2,1,0:T(8,128)(2,1)S(1)}, u32[]{:S(2)}, u32[]{:S(2)}) async-start(bf16[16,16,640]{2,1,0:T(8,128)(2,1)} %join.1), calls=%async_computation.1 | async-start | bytes 655360 | tf_op jit(solution)/shard_map/all_to_all | solution.py:234
  78.6 0.0 copy-done.3
  78.6 13.0 %psum.7 = f32[32,1]{1,0:T(8,128)S(1)} all-reduce(f32[32,1]{1,0:T(8,128)S(1)} %copy-done.3), channel_id=1, replica_groups=mesh['z'=8,'xh'=2,'co'=2,'xl'=2,'y'=8] {'xh','co'}, use_global_device_ids=true, to_apply=%region_0.0 | all-reduce | flops 32 | bytes 256 | tf_op jit(solution)/shard_map/psum | solution.py:235
  91.6 0.0 all-to-all-done.1.both_ref
  91.6 0.8 arrange.1
  92.4 7.3 %all-to-all-start.2 = ((bf16[4,4,16,1024]{3,2,1,0:T(8,128)(2,1)}), bf16[4,4,16,1024]{3,2,1,0:T(8,128)(2,1)S(1)}, u32[]{:S(2)}, u32[]{:S(2)}) async-start(bf16[4,4,16,1024]{3,2,1,0:T(8,128)(2,1)} %arrange.1), calls=%async_computation.2 | async-start | bytes 1048576 | tf_op jit(solution)/shard_map/all_to_all | solution.py:237
  99.7 9.5 %all-to-all-done.2 = bf16[4,4,16,1024]{3,2,1,0:T(8,128)(2,1)S(1)} async-done(((bf16[4,4,16,1024]{3,2,1,0:T(8,128)(2,1)}), bf16[4,4,16,1024]{3,2,1,0:T(8,128)(2,1)S(1)}, u32[]{:S(2)}, u32[]{:S(2)}) %all-to-all-start.2) | async-done | bytes 524320 | tf_op jit(solution)/shard_map/all_to_all | solution.py:237
  109.2 0.0 copy-done.2
  109.2 2.1 %attend.1 = (bf16[32,2048]{1,0:T(8,128)(2,1)S(1)}, bf16[32,2048]{1,0:T(8,128)(2,1)}) custom-call(s32[1,2]{1,0:T(1,128)S(1)} %copy-done.2, s32[1]{0:T(128)} %bitcast.place_ref, bf16[2,2,4,16,1024]{4,3,2,1,0:T(8,128)(2,1)S(1)} %bitcast.9, f32[32,1]{1,0:T(8,128)S(1)} %add_rsqrt_fusion.scale_ref, bf16[2,2,2,256,128]{4,3,2,1,0:T(8,128)(2,1)S(1)} %get-tuple-element.34.refs_0_, ...), custom_call_target="tpu_custom_call" | custom-call | tf_op jit(solution)/shard_map/attend/pallas_call | solution.py:210
  111.3 3.7 %collective-permute-start.4 = (bf16[1,32,2048]{2,1,0:T(8,128)(2,1)S(1)}, bf16[1,32,2048]{2,1,0:T(8,128)(2,1)S(1)}, u32[]{:S(2)}, u32[]{:S(2)}) collective-permute-start(bf16[1,32,2048]{2,1,0:T(8,128)(2,1)S(1)} %bitcast.11), channel_id=1, source_target_pairs={{448,0},{0,64},{64,128},{128,192},{192,256},{256,320},{320,384},{3... | collective-permute-start | bytes 393224 | tf_op jit(solution)/shard_map/ppermute | solution.py:243
  115.1 9.7 %collective-permute-done.4 = bf16[1,32,2048]{2,1,0:T(8,128)(2,1)S(1)} collective-permute-done((bf16[1,32,2048]{2,1,0:T(8,128)(2,1)S(1)}, bf16[1,32,2048]{2,1,0:T(8,128)(2,1)S(1)}, u32[]{:S(2)}, u32[]{:S(2)}) %collective-permute-start.4) | collective-permute-done | bytes 131104 | tf_op jit(solution)/shard_map/ppermute | solution.py:243
  124.7 0.7 copy.9
  (1 shorter events, 0.0 us)
Async XLA Ops:
  3.7 8.9 %copy-start = (bf16[1,2,256,2,1024]{4,3,2,1,0:T(2,128)(2,1)S(1)}, bf16[1,2,256,2,1024]{4,3,2,1,0:T(2,128)(2,1)}, u32[]{:S(2)}) copy-start(bf16[1,2,256,2,1024]{4,3,2,1,0:T(2,128)(2,1)} %param.10) | copy-start | bytes 6291460
  3.7 56.3 %all-to-all-start = ((bf16[16,32,2048]{2,1,0:T(8,128)(2,1)}), bf16[16,32,2048]{2,1,0:T(8,128)(2,1)}, u32[]{:S(2)}, u32[]{:S(2)}) async-start(bf16[16,32,2048]{2,1,0:T(8,128)(2,1)} %get-tuple-element.21), calls=%async_computation | async-start | bytes 4194304 | tf_op jit(solution)/shard_map/all_to_all | solution.py:226
  17.6 48.4 %collective-permute-start = (bf16[2,2,2,256,128]{4,3,2,1,0:T(8,128)(2,1)}, bf16[2,2,2,256,128]{4,3,2,1,0:T(8,128)(2,1)S(1)}, u32[]{:S(2)}, u32[]{:S(2)}) collective-permute-start(bf16[2,2,2,256,128]{4,3,2,1,0:T(8,128)(2,1)} %get-tuple-element.25), channel_id=1, source_target_pairs={{0,16},{16,0},{32,48},{48,32},{1,17},{17,1},{33,49},{49,33},{2,18}... | collective-permute-start | bytes 1572872 | tf_op jit(solution)/shard_map/ppermute | solution.py:229
  22.1 43.9 %collective-permute-start.1 = (bf16[2,2,2,256,128]{4,3,2,1,0:T(8,128)(2,1)}, bf16[2,2,2,256,128]{4,3,2,1,0:T(8,128)(2,1)S(1)}, u32[]{:S(2)}, u32[]{:S(2)}) collective-permute-start(bf16[2,2,2,256,128]{4,3,2,1,0:T(8,128)(2,1)} %get-tuple-element.26), channel_id=1, source_target_pairs={{0,32},{16,48},{32,0},{48,16},{1,33},{17,49},{33,1},{49,17},{2,34}... | collective-permute-start | bytes 1572872 | tf_op jit(solution)/shard_map/ppermute | solution.py:229
  24.9 41.2 %collective-permute-start.2 = (bf16[2,2,2,256,128]{4,3,2,1,0:T(8,128)(2,1)S(1)}, bf16[2,2,2,256,128]{4,3,2,1,0:T(8,128)(2,1)S(1)}, u32[]{:S(2)}, u32[]{:S(2)}) collective-permute-start(bf16[2,2,2,256,128]{4,3,2,1,0:T(8,128)(2,1)S(1)} %get-tuple-element.27), channel_id=1, source_target_pairs={{0,48},{16,32},{32,16},{48,0},{1,49},{17,33},{33,17},{49,1},{2,50}... | collective-permute-start | bytes 1572872 | tf_op jit(solution)/shard_map/ppermute | solution.py:229
  60.0 18.6 %copy-start.3 = (f32[32,1]{1,0:T(8,128)S(1)}, f32[32,1]{1,0:T(8,128)}, u32[]{:S(2)}) copy-start(f32[32,1]{1,0:T(8,128)} %get-tuple-element.31) | copy-start | bytes 388
  66.0 43.2 %copy-start.2 = (s32[1,2]{1,0:T(1,128)S(1)}, s32[1,2]{1,0:T(1,128)}, u32[]{:S(2)}) copy-start(s32[1,2]{1,0:T(1,128)} %lengths_ref.1) | copy-start | bytes 28
  66.0 6.3 %collective-permute-start.3 = (bf16[16,16,640]{2,1,0:T(8,128)(2,1)}, bf16[16,16,640]{2,1,0:T(8,128)(2,1)S(1)}, u32[]{:S(2)}, u32[]{:S(2)}) collective-permute-start(bf16[16,16,640]{2,1,0:T(8,128)(2,1)} %get-tuple-element.28), channel_id=1, source_target_pairs={{0,16},{16,0},{1,17},{17,1},{2,18},{18,2},{3,19},{19,3},{4,20},{20... | collective-permute-start | bytes 983048 | tf_op jit(solution)/shard_map/ppermute | solution.py:232
  72.4 1.0 copy-start.1
  74.1 17.5 %all-to-all-start.1 = ((bf16[16,16,640]{2,1,0:T(8,128)(2,1)}), bf16[16,16,640]{2,1,0:T(8,128)(2,1)S(1)}, u32[]{:S(2)}, u32[]{:S(2)}) async-start(bf16[16,16,640]{2,1,0:T(8,128)(2,1)} %join.1), calls=%async_computation.1 | async-start | bytes 655360 | tf_op jit(solution)/shard_map/all_to_all | solution.py:234
  92.4 16.8 %all-to-all-start.2 = ((bf16[4,4,16,1024]{3,2,1,0:T(8,128)(2,1)}), bf16[4,4,16,1024]{3,2,1,0:T(8,128)(2,1)S(1)}, u32[]{:S(2)}, u32[]{:S(2)}) async-start(bf16[4,4,16,1024]{3,2,1,0:T(8,128)(2,1)} %arrange.1), calls=%async_computation.2 | async-start | bytes 1048576 | tf_op jit(solution)/shard_map/all_to_all | solution.py:237
  111.3 13.4 %collective-permute-start.4 = (bf16[1,32,2048]{2,1,0:T(8,128)(2,1)S(1)}, bf16[1,32,2048]{2,1,0:T(8,128)(2,1)S(1)}, u32[]{:S(2)}, u32[]{:S(2)}) collective-permute-start(bf16[1,32,2048]{2,1,0:T(8,128)(2,1)S(1)} %bitcast.11), channel_id=1, source_target_pairs={{448,0},{0,64},{64,128},{128,192},{192,256},{256,320},{320,384},{3... | collective-permute-start | bytes 393224 | tf_op jit(solution)/shard_map/ppermute | solution.py:243

commit v9 on v7

--- a/solution.py
+++ b/solution.py
@@ -14,48 +14,35 @@
 BF = jnp.bfloat16
 F32 = jnp.float32
 VMEM = pl.BlockSpec(memory_space=pltpu.VMEM)
-HBM = pl.BlockSpec(memory_space=pltpu.HBM)
 SMEM = pl.BlockSpec(memory_space=pltpu.SMEM)
 PARAMS = pltpu.CompilerParams(vmem_limit_bytes=32 * 1024 * 1024)
-FULL = pltpu.CompilerParams(vmem_limit_bytes=56 * 1024 * 1024)
-
-
-def project_kernel(place_ref, gathered_ref, query_ref, pair_ref, keep_ref, send_ref, *scratch):
-    gathered, query, pair, sems = scratch
+
+
+def project_kernel(place_ref, gathered_ref, query_ref, pair_ref, keep_ref, send_ref):
     count, rows, width = gathered_ref.shape
     half = rows // 2
-    step = count // 4
-    moves = [(query_ref, query), (pair_ref, pair)]
-    for n in range(4):
-        part = pl.ds(n * step, step)
-        moves.append((gathered_ref.at[part], gathered.at[part]))
-    copies = [pltpu.make_async_copy(a, b, sems.at[n]) for n, (a, b) in enumerate(moves)]
-    for copy in copies:
-        copy.start()
-    copies[0].wait()
-    copies[1].wait()
-    for n in range(4):
-        copies[2 + n].wait()
-        block = gathered[n * step : (n + 1) * step].reshape(step * rows, width)
-        for weight, lanes in ((query, slice(0, 512)), (pair, slice(512, 640))):
-            part = jnp.dot(block, weight[...], preferred_element_type=F32)
+    step = count // 2
+    for n in range(2):
+        cols = slice(n * step, (n + 1) * step)
+        block = gathered_ref[cols].reshape(step * rows, width)
+        for weight_ref, lanes in ((query_ref, slice(0, 512)), (pair_ref, slice(512, 640))):
+            part = jnp.dot(block, weight_ref[...], preferred_element_type=F32)
             part = part.astype(BF).reshape(step, 2, half, part.shape[1])
             for core in range(2):
 
                 @pl.when(place_ref[0] == core)
                 def _():
-                    keep_ref[n * step : (n + 1) * step, :, lanes] = part[:, core]
-                    send_ref[n * step : (n + 1) * step, :, lanes] = part[:, 1 - core]
+                    keep_ref[cols, :, lanes] = part[:, core]
+                    send_ref[cols, :, lanes] = part[:, 1 - core]
 
 
 def project(place, *operands):
     return pl.pallas_call(
         project_kernel,
         out_shape=[jax.ShapeDtypeStruct((16, 16, 640), BF)] * 2,
-        in_specs=[SMEM] + [HBM] * 3,
+        in_specs=[SMEM] + [VMEM] * 3,
         out_specs=[VMEM] * 2,
-        scratch_shapes=[pltpu.VMEM(x.shape, BF) for x in operands] + [pltpu.SemaphoreType.DMA((6,))],
-        compiler_params=FULL,
+        compiler_params=PARAMS,
         name="project",
     )(place, *operands)
 

time: 122 us -> 121 us (level)
  local copies, waits for them, and re-layouts: 2.34 us -> 5.52 us
  Pallas kernels: 13.8 us -> 11.1 us
    pallas_call x1, Pallas kernels: 5.73 us -> 2.32 us  [project(): pl.pallas_call(project_kernel, out_shape=[jax.ShapeDtypeStruct((16, 16, 6...]
    unnamed x5 -> x9, local copies, waits for them, and re-layouts: 0.67 us -> 3.84 us
    ppermute x3, waiting for transfers between devices: 0.01 us -> 2.44 us  [shards(): lax.ppermute(caches[k], ROW, [(i, i ^ k) for i in range(row_count)])]
    all_to_all x1, starting transfers between devices: 4.65 us -> 6.85 us  [shards(): both = lax.all_to_all(both, COL, 0, 0)]
    all_to_all x1, waiting for transfers between devices: 30.9 us -> 29.2 us  [shards(): lax.all_to_all(jnp.broadcast_to(sent[None], (count, rows, width)), COL, 0...]
    ppermute x1, starting transfers between devices: 4.96 us -> 3.53 us  [shards(): lax.ppermute(send, 'co', swap).astype(F32)]
  transfers between devices with their start and end apart: 8 -> 8, of which waited for: 5 -> 6; matrix products, arithmetic and copies ran while one was open for 0% -> 0% of each run, Pallas kernels for 9% -> 6%
where the time goes in v9:
time: 121 us
  waiting for transfers between devices  54.9 us (45%)
  starting transfers between devices  39.3 us (32%)
  Pallas kernels  11.1 us (9%)
  blocking collectives  7.17 us (6%)
  local copies, waits for them, and re-layouts  5.52 us (5%)
  other arithmetic  1.86 us (2%)
    all_to_all x1, waiting for transfers between devices, shards(): lax.all_to_all(jnp.broadcast_to(sent[None], (count, rows, width)), COL, 0...  29.2 us
    ppermute x3, starting transfers between devices, shards(): lax.ppermute(caches[k], ROW, [(i, i ^ k) for i in range(row_count)])  10.8 us
    ppermute x1, waiting for transfers between devices, shards(): lax.ppermute(attended[None], 'z', [((i - 1) % count, i) for i in range(co...  9.65 us
    all_to_all x1, waiting for transfers between devices, shards(): parts = lax.all_to_all(arrange(both), ROW, 0, 0)  9.39 us
    all_to_all x1, starting transfers between devices, shards(): lax.all_to_all(jnp.broadcast_to(sent[None], (count, rows, width)), COL, 0...  8.81 us
    psum x1, blocking collectives, shards(): squares = lax.psum(local_squares, ROW)  7.17 us
    all_to_all x1, starting transfers between devices, shards(): both = lax.all_to_all(both, COL, 0, 0)  6.85 us
    all_to_all x1, starting transfers between devices, shards(): parts = lax.all_to_all(arrange(both), ROW, 0, 0)  5.56 us
  transfers between devices with their start and end apart: 8, of which 6 were waited for; matrix products, arithmetic and copies ran while one was open for 0% of the time, Pallas kernels for 6%

profile of v9, /device:TPU:1, one launch (start us, length us, event | category | flops | bytes accessed | tf_op | source)
XLA Modules:
  0.0 120.6 jit_solution(12489739083698803306)
XLA Ops:
  0.6 1.1 fusion.1
  1.7 1.6 %broadcast_in_dim.27 = bf16[16,32,2048]{2,1,0:T(8,128)(2,1)} broadcast(bf16[32,2048]{1,0:T(8,128)(2,1)S(1)} %get-tuple-element.37), dimensions={1,2} | broadcast | bytes 2228224 | tf_op jit(solution)/shard_map/broadcast_in_dim | solution.py:173
  3.3 0.0 copy-start.2
  3.3 8.8 %all-to-all-start = ((bf16[16,32,2048]{2,1,0:T(8,128)(2,1)}), bf16[16,32,2048]{2,1,0:T(8,128)(2,1)S(1)}, u32[]{:S(2)}, u32[]{:S(2)}) async-start(bf16[16,32,2048]{2,1,0:T(8,128)(2,1)} %broadcast_in_dim.27), calls=%async_computation | async-start | bytes 4194304 | tf_op jit(solution)/shard_map/all_to_all | solution.py:173
  12.1 0.0 copy-start.1
  12.1 1.6 %copy-done.1 = bf16[1,2,256,2,1024]{4,3,2,1,0:T(2,128)(2,1)S(1)} copy-done((bf16[1,2,256,2,1024]{4,3,2,1,0:T(2,128)(2,1)S(1)}, bf16[1,2,256,2,1024]{4,3,2,1,0:T(2,128)(2,1)}, u32[]{:S(2)}) %copy-start.1) | copy-done | bytes 2097176
  13.7 5.0 %pick.1 = (bf16[2,2,2,256,128]{4,3,2,1,0:T(8,128)(2,1)S(1)}, bf16[2,2,2,256,128]{4,3,2,1,0:T(8,128)(2,1)}, bf16[2,2,2,256,128]{4,3,2,1,0:T(8,128)(2,1)}, bf16[2,2,2,256,128]{4,3,2,1,0:T(8,128)(2,1)}) custom-call(s32[1]{0:T(128)} %bitcast.place_ref, bf16[2,256,2,1024]{3,2,1,0:T(2,128)(2,1)S(1)} %bitcast.15), custom_call_target="tpu_custom_call" | custom-call | tf_op jit(solution)/shard_map/pick/pallas_call | solution.py:62
  18.7 3.8 %collective-permute-start = (bf16[2,2,2,256,128]{4,3,2,1,0:T(8,128)(2,1)}, bf16[2,2,2,256,128]{4,3,2,1,0:T(8,128)(2,1)}, u32[]{:S(2)}, u32[]{:S(2)}) collective-permute-start(bf16[2,2,2,256,128]{4,3,2,1,0:T(8,128)(2,1)} %get-tuple-element.22), channel_id=1, source_target_pairs={{0,16},{16,0},{32,48},{48,32},{1,17},{17,1},{33,49},{49,33},{2,18}... | collective-permute-start | bytes 1572872 | tf_op jit(solution)/shard_map/ppermute | solution.py:176
  22.5 3.4 %collective-permute-start.1 = (bf16[2,2,2,256,128]{4,3,2,1,0:T(8,128)(2,1)}, bf16[2,2,2,256,128]{4,3,2,1,0:T(8,128)(2,1)}, u32[]{:S(2)}, u32[]{:S(2)}) collective-permute-start(bf16[2,2,2,256,128]{4,3,2,1,0:T(8,128)(2,1)} %get-tuple-element.23), channel_id=1, source_target_pairs={{0,32},{16,48},{32,0},{48,16},{1,33},{17,49},{33,1},{49,17},{2,34}... | collective-permute-start | bytes 1572872 | tf_op jit(solution)/shard_map/ppermute | solution.py:176
  25.9 3.6 %collective-permute-start.2 = (bf16[2,2,2,256,128]{4,3,2,1,0:T(8,128)(2,1)}, bf16[2,2,2,256,128]{4,3,2,1,0:T(8,128)(2,1)}, u32[]{:S(2)}, u32[]{:S(2)}) collective-permute-start(bf16[2,2,2,256,128]{4,3,2,1,0:T(8,128)(2,1)} %get-tuple-element.24), channel_id=1, source_target_pairs={{0,48},{16,32},{32,16},{48,0},{1,49},{17,33},{33,17},{49,1},{2,50}... | collective-permute-start | bytes 1572872 | tf_op jit(solution)/shard_map/ppermute | solution.py:176
  29.5 29.2 %all-to-all-done.gathered_ref = bf16[16,32,2048]{2,1,0:T(8,128)(2,1)S(1)} async-done(((bf16[16,32,2048]{2,1,0:T(8,128)(2,1)}), bf16[16,32,2048]{2,1,0:T(8,128)(2,1)S(1)}, u32[]{:S(2)}, u32[]{:S(2)}) %all-to-all-start) | async-done | bytes 2097184 | tf_op jit(solution)/shard_map/all_to_all | solution.py:173
  58.7 0.0 copy-done.2
  58.7 0.0 copy-start
  58.7 1.6 %copy-done = bf16[1,2048,512]{2,1,0:T(8,128)(2,1)S(1)} copy-done((bf16[1,2048,512]{2,1,0:T(8,128)(2,1)S(1)}, bf16[1,2048,512]{2,1,0:T(8,128)(2,1)}, u32[]{:S(2)}) %copy-start) | copy-done | bytes 2097176
  60.3 2.3 %project.1 = (bf16[16,16,640]{2,1,0:T(8,128)(2,1)S(1)}, bf16[16,16,640]{2,1,0:T(8,128)(2,1)S(1)}) custom-call(s32[1]{0:T(128)} %bitcast.1.place_ref, bf16[16,32,2048]{2,1,0:T(8,128)(2,1)S(1)} %all-to-all-done.gathered_ref, bf16[2048,512]{1,0:T(8,128)(2,1)S(1)} %bitcast.13, bf16[2048,128]{1,0:T(8,128)(2,1)S(1)} %bitcast.16), custom_call_target="tpu_custom_call" | custom-call | tf_op jit(solution)/shard_map/project/pallas_call | solution.py:40
  62.6 0.0 copy-start.3
  62.6 0.0 collective-permute-done.refs_1_
  62.6 0.0 collective-permute-done.1.refs_2_
  62.6 2.4 %collective-permute-done.2.refs_3_ = bf16[2,2,2,256,128]{4,3,2,1,0:T(8,128)(2,1)} collective-permute-done((bf16[2,2,2,256,128]{4,3,2,1,0:T(8,128)(2,1)}, bf16[2,2,2,256,128]{4,3,2,1,0:T(8,128)(2,1)}, u32[]{:S(2)}, u32[]{:S(2)}) %collective-permute-start.2) | collective-permute-done | bytes 524320 | tf_op jit(solution)/shard_map/ppermute | solution.py:176
  65.1 3.5 %collective-permute-start.3 = (bf16[16,16,640]{2,1,0:T(8,128)(2,1)S(1)}, bf16[16,16,640]{2,1,0:T(8,128)(2,1)S(1)}, u32[]{:S(2)}, u32[]{:S(2)}) collective-permute-start(bf16[16,16,640]{2,1,0:T(8,128)(2,1)S(1)} %get-tuple-element.25), channel_id=1, source_target_pairs={{0,16},{16,0},{1,17},{17,1},{2,18},{18,2},{3,19},{19,3},{4,20},{20... | collective-permute-start | bytes 983048 | tf_op jit(solution)/shard_map/ppermute | solution.py:179
  68.6 1.2 %collective-permute-done.3 = bf16[16,16,640]{2,1,0:T(8,128)(2,1)S(1)} collective-permute-done((bf16[16,16,640]{2,1,0:T(8,128)(2,1)S(1)}, bf16[16,16,640]{2,1,0:T(8,128)(2,1)S(1)}, u32[]{:S(2)}, u32[]{:S(2)}) %collective-permute-start.3) | collective-permute-done | bytes 327712 | tf_op jit(solution)/shard_map/ppermute | solution.py:179
  69.8 0.8 add_convert_fusion
  70.6 6.8 %all-to-all-start.1 = ((bf16[16,16,640]{2,1,0:T(8,128)(2,1)}), bf16[16,16,640]{2,1,0:T(8,128)(2,1)S(1)}, u32[]{:S(2)}, u32[]{:S(2)}) async-start(bf16[16,16,640]{2,1,0:T(8,128)(2,1)} %add_convert_fusion), calls=%async_computation.1 | async-start | bytes 655360 | tf_op jit(solution)/shard_map/all_to_all | solution.py:181
  77.5 7.2 %psum.7 = f32[32]{0:T(128)S(1)} all-reduce(f32[32]{0:T(128)S(1)} %get-tuple-element.27), channel_id=1, replica_groups=mesh['z'=8,'xh'=2,'co'=2,'xl'=2,'y'=8] {'xh','co'}, use_global_device_ids=true, to_apply=%region_1.0 | all-reduce | flops 32 | bytes 256 | tf_op jit(solution)/shard_map/psum | solution.py:182
  84.7 3.0 %all-to-all-done.1.both_ref = bf16[16,16,640]{2,1,0:T(8,128)(2,1)S(1)} async-done(((bf16[16,16,640]{2,1,0:T(8,128)(2,1)}), bf16[16,16,640]{2,1,0:T(8,128)(2,1)S(1)}, u32[]{:S(2)}, u32[]{:S(2)}) %all-to-all-start.1) | async-done | bytes 327712 | tf_op jit(solution)/shard_map/all_to_all | solution.py:181
  87.7 0.8 arrange.1
  88.5 5.6 %all-to-all-start.2 = ((bf16[4,4,16,1024]{3,2,1,0:T(8,128)(2,1)}), bf16[4,4,16,1024]{3,2,1,0:T(8,128)(2,1)S(1)}, u32[]{:S(2)}, u32[]{:S(2)}) async-start(bf16[4,4,16,1024]{3,2,1,0:T(8,128)(2,1)} %arrange.1), calls=%async_computation.2 | async-start | bytes 1048576 | tf_op jit(solution)/shard_map/all_to_all | solution.py:184
  94.1 0.1 copy.8.scale_ref
  94.2 9.4 %all-to-all-done.2 = bf16[4,4,16,1024]{3,2,1,0:T(8,128)(2,1)S(1)} async-done(((bf16[4,4,16,1024]{3,2,1,0:T(8,128)(2,1)}), bf16[4,4,16,1024]{3,2,1,0:T(8,128)(2,1)S(1)}, u32[]{:S(2)}, u32[]{:S(2)}) %all-to-all-start.2) | async-done | bytes 524320 | tf_op jit(solution)/shard_map/all_to_all | solution.py:184
  103.6 0.0 copy-done.3
  103.6 2.9 %attend.1 = (bf16[32,2048]{1,0:T(8,128)(2,1)S(1)}, bf16[32,2048]{1,0:T(8,128)(2,1)}) custom-call(s32[1,2]{1,0:T(1,128)S(1)} %copy-done.3, s32[1]{0:T(128)} %bitcast.place_ref, bf16[2,2,4,16,1024]{4,3,2,1,0:T(8,128)(2,1)S(1)} %bitcast.14, f32[32,1]{1,0:T(8,128)S(1)} %copy.8.scale_ref, bf16[2,2,2,256,128]{4,3,2,1,0:T(8,128)(2,1)S(1)} %get-tuple-element.30.refs_0_, ...), custom_call_target="tpu_custom_call" | custom-call | tf_op jit(solution)/shard_map/attend/pallas_call | solution.py:153
  106.5 3.8 %collective-permute-start.4 = (bf16[1,32,2048]{2,1,0:T(8,128)(2,1)S(1)}, bf16[1,32,2048]{2,1,0:T(8,128)(2,1)S(1)}, u32[]{:S(2)}, u32[]{:S(2)}) collective-permute-start(bf16[1,32,2048]{2,1,0:T(8,128)(2,1)S(1)} %bitcast.17), channel_id=1, source_target_pairs={{448,0},{0,64},{64,128},{128,192},{192,256},{256,320},{320,384},{3... | collective-permute-start | bytes 393224 | tf_op jit(solution)/shard_map/ppermute | solution.py:190
  110.3 9.6 %collective-permute-done.4 = bf16[1,32,2048]{2,1,0:T(8,128)(2,1)S(1)} collective-permute-done((bf16[1,32,2048]{2,1,0:T(8,128)(2,1)S(1)}, bf16[1,32,2048]{2,1,0:T(8,128)(2,1)S(1)}, u32[]{:S(2)}, u32[]{:S(2)}) %collective-permute-start.4) | collective-permute-done | bytes 131104 | tf_op jit(solution)/shard_map/ppermute | solution.py:190
  119.9 0.7 copy.10
  (1 shorter events, 0.0 us)
Async XLA Ops:
  3.3 55.4 %copy-start.2 = (bf16[1,2048,128]{2,1,0:T(8,128)(2,1)S(1)}, bf16[1,2048,128]{2,1,0:T(8,128)(2,1)}, u32[]{:S(2)}) copy-start(bf16[1,2048,128]{2,1,0:T(8,128)(2,1)} %param.9) | copy-start | bytes 1572868
  3.3 55.4 %all-to-all-start = ((bf16[16,32,2048]{2,1,0:T(8,128)(2,1)}), bf16[16,32,2048]{2,1,0:T(8,128)(2,1)S(1)}, u32[]{:S(2)}, u32[]{:S(2)}) async-start(bf16[16,32,2048]{2,1,0:T(8,128)(2,1)} %broadcast_in_dim.27), calls=%async_computation | async-start | bytes 4194304 | tf_op jit(solution)/shard_map/all_to_all | solution.py:173
  12.1 1.6 %copy-start.1 = (bf16[1,2,256,2,1024]{4,3,2,1,0:T(2,128)(2,1)S(1)}, bf16[1,2,256,2,1024]{4,3,2,1,0:T(2,128)(2,1)}, u32[]{:S(2)}) copy-start(bf16[1,2,256,2,1024]{4,3,2,1,0:T(2,128)(2,1)} %param.10) | copy-start | bytes 6291460
  18.7 43.9 %collective-permute-start = (bf16[2,2,2,256,128]{4,3,2,1,0:T(8,128)(2,1)}, bf16[2,2,2,256,128]{4,3,2,1,0:T(8,128)(2,1)}, u32[]{:S(2)}, u32[]{:S(2)}) collective-permute-start(bf16[2,2,2,256,128]{4,3,2,1,0:T(8,128)(2,1)} %get-tuple-element.22), channel_id=1, source_target_pairs={{0,16},{16,0},{32,48},{48,32},{1,17},{17,1},{33,49},{49,33},{2,18}... | collective-permute-start | bytes 1572872 | tf_op jit(solution)/shard_map/ppermute | solution.py:176
  22.5 40.1 %collective-permute-start.1 = (bf16[2,2,2,256,128]{4,3,2,1,0:T(8,128)(2,1)}, bf16[2,2,2,256,128]{4,3,2,1,0:T(8,128)(2,1)}, u32[]{:S(2)}, u32[]{:S(2)}) collective-permute-start(bf16[2,2,2,256,128]{4,3,2,1,0:T(8,128)(2,1)} %get-tuple-element.23), channel_id=1, source_target_pairs={{0,32},{16,48},{32,0},{48,16},{1,33},{17,49},{33,1},{49,17},{2,34}... | collective-permute-start | bytes 1572872 | tf_op jit(solution)/shard_map/ppermute | solution.py:176
  25.9 39.1 %collective-permute-start.2 = (bf16[2,2,2,256,128]{4,3,2,1,0:T(8,128)(2,1)}, bf16[2,2,2,256,128]{4,3,2,1,0:T(8,128)(2,1)}, u32[]{:S(2)}, u32[]{:S(2)}) collective-permute-start(bf16[2,2,2,256,128]{4,3,2,1,0:T(8,128)(2,1)} %get-tuple-element.24), channel_id=1, source_target_pairs={{0,48},{16,32},{32,16},{48,0},{1,49},{17,33},{33,17},{49,1},{2,50}... | collective-permute-start | bytes 1572872 | tf_op jit(solution)/shard_map/ppermute | solution.py:176
  58.7 1.6 %copy-start = (bf16[1,2048,512]{2,1,0:T(8,128)(2,1)S(1)}, bf16[1,2048,512]{2,1,0:T(8,128)(2,1)}, u32[]{:S(2)}) copy-start(bf16[1,2048,512]{2,1,0:T(8,128)(2,1)} %param.8) | copy-start | bytes 6291460
  62.6 41.0 %copy-start.3 = (s32[1,2]{1,0:T(1,128)S(1)}, s32[1,2]{1,0:T(1,128)}, u32[]{:S(2)}) copy-start(s32[1,2]{1,0:T(1,128)} %lengths_ref.1) | copy-start | bytes 28
  65.1 4.8 %collective-permute-start.3 = (bf16[16,16,640]{2,1,0:T(8,128)(2,1)S(1)}, bf16[16,16,640]{2,1,0:T(8,128)(2,1)S(1)}, u32[]{:S(2)}, u32[]{:S(2)}) collective-permute-start(bf16[16,16,640]{2,1,0:T(8,128)(2,1)S(1)} %get-tuple-element.25), channel_id=1, source_target_pairs={{0,16},{16,0},{1,17},{17,1},{2,18},{18,2},{3,19},{19,3},{4,20},{20... | collective-permute-start | bytes 983048 | tf_op jit(solution)/shard_map/ppermute | solution.py:179
  70.6 17.0 %all-to-all-start.1 = ((bf16[16,16,640]{2,1,0:T(8,128)(2,1)}), bf16[16,16,640]{2,1,0:T(8,128)(2,1)S(1)}, u32[]{:S(2)}, u32[]{:S(2)}) async-start(bf16[16,16,640]{2,1,0:T(8,128)(2,1)} %add_convert_fusion), calls=%async_computation.1 | async-start | bytes 655360 | tf_op jit(solution)/shard_map/all_to_all | solution.py:181
  88.5 15.0 %all-to-all-start.2 = ((bf16[4,4,16,1024]{3,2,1,0:T(8,128)(2,1)}), bf16[4,4,16,1024]{3,2,1,0:T(8,128)(2,1)S(1)}, u32[]{:S(2)}, u32[]{:S(2)}) async-start(bf16[4,4,16,1024]{3,2,1,0:T(8,128)(2,1)} %arrange.1), calls=%async_computation.2 | async-start | bytes 1048576 | tf_op jit(solution)/shard_map/all_to_all | solution.py:184
  106.5 13.4 %collective-permute-start.4 = (bf16[1,32,2048]{2,1,0:T(8,128)(2,1)S(1)}, bf16[1,32,2048]{2,1,0:T(8,128)(2,1)S(1)}, u32[]{:S(2)}, u32[]{:S(2)}) collective-permute-start(bf16[1,32,2048]{2,1,0:T(8,128)(2,1)S(1)} %bitcast.17), channel_id=1, source_target_pairs={{448,0},{0,64},{64,128},{128,192},{192,256},{256,320},{320,384},{3... | collective-permute-start | bytes 393224 | tf_op jit(solution)/shard_map/ppermute | solution.py:190

commit v10 on v9

--- a/solution.py
+++ b/solution.py
@@ -15,6 +15,7 @@
 F32 = jnp.float32
 VMEM = pl.BlockSpec(memory_space=pltpu.VMEM)
 SMEM = pl.BlockSpec(memory_space=pltpu.SMEM)
+MOST = pltpu.CompilerParams(vmem_limit_bytes=59 * 1024 * 1024)
 PARAMS = pltpu.CompilerParams(vmem_limit_bytes=32 * 1024 * 1024)
 
 
@@ -65,7 +66,7 @@
         out_shape=[jax.ShapeDtypeStruct((prompts, 2, 2, chunk, HEAD_DIM), BF)] * len(places),
         in_specs=[SMEM, pl.BlockSpec((1,) + cache.shape[1:], lambda p: (p, 0, 0, 0))],
         out_specs=[block] * len(places),
-        compiler_params=PARAMS,
+        compiler_params=MOST,
         name="pick",
     )(place, cache)
 
@@ -172,10 +173,11 @@
     count = 16
     gathered = lax.all_to_all(jnp.broadcast_to(sent[None], (count, rows, width)), COL, 0, 0)
     caches = list(pick((0, 1, 2, 3), row_index[None], kv_cache[0]))
-    for k in range(1, row_count):
+    for k in (2, 3, 1):
         caches[k] = lax.ppermute(caches[k], ROW, [(i, i ^ k) for i in range(row_count)])
     keep, send = project(lax.axis_index("co")[None], gathered, q_weight[0], kv_weight[0])
-    send, caches = lax.optimization_barrier((send, caches))
+    send, *moved = lax.optimization_barrier((send, caches[0], caches[2], caches[3], caches[1]))
+    caches = [moved[0], moved[3], moved[1], moved[2]]
     both = (keep.astype(F32) + lax.ppermute(send, "co", swap).astype(F32)).astype(BF)
     both, local_squares = lax.optimization_barrier((both, local_squares))
     both = lax.all_to_all(both, COL, 0, 0)

time: 121 us -> 120 us (level)
  waiting for transfers between devices: 54.9 us -> 52.4 us
  Pallas kernels: 11.1 us -> 12.7 us
  local copies, waits for them, and re-layouts: 5.52 us -> 3.94 us
    ppermute x1, starting transfers between devices: 3.53 us -> 6.09 us  [shards(): lax.ppermute(send, 'co', swap).astype(F32)]
    ppermute x3, waiting for transfers between devices: 2.44 us -> 0.01 us  [shards(): lax.ppermute(caches[k], ROW, [(i, i ^ k) for i in range(row_count)])]
    all_to_all x1, starting transfers between devices: 6.85 us -> 4.65 us  [shards(): both = lax.all_to_all(both, COL, 0, 0)]
    pallas_call x1, Pallas kernels: 5.01 us -> 6.74 us  [pick(): pl.pallas_call(pick_kernel, grid=(prompts,), out_shape=[jax.ShapeDtypeStr...]
    unnamed x9, local copies, waits for them, and re-layouts: 3.84 us -> 2.26 us
  transfers between devices with their start and end apart: 8 -> 8, of which waited for: 6 -> 5; matrix products, arithmetic and copies ran while one was open for 0% -> 0% of each run, Pallas kernels for 6% -> 8%
where the time goes in v10:
time: 120 us; the launch traced here: 119 us
  waiting for transfers between devices  52.4 us (44%)
  starting transfers between devices  40.3 us (34%)
  Pallas kernels  12.7 us (11%)
  blocking collectives  7.05 us (6%)
  local copies, waits for them, and re-layouts  3.94 us (3%)
  other arithmetic  1.86 us (2%)
    all_to_all x1, waiting for transfers between devices, shards(): lax.all_to_all(jnp.broadcast_to(sent[None], (count, rows, width)), COL, 0...  29 us
    ppermute x3, starting transfers between devices, shards(): lax.ppermute(caches[k], ROW, [(i, i ^ k) for i in range(row_count)])  10.8 us
    ppermute x1, waiting for transfers between devices, shards(): lax.ppermute(attended[None], 'z', [((i - 1) % count, i) for i in range(co...  9.65 us
    all_to_all x1, waiting for transfers between devices, shards(): parts = lax.all_to_all(arrange(both), ROW, 0, 0)  9.39 us
    all_to_all x1, starting transfers between devices, shards(): lax.all_to_all(jnp.broadcast_to(sent[None], (count, rows, width)), COL, 0...  8.68 us
    psum x1, blocking collectives, shards(): squares = lax.psum(local_squares, ROW)  7.05 us
    pallas_call x1, Pallas kernels, pick(): pl.pallas_call(pick_kernel, grid=(prompts,), out_shape=[jax.ShapeDtypeStr...  6.74 us
    all_to_all x1, starting transfers between devices, shards(): parts = lax.all_to_all(arrange(both), ROW, 0, 0)  6.14 us
  transfers between devices with their start and end apart: 8, of which 5 were waited for; matrix products, arithmetic and copies ran while one was open for 0% of the time, Pallas kernels for 8%

profile of v10, /device:TPU:1, one launch (start us, length us, event | category | flops | bytes accessed | tf_op | source)
XLA Modules:
  0.0 119.1 jit_solution(7957954786176632317)
XLA Ops:
  0.6 1.1 fusion.1
  1.7 1.6 %broadcast_in_dim.27 = bf16[16,32,2048]{2,1,0:T(8,128)(2,1)} broadcast(bf16[32,2048]{1,0:T(8,128)(2,1)S(1)} %get-tuple-element.37), dimensions={1,2} | broadcast | bytes 2228224 | tf_op jit(solution)/shard_map/broadcast_in_dim | solution.py:174
  3.3 8.7 %all-to-all-start = ((bf16[16,32,2048]{2,1,0:T(8,128)(2,1)}), bf16[16,32,2048]{2,1,0:T(8,128)(2,1)S(1)}, u32[]{:S(2)}, u32[]{:S(2)}) async-start(bf16[16,32,2048]{2,1,0:T(8,128)(2,1)} %broadcast_in_dim.27), calls=%async_computation | async-start | bytes 4194304 | tf_op jit(solution)/shard_map/all_to_all | solution.py:174
  12.0 0.0 copy-start.1
  12.0 6.7 %pick.1 = (bf16[2,2,2,256,128]{4,3,2,1,0:T(8,128)(2,1)}, bf16[2,2,2,256,128]{4,3,2,1,0:T(8,128)(2,1)}, bf16[2,2,2,256,128]{4,3,2,1,0:T(8,128)(2,1)}, bf16[2,2,2,256,128]{4,3,2,1,0:T(8,128)(2,1)}) custom-call(s32[1]{0:T(128)} %bitcast.place_ref, bf16[2,256,2,1024]{3,2,1,0:T(2,128)(2,1)} %bitcast.17), custom_call_target="tpu_custom_call" | custom-call | tf_op jit(solution)/shard_map/pick/pallas_call | solution.py:63
  18.7 4.3 %collective-permute-start = (bf16[2,2,2,256,128]{4,3,2,1,0:T(8,128)(2,1)}, bf16[2,2,2,256,128]{4,3,2,1,0:T(8,128)(2,1)S(1)}, u32[]{:S(2)}, u32[]{:S(2)}) collective-permute-start(bf16[2,2,2,256,128]{4,3,2,1,0:T(8,128)(2,1)} %get-tuple-element.22), channel_id=1, source_target_pairs={{0,32},{16,48},{32,0},{48,16},{1,33},{17,49},{33,1},{49,17},{2,34}... | collective-permute-start | bytes 1572872 | tf_op jit(solution)/shard_map/ppermute | solution.py:177
  23.1 4.5 %collective-permute-start.1 = (bf16[2,2,2,256,128]{4,3,2,1,0:T(8,128)(2,1)}, bf16[2,2,2,256,128]{4,3,2,1,0:T(8,128)(2,1)}, u32[]{:S(2)}, u32[]{:S(2)}) collective-permute-start(bf16[2,2,2,256,128]{4,3,2,1,0:T(8,128)(2,1)} %get-tuple-element.23), channel_id=1, source_target_pairs={{0,48},{16,32},{32,16},{48,0},{1,49},{17,33},{33,17},{49,1},{2,50}... | collective-permute-start | bytes 1572872 | tf_op jit(solution)/shard_map/ppermute | solution.py:177
  27.6 1.9 %collective-permute-start.2 = (bf16[2,2,2,256,128]{4,3,2,1,0:T(8,128)(2,1)}, bf16[2,2,2,256,128]{4,3,2,1,0:T(8,128)(2,1)}, u32[]{:S(2)}, u32[]{:S(2)}) collective-permute-start(bf16[2,2,2,256,128]{4,3,2,1,0:T(8,128)(2,1)} %get-tuple-element.24), channel_id=1, source_target_pairs={{0,16},{16,0},{32,48},{48,32},{1,17},{17,1},{33,49},{49,33},{2,18}... | collective-permute-start | bytes 1572872 | tf_op jit(solution)/shard_map/ppermute | solution.py:177
  29.5 29.0 %all-to-all-done.gathered_ref = bf16[16,32,2048]{2,1,0:T(8,128)(2,1)S(1)} async-done(((bf16[16,32,2048]{2,1,0:T(8,128)(2,1)}), bf16[16,32,2048]{2,1,0:T(8,128)(2,1)S(1)}, u32[]{:S(2)}, u32[]{:S(2)}) %all-to-all-start) | async-done | bytes 2097184 | tf_op jit(solution)/shard_map/all_to_all | solution.py:174
  58.5 0.0 copy-done.1
  58.5 0.0 copy-start
  58.5 1.6 %copy-done = bf16[1,2048,512]{2,1,0:T(8,128)(2,1)S(1)} copy-done((bf16[1,2048,512]{2,1,0:T(8,128)(2,1)S(1)}, bf16[1,2048,512]{2,1,0:T(8,128)(2,1)}, u32[]{:S(2)}) %copy-start) | copy-done | bytes 2097176
  60.1 2.3 %project.1 = (bf16[16,16,640]{2,1,0:T(8,128)(2,1)S(1)}, bf16[16,16,640]{2,1,0:T(8,128)(2,1)S(1)}) custom-call(s32[1]{0:T(128)} %bitcast.1.place_ref, bf16[16,32,2048]{2,1,0:T(8,128)(2,1)S(1)} %all-to-all-done.gathered_ref, bf16[2048,512]{1,0:T(8,128)(2,1)S(1)} %bitcast.13, bf16[2048,128]{1,0:T(8,128)(2,1)S(1)} %bitcast.15), custom_call_target="tpu_custom_call" | custom-call | tf_op jit(solution)/shard_map/project/pallas_call | solution.py:41
  62.5 0.0 copy-start.2
  62.5 0.0 copy-start.3
  62.5 0.0 collective-permute-done.refs_2_
  62.5 0.0 collective-permute-done.1.refs_3_
  62.5 0.0 collective-permute-done.2.refs_1_
  62.5 6.1 %collective-permute-start.3 = (bf16[16,16,640]{2,1,0:T(8,128)(2,1)S(1)}, bf16[16,16,640]{2,1,0:T(8,128)(2,1)S(1)}, u32[]{:S(2)}, u32[]{:S(2)}) collective-permute-start(bf16[16,16,640]{2,1,0:T(8,128)(2,1)S(1)} %get-tuple-element.25), channel_id=1, source_target_pairs={{0,16},{16,0},{1,17},{17,1},{2,18},{18,2},{3,19},{19,3},{4,20},{20... | collective-permute-start | bytes 983048 | tf_op jit(solution)/shard_map/ppermute | solution.py:181
  68.6 1.2 %collective-permute-done.3 = bf16[16,16,640]{2,1,0:T(8,128)(2,1)S(1)} collective-permute-done((bf16[16,16,640]{2,1,0:T(8,128)(2,1)S(1)}, bf16[16,16,640]{2,1,0:T(8,128)(2,1)S(1)}, u32[]{:S(2)}, u32[]{:S(2)}) %collective-permute-start.3) | collective-permute-done | bytes 327712 | tf_op jit(solution)/shard_map/ppermute | solution.py:181
  69.8 0.8 add_convert_fusion
  70.6 4.7 %all-to-all-start.1 = ((bf16[16,16,640]{2,1,0:T(8,128)(2,1)}), bf16[16,16,640]{2,1,0:T(8,128)(2,1)S(1)}, u32[]{:S(2)}, u32[]{:S(2)}) async-start(bf16[16,16,640]{2,1,0:T(8,128)(2,1)} %add_convert_fusion), calls=%async_computation.1 | async-start | bytes 655360 | tf_op jit(solution)/shard_map/all_to_all | solution.py:183
  75.3 7.1 %psum.7 = f32[32]{0:T(128)S(1)} all-reduce(f32[32]{0:T(128)S(1)} %get-tuple-element.27), channel_id=1, replica_groups=mesh['z'=8,'xh'=2,'co'=2,'xl'=2,'y'=8] {'xh','co'}, use_global_device_ids=true, to_apply=%region_1.0 | all-reduce | flops 32 | bytes 256 | tf_op jit(solution)/shard_map/psum | solution.py:184
  82.4 3.1 %all-to-all-done.1.both_ref = bf16[16,16,640]{2,1,0:T(8,128)(2,1)S(1)} async-done(((bf16[16,16,640]{2,1,0:T(8,128)(2,1)}), bf16[16,16,640]{2,1,0:T(8,128)(2,1)S(1)}, u32[]{:S(2)}, u32[]{:S(2)}) %all-to-all-start.1) | async-done | bytes 327712 | tf_op jit(solution)/shard_map/all_to_all | solution.py:183
  85.5 0.8 arrange.1
  86.3 6.1 %all-to-all-start.2 = ((bf16[4,4,16,1024]{3,2,1,0:T(8,128)(2,1)}), bf16[4,4,16,1024]{3,2,1,0:T(8,128)(2,1)S(1)}, u32[]{:S(2)}, u32[]{:S(2)}) async-start(bf16[4,4,16,1024]{3,2,1,0:T(8,128)(2,1)} %arrange.1), calls=%async_computation.2 | async-start | bytes 1048576 | tf_op jit(solution)/shard_map/all_to_all | solution.py:186
  92.5 0.1 copy.8.scale_ref
  92.6 9.4 %all-to-all-done.2 = bf16[4,4,16,1024]{3,2,1,0:T(8,128)(2,1)S(1)} async-done(((bf16[4,4,16,1024]{3,2,1,0:T(8,128)(2,1)}), bf16[4,4,16,1024]{3,2,1,0:T(8,128)(2,1)S(1)}, u32[]{:S(2)}, u32[]{:S(2)}) %all-to-all-start.2) | async-done | bytes 524320 | tf_op jit(solution)/shard_map/all_to_all | solution.py:186
  102.0 0.0 copy-done.2
  102.0 0.0 copy-done.3
  102.0 2.8 %attend.1 = (bf16[32,2048]{1,0:T(8,128)(2,1)S(1)}, bf16[32,2048]{1,0:T(8,128)(2,1)}) custom-call(s32[1,2]{1,0:T(1,128)S(1)} %copy-done.3, s32[1]{0:T(128)} %bitcast.place_ref, bf16[2,2,4,16,1024]{4,3,2,1,0:T(8,128)(2,1)S(1)} %bitcast.14, f32[32,1]{1,0:T(8,128)S(1)} %copy.8.scale_ref, bf16[2,2,2,256,128]{4,3,2,1,0:T(8,128)(2,1)S(1)} %copy-done.2, ...), custom_call_target="tpu_custom_call" | custom-call | tf_op jit(solution)/shard_map/attend/pallas_call | solution.py:154
  104.8 4.0 %collective-permute-start.4 = (bf16[1,32,2048]{2,1,0:T(8,128)(2,1)S(1)}, bf16[1,32,2048]{2,1,0:T(8,128)(2,1)S(1)}, u32[]{:S(2)}, u32[]{:S(2)}) collective-permute-start(bf16[1,32,2048]{2,1,0:T(8,128)(2,1)S(1)} %bitcast.16), channel_id=1, source_target_pairs={{448,0},{0,64},{64,128},{128,192},{192,256},{256,320},{320,384},{3... | collective-permute-start | bytes 393224 | tf_op jit(solution)/shard_map/ppermute | solution.py:192
  108.8 9.6 %collective-permute-done.4 = bf16[1,32,2048]{2,1,0:T(8,128)(2,1)S(1)} collective-permute-done((bf16[1,32,2048]{2,1,0:T(8,128)(2,1)S(1)}, bf16[1,32,2048]{2,1,0:T(8,128)(2,1)S(1)}, u32[]{:S(2)}, u32[]{:S(2)}) %collective-permute-start.4) | collective-permute-done | bytes 131104 | tf_op jit(solution)/shard_map/ppermute | solution.py:192
  118.4 0.7 copy.10
  (1 shorter events, 0.0 us)
Async XLA Ops:
  3.3 55.3 %all-to-all-start = ((bf16[16,32,2048]{2,1,0:T(8,128)(2,1)}), bf16[16,32,2048]{2,1,0:T(8,128)(2,1)S(1)}, u32[]{:S(2)}, u32[]{:S(2)}) async-start(bf16[16,32,2048]{2,1,0:T(8,128)(2,1)} %broadcast_in_dim.27), calls=%async_computation | async-start | bytes 4194304 | tf_op jit(solution)/shard_map/all_to_all | solution.py:174
  12.0 46.6 %copy-start.1 = (bf16[1,2048,128]{2,1,0:T(8,128)(2,1)S(1)}, bf16[1,2048,128]{2,1,0:T(8,128)(2,1)}, u32[]{:S(2)}) copy-start(bf16[1,2048,128]{2,1,0:T(8,128)(2,1)} %param.9) | copy-start | bytes 1572868
  18.7 43.8 %collective-permute-start = (bf16[2,2,2,256,128]{4,3,2,1,0:T(8,128)(2,1)}, bf16[2,2,2,256,128]{4,3,2,1,0:T(8,128)(2,1)S(1)}, u32[]{:S(2)}, u32[]{:S(2)}) collective-permute-start(bf16[2,2,2,256,128]{4,3,2,1,0:T(8,128)(2,1)} %get-tuple-element.22), channel_id=1, source_target_pairs={{0,32},{16,48},{32,0},{48,16},{1,33},{17,49},{33,1},{49,17},{2,34}... | collective-permute-start | bytes 1572872 | tf_op jit(solution)/shard_map/ppermute | solution.py:177
  23.1 39.4 %collective-permute-start.1 = (bf16[2,2,2,256,128]{4,3,2,1,0:T(8,128)(2,1)}, bf16[2,2,2,256,128]{4,3,2,1,0:T(8,128)(2,1)}, u32[]{:S(2)}, u32[]{:S(2)}) collective-permute-start(bf16[2,2,2,256,128]{4,3,2,1,0:T(8,128)(2,1)} %get-tuple-element.23), channel_id=1, source_target_pairs={{0,48},{16,32},{32,16},{48,0},{1,49},{17,33},{33,17},{49,1},{2,50}... | collective-permute-start | bytes 1572872 | tf_op jit(solution)/shard_map/ppermute | solution.py:177
  27.6 34.9 %collective-permute-start.2 = (bf16[2,2,2,256,128]{4,3,2,1,0:T(8,128)(2,1)}, bf16[2,2,2,256,128]{4,3,2,1,0:T(8,128)(2,1)}, u32[]{:S(2)}, u32[]{:S(2)}) collective-permute-start(bf16[2,2,2,256,128]{4,3,2,1,0:T(8,128)(2,1)} %get-tuple-element.24), channel_id=1, source_target_pairs={{0,16},{16,0},{32,48},{48,32},{1,17},{17,1},{33,49},{49,33},{2,18}... | collective-permute-start | bytes 1572872 | tf_op jit(solution)/shard_map/ppermute | solution.py:177
  58.5 1.6 %copy-start = (bf16[1,2048,512]{2,1,0:T(8,128)(2,1)S(1)}, bf16[1,2048,512]{2,1,0:T(8,128)(2,1)}, u32[]{:S(2)}) copy-start(bf16[1,2048,512]{2,1,0:T(8,128)(2,1)} %param.8) | copy-start | bytes 6291460
  62.5 39.5 %copy-start.2 = (bf16[2,2,2,256,128]{4,3,2,1,0:T(8,128)(2,1)S(1)}, bf16[2,2,2,256,128]{4,3,2,1,0:T(8,128)(2,1)}, u32[]{:S(2)}) copy-start(bf16[2,2,2,256,128]{4,3,2,1,0:T(8,128)(2,1)} %get-tuple-element.30.refs_0_) | copy-start | bytes 1572868
  62.5 39.5 %copy-start.3 = (s32[1,2]{1,0:T(1,128)S(1)}, s32[1,2]{1,0:T(1,128)}, u32[]{:S(2)}) copy-start(s32[1,2]{1,0:T(1,128)} %lengths_ref.1) | copy-start | bytes 28
  62.5 7.3 %collective-permute-start.3 = (bf16[16,16,640]{2,1,0:T(8,128)(2,1)S(1)}, bf16[16,16,640]{2,1,0:T(8,128)(2,1)S(1)}, u32[]{:S(2)}, u32[]{:S(2)}) collective-permute-start(bf16[16,16,640]{2,1,0:T(8,128)(2,1)S(1)} %get-tuple-element.25), channel_id=1, source_target_pairs={{0,16},{16,0},{1,17},{17,1},{2,18},{18,2},{3,19},{19,3},{4,20},{20... | collective-permute-start | bytes 983048 | tf_op jit(solution)/shard_map/ppermute | solution.py:181
  70.6 14.9 %all-to-all-start.1 = ((bf16[16,16,640]{2,1,0:T(8,128)(2,1)}), bf16[16,16,640]{2,1,0:T(8,128)(2,1)S(1)}, u32[]{:S(2)}, u32[]{:S(2)}) async-start(bf16[16,16,640]{2,1,0:T(8,128)(2,1)} %add_convert_fusion), calls=%async_computation.1 | async-start | bytes 655360 | tf_op jit(solution)/shard_map/all_to_all | solution.py:183
  86.3 15.6 %all-to-all-start.2 = ((bf16[4,4,16,1024]{3,2,1,0:T(8,128)(2,1)}), bf16[4,4,16,1024]{3,2,1,0:T(8,128)(2,1)S(1)}, u32[]{:S(2)}, u32[]{:S(2)}) async-start(bf16[4,4,16,1024]{3,2,1,0:T(8,128)(2,1)} %arrange.1), calls=%async_computation.2 | async-start | bytes 1048576 | tf_op jit(solution)/shard_map/all_to_all | solution.py:186
  104.8 13.7 %collective-permute-start.4 = (bf16[1,32,2048]{2,1,0:T(8,128)(2,1)S(1)}, bf16[1,32,2048]{2,1,0:T(8,128)(2,1)S(1)}, u32[]{:S(2)}, u32[]{:S(2)}) collective-permute-start(bf16[1,32,2048]{2,1,0:T(8,128)(2,1)S(1)} %bitcast.16), channel_id=1, source_target_pairs={{448,0},{0,64},{64,128},{128,192},{192,256},{256,320},{320,384},{3... | collective-permute-start | bytes 393224 | tf_op jit(solution)/shard_map/ppermute | solution.py:192

commit v11 on v10

--- a/solution.py
+++ b/solution.py
@@ -59,12 +59,13 @@
                 for v in range(2):
                     piece_ref[0, v, g] = block[:, v, :]
 
-    block = pl.BlockSpec((1, 2, 2, chunk, HEAD_DIM), lambda p: (p, 0, 0, 0, 0))
+    step = 64
+    block = pl.BlockSpec((1, 2, 2, step, HEAD_DIM), lambda p, i: (p, 0, 0, i, 0))
     return pl.pallas_call(
         pick_kernel,
-        grid=(prompts,),
+        grid=(prompts, chunk // step),
         out_shape=[jax.ShapeDtypeStruct((prompts, 2, 2, chunk, HEAD_DIM), BF)] * len(places),
-        in_specs=[SMEM, pl.BlockSpec((1,) + cache.shape[1:], lambda p: (p, 0, 0, 0))],
+        in_specs=[SMEM, pl.BlockSpec((1, step) + cache.shape[2:], lambda p, i: (p, i, 0, 0))],
         out_specs=[block] * len(places),
         compiler_params=MOST,
         name="pick",

time: 120 us -> 120 us (level)
  Pallas kernels: 12.7 us -> 13.9 us
    pallas_call x1, Pallas kernels: 6.74 us -> 7.99 us  [pick(): pl.pallas_call(pick_kernel, grid=(prompts, chunk // step), out_shape=[jax...]
    all_to_all x1, waiting for transfers between devices: 29 us -> 27.8 us  [shards(): lax.all_to_all(jnp.broadcast_to(sent[None], (count, rows, width)), COL, 0...]
  transfers between devices with their start and end apart: 8 -> 8, of which waited for: 5 -> 6; matrix products, arithmetic and copies ran while one was open for 0% -> 0% of each run, Pallas kernels for 8% -> 9%
where the time goes in v11:
time: 120 us; the launch traced here: 119 us
  waiting for transfers between devices  52 us (43%)
  starting transfers between devices  39.7 us (33%)
  Pallas kernels  13.9 us (12%)
  blocking collectives  6.96 us (6%)
  local copies, waits for them, and re-layouts  3.94 us (3%)
  other arithmetic  1.86 us (2%)
    all_to_all x1, waiting for transfers between devices, shards(): lax.all_to_all(jnp.broadcast_to(sent[None], (count, rows, width)), COL, 0...  27.8 us
    ppermute x3, starting transfers between devices, shards(): lax.ppermute(caches[k], ROW, [(i, i ^ k) for i in range(row_count)])  10.8 us
    ppermute x1, waiting for transfers between devices, shards(): lax.ppermute(attended[None], 'z', [((i - 1) % count, i) for i in range(co...  9.63 us
    all_to_all x1, waiting for transfers between devices, shards(): parts = lax.all_to_all(arrange(both), ROW, 0, 0)  9.39 us
    all_to_all x1, starting transfers between devices, shards(): lax.all_to_all(jnp.broadcast_to(sent[None], (count, rows, width)), COL, 0...  8.68 us
    pallas_call x1, Pallas kernels, pick(): pl.pallas_call(pick_kernel, grid=(prompts, chunk // step), out_shape=[jax...  7.99 us
    psum x1, blocking collectives, shards(): squares = lax.psum(local_squares, ROW)  6.96 us
    all_to_all x1, starting transfers between devices, shards(): parts = lax.all_to_all(arrange(both), ROW, 0, 0)  6.12 us
  transfers between devices with their start and end apart: 8, of which 6 were waited for; matrix products, arithmetic and copies ran while one was open for 0% of the time, Pallas kernels for 9%

profile of v11, /device:TPU:1, one launch (start us, length us, event | category | flops | bytes accessed | tf_op | source)
XLA Modules:
  0.0 119.2 jit_solution(5876968353926264418)
XLA Ops:
  0.6 1.1 fusion.1
  1.7 1.6 %broadcast_in_dim.27 = bf16[16,32,2048]{2,1,0:T(8,128)(2,1)} broadcast(bf16[32,2048]{1,0:T(8,128)(2,1)S(1)} %get-tuple-element.37), dimensions={1,2} | broadcast | bytes 2228224 | tf_op jit(solution)/shard_map/broadcast_in_dim | solution.py:175
  3.3 8.7 %all-to-all-start = ((bf16[16,32,2048]{2,1,0:T(8,128)(2,1)}), bf16[16,32,2048]{2,1,0:T(8,128)(2,1)S(1)}, u32[]{:S(2)}, u32[]{:S(2)}) async-start(bf16[16,32,2048]{2,1,0:T(8,128)(2,1)} %broadcast_in_dim.27), calls=%async_computation | async-start | bytes 4194304 | tf_op jit(solution)/shard_map/all_to_all | solution.py:175
  12.0 0.0 copy-start.1
  12.0 8.0 %pick.1 = (bf16[2,2,2,256,128]{4,3,2,1,0:T(8,128)(2,1)}, bf16[2,2,2,256,128]{4,3,2,1,0:T(8,128)(2,1)}, bf16[2,2,2,256,128]{4,3,2,1,0:T(8,128)(2,1)}, bf16[2,2,2,256,128]{4,3,2,1,0:T(8,128)(2,1)}) custom-call(s32[1]{0:T(128)} %bitcast.place_ref, bf16[2,256,2,1024]{3,2,1,0:T(2,128)(2,1)} %bitcast.17), custom_call_target="tpu_custom_call" | custom-call | tf_op jit(solution)/shard_map/pick/pallas_call | solution.py:64
  20.0 4.3 %collective-permute-start = (bf16[2,2,2,256,128]{4,3,2,1,0:T(8,128)(2,1)}, bf16[2,2,2,256,128]{4,3,2,1,0:T(8,128)(2,1)S(1)}, u32[]{:S(2)}, u32[]{:S(2)}) collective-permute-start(bf16[2,2,2,256,128]{4,3,2,1,0:T(8,128)(2,1)} %get-tuple-element.22), channel_id=1, source_target_pairs={{0,32},{16,48},{32,0},{48,16},{1,33},{17,49},{33,1},{49,17},{2,34}... | collective-permute-start | bytes 1572872 | tf_op jit(solution)/shard_map/ppermute | solution.py:178
  24.3 4.5 %collective-permute-start.1 = (bf16[2,2,2,256,128]{4,3,2,1,0:T(8,128)(2,1)}, bf16[2,2,2,256,128]{4,3,2,1,0:T(8,128)(2,1)}, u32[]{:S(2)}, u32[]{:S(2)}) collective-permute-start(bf16[2,2,2,256,128]{4,3,2,1,0:T(8,128)(2,1)} %get-tuple-element.23), channel_id=1, source_target_pairs={{0,48},{16,32},{32,16},{48,0},{1,49},{17,33},{33,17},{49,1},{2,50}... | collective-permute-start | bytes 1572872 | tf_op jit(solution)/shard_map/ppermute | solution.py:178
  28.8 1.9 %collective-permute-start.2 = (bf16[2,2,2,256,128]{4,3,2,1,0:T(8,128)(2,1)}, bf16[2,2,2,256,128]{4,3,2,1,0:T(8,128)(2,1)}, u32[]{:S(2)}, u32[]{:S(2)}) collective-permute-start(bf16[2,2,2,256,128]{4,3,2,1,0:T(8,128)(2,1)} %get-tuple-element.24), channel_id=1, source_target_pairs={{0,16},{16,0},{32,48},{48,32},{1,17},{17,1},{33,49},{49,33},{2,18}... | collective-permute-start | bytes 1572872 | tf_op jit(solution)/shard_map/ppermute | solution.py:178
  30.8 27.8 %all-to-all-done.gathered_ref = bf16[16,32,2048]{2,1,0:T(8,128)(2,1)S(1)} async-done(((bf16[16,32,2048]{2,1,0:T(8,128)(2,1)}), bf16[16,32,2048]{2,1,0:T(8,128)(2,1)S(1)}, u32[]{:S(2)}, u32[]{:S(2)}) %all-to-all-start) | async-done | bytes 2097184 | tf_op jit(solution)/shard_map/all_to_all | solution.py:175
  58.5 0.0 copy-done.1
  58.5 0.0 copy-start
  58.5 1.6 %copy-done = bf16[1,2048,512]{2,1,0:T(8,128)(2,1)S(1)} copy-done((bf16[1,2048,512]{2,1,0:T(8,128)(2,1)S(1)}, bf16[1,2048,512]{2,1,0:T(8,128)(2,1)}, u32[]{:S(2)}) %copy-start) | copy-done | bytes 2097176
  60.1 2.3 %project.1 = (bf16[16,16,640]{2,1,0:T(8,128)(2,1)S(1)}, bf16[16,16,640]{2,1,0:T(8,128)(2,1)S(1)}) custom-call(s32[1]{0:T(128)} %bitcast.1.place_ref, bf16[16,32,2048]{2,1,0:T(8,128)(2,1)S(1)} %all-to-all-done.gathered_ref, bf16[2048,512]{1,0:T(8,128)(2,1)S(1)} %bitcast.13, bf16[2048,128]{1,0:T(8,128)(2,1)S(1)} %bitcast.15), custom_call_target="tpu_custom_call" | custom-call | tf_op jit(solution)/shard_map/project/pallas_call | solution.py:41
  62.5 0.0 copy-start.2
  62.5 0.0 copy-start.3
  62.5 0.0 collective-permute-done.refs_2_
  62.5 0.8 collective-permute-done.1.refs_3_
  63.3 0.0 collective-permute-done.2.refs_1_
  63.3 5.3 %collective-permute-start.3 = (bf16[16,16,640]{2,1,0:T(8,128)(2,1)S(1)}, bf16[16,16,640]{2,1,0:T(8,128)(2,1)S(1)}, u32[]{:S(2)}, u32[]{:S(2)}) collective-permute-start(bf16[16,16,640]{2,1,0:T(8,128)(2,1)S(1)} %get-tuple-element.25), channel_id=1, source_target_pairs={{0,16},{16,0},{1,17},{17,1},{2,18},{18,2},{3,19},{19,3},{4,20},{20... | collective-permute-start | bytes 983048 | tf_op jit(solution)/shard_map/ppermute | solution.py:182
  68.6 1.2 %collective-permute-done.3 = bf16[16,16,640]{2,1,0:T(8,128)(2,1)S(1)} collective-permute-done((bf16[16,16,640]{2,1,0:T(8,128)(2,1)S(1)}, bf16[16,16,640]{2,1,0:T(8,128)(2,1)S(1)}, u32[]{:S(2)}, u32[]{:S(2)}) %collective-permute-start.3) | collective-permute-done | bytes 327712 | tf_op jit(solution)/shard_map/ppermute | solution.py:182
  69.8 0.8 add_convert_fusion
  70.7 5.5 %all-to-all-start.1 = ((bf16[16,16,640]{2,1,0:T(8,128)(2,1)}), bf16[16,16,640]{2,1,0:T(8,128)(2,1)S(1)}, u32[]{:S(2)}, u32[]{:S(2)}) async-start(bf16[16,16,640]{2,1,0:T(8,128)(2,1)} %add_convert_fusion), calls=%async_computation.1 | async-start | bytes 655360 | tf_op jit(solution)/shard_map/all_to_all | solution.py:184
  76.1 7.0 %psum.7 = f32[32]{0:T(128)S(1)} all-reduce(f32[32]{0:T(128)S(1)} %get-tuple-element.27), channel_id=1, replica_groups=mesh['z'=8,'xh'=2,'co'=2,'xl'=2,'y'=8] {'xh','co'}, use_global_device_ids=true, to_apply=%region_1.0 | all-reduce | flops 32 | bytes 256 | tf_op jit(solution)/shard_map/psum | solution.py:185
  83.1 3.2 %all-to-all-done.1.both_ref = bf16[16,16,640]{2,1,0:T(8,128)(2,1)S(1)} async-done(((bf16[16,16,640]{2,1,0:T(8,128)(2,1)}), bf16[16,16,640]{2,1,0:T(8,128)(2,1)S(1)}, u32[]{:S(2)}, u32[]{:S(2)}) %all-to-all-start.1) | async-done | bytes 327712 | tf_op jit(solution)/shard_map/all_to_all | solution.py:184
  86.3 0.8 arrange.1
  87.1 6.1 %all-to-all-start.2 = ((bf16[4,4,16,1024]{3,2,1,0:T(8,128)(2,1)}), bf16[4,4,16,1024]{3,2,1,0:T(8,128)(2,1)S(1)}, u32[]{:S(2)}, u32[]{:S(2)}) async-start(bf16[4,4,16,1024]{3,2,1,0:T(8,128)(2,1)} %arrange.1), calls=%async_computation.2 | async-start | bytes 1048576 | tf_op jit(solution)/shard_map/all_to_all | solution.py:187
  93.2 0.1 copy.8.scale_ref
  93.3 9.4 %all-to-all-done.2 = bf16[4,4,16,1024]{3,2,1,0:T(8,128)(2,1)S(1)} async-done(((bf16[4,4,16,1024]{3,2,1,0:T(8,128)(2,1)}), bf16[4,4,16,1024]{3,2,1,0:T(8,128)(2,1)S(1)}, u32[]{:S(2)}, u32[]{:S(2)}) %all-to-all-start.2) | async-done | bytes 524320 | tf_op jit(solution)/shard_map/all_to_all | solution.py:187
  102.7 0.0 copy-done.2
  102.7 0.0 copy-done.3
  102.7 2.8 %attend.1 = (bf16[32,2048]{1,0:T(8,128)(2,1)S(1)}, bf16[32,2048]{1,0:T(8,128)(2,1)}) custom-call(s32[1,2]{1,0:T(1,128)S(1)} %copy-done.3, s32[1]{0:T(128)} %bitcast.place_ref, bf16[2,2,4,16,1024]{4,3,2,1,0:T(8,128)(2,1)S(1)} %bitcast.14, f32[32,1]{1,0:T(8,128)S(1)} %copy.8.scale_ref, bf16[2,2,2,256,128]{4,3,2,1,0:T(8,128)(2,1)S(1)} %copy-done.2, ...), custom_call_target="tpu_custom_call" | custom-call | tf_op jit(solution)/shard_map/attend/pallas_call | solution.py:155
  105.5 3.4 %collective-permute-start.4 = (bf16[1,32,2048]{2,1,0:T(8,128)(2,1)S(1)}, bf16[1,32,2048]{2,1,0:T(8,128)(2,1)S(1)}, u32[]{:S(2)}, u32[]{:S(2)}) collective-permute-start(bf16[1,32,2048]{2,1,0:T(8,128)(2,1)S(1)} %bitcast.16), channel_id=1, source_target_pairs={{448,0},{0,64},{64,128},{128,192},{192,256},{256,320},{320,384},{3... | collective-permute-start | bytes 393224 | tf_op jit(solution)/shard_map/ppermute | solution.py:193
  108.9 9.6 %collective-permute-done.4 = bf16[1,32,2048]{2,1,0:T(8,128)(2,1)S(1)} collective-permute-done((bf16[1,32,2048]{2,1,0:T(8,128)(2,1)S(1)}, bf16[1,32,2048]{2,1,0:T(8,128)(2,1)S(1)}, u32[]{:S(2)}, u32[]{:S(2)}) %collective-permute-start.4) | collective-permute-done | bytes 131104 | tf_op jit(solution)/shard_map/ppermute | solution.py:193
  118.5 0.7 copy.10
  (1 shorter events, 0.0 us)
Async XLA Ops:
  3.3 55.3 %all-to-all-start = ((bf16[16,32,2048]{2,1,0:T(8,128)(2,1)}), bf16[16,32,2048]{2,1,0:T(8,128)(2,1)S(1)}, u32[]{:S(2)}, u32[]{:S(2)}) async-start(bf16[16,32,2048]{2,1,0:T(8,128)(2,1)} %broadcast_in_dim.27), calls=%async_computation | async-start | bytes 4194304 | tf_op jit(solution)/shard_map/all_to_all | solution.py:175
  12.0 46.6 %copy-start.1 = (bf16[1,2048,128]{2,1,0:T(8,128)(2,1)S(1)}, bf16[1,2048,128]{2,1,0:T(8,128)(2,1)}, u32[]{:S(2)}) copy-start(bf16[1,2048,128]{2,1,0:T(8,128)(2,1)} %param.9) | copy-start | bytes 1572868
  20.0 42.5 %collective-permute-start = (bf16[2,2,2,256,128]{4,3,2,1,0:T(8,128)(2,1)}, bf16[2,2,2,256,128]{4,3,2,1,0:T(8,128)(2,1)S(1)}, u32[]{:S(2)}, u32[]{:S(2)}) collective-permute-start(bf16[2,2,2,256,128]{4,3,2,1,0:T(8,128)(2,1)} %get-tuple-element.22), channel_id=1, source_target_pairs={{0,32},{16,48},{32,0},{48,16},{1,33},{17,49},{33,1},{49,17},{2,34}... | collective-permute-start | bytes 1572872 | tf_op jit(solution)/shard_map/ppermute | solution.py:178
  24.3 39.0 %collective-permute-start.1 = (bf16[2,2,2,256,128]{4,3,2,1,0:T(8,128)(2,1)}, bf16[2,2,2,256,128]{4,3,2,1,0:T(8,128)(2,1)}, u32[]{:S(2)}, u32[]{:S(2)}) collective-permute-start(bf16[2,2,2,256,128]{4,3,2,1,0:T(8,128)(2,1)} %get-tuple-element.23), channel_id=1, source_target_pairs={{0,48},{16,32},{32,16},{48,0},{1,49},{17,33},{33,17},{49,1},{2,50}... | collective-permute-start | bytes 1572872 | tf_op jit(solution)/shard_map/ppermute | solution.py:178
  28.8 34.5 %collective-permute-start.2 = (bf16[2,2,2,256,128]{4,3,2,1,0:T(8,128)(2,1)}, bf16[2,2,2,256,128]{4,3,2,1,0:T(8,128)(2,1)}, u32[]{:S(2)}, u32[]{:S(2)}) collective-permute-start(bf16[2,2,2,256,128]{4,3,2,1,0:T(8,128)(2,1)} %get-tuple-element.24), channel_id=1, source_target_pairs={{0,16},{16,0},{32,48},{48,32},{1,17},{17,1},{33,49},{49,33},{2,18}... | collective-permute-start | bytes 1572872 | tf_op jit(solution)/shard_map/ppermute | solution.py:178
  58.5 1.6 %copy-start = (bf16[1,2048,512]{2,1,0:T(8,128)(2,1)S(1)}, bf16[1,2048,512]{2,1,0:T(8,128)(2,1)}, u32[]{:S(2)}) copy-start(bf16[1,2048,512]{2,1,0:T(8,128)(2,1)} %param.8) | copy-start | bytes 6291460
  62.5 40.2 %copy-start.2 = (bf16[2,2,2,256,128]{4,3,2,1,0:T(8,128)(2,1)S(1)}, bf16[2,2,2,256,128]{4,3,2,1,0:T(8,128)(2,1)}, u32[]{:S(2)}) copy-start(bf16[2,2,2,256,128]{4,3,2,1,0:T(8,128)(2,1)} %get-tuple-element.30.refs_0_) | copy-start | bytes 1572868
  62.5 40.2 %copy-start.3 = (s32[1,2]{1,0:T(1,128)S(1)}, s32[1,2]{1,0:T(1,128)}, u32[]{:S(2)}) copy-start(s32[1,2]{1,0:T(1,128)} %lengths_ref.1) | copy-start | bytes 28
  63.3 6.5 %collective-permute-start.3 = (bf16[16,16,640]{2,1,0:T(8,128)(2,1)S(1)}, bf16[16,16,640]{2,1,0:T(8,128)(2,1)S(1)}, u32[]{:S(2)}, u32[]{:S(2)}) collective-permute-start(bf16[16,16,640]{2,1,0:T(8,128)(2,1)S(1)} %get-tuple-element.25), channel_id=1, source_target_pairs={{0,16},{16,0},{1,17},{17,1},{2,18},{18,2},{3,19},{19,3},{4,20},{20... | collective-permute-start | bytes 983048 | tf_op jit(solution)/shard_map/ppermute | solution.py:182
  70.7 15.6 %all-to-all-start.1 = ((bf16[16,16,640]{2,1,0:T(8,128)(2,1)}), bf16[16,16,640]{2,1,0:T(8,128)(2,1)S(1)}, u32[]{:S(2)}, u32[]{:S(2)}) async-start(bf16[16,16,640]{2,1,0:T(8,128)(2,1)} %add_convert_fusion), calls=%async_computation.1 | async-start | bytes 655360 | tf_op jit(solution)/shard_map/all_to_all | solution.py:184
  87.1 15.6 %all-to-all-start.2 = ((bf16[4,4,16,1024]{3,2,1,0:T(8,128)(2,1)}), bf16[4,4,16,1024]{3,2,1,0:T(8,128)(2,1)S(1)}, u32[]{:S(2)}, u32[]{:S(2)}) async-start(bf16[4,4,16,1024]{3,2,1,0:T(8,128)(2,1)} %arrange.1), calls=%async_computation.2 | async-start | bytes 1048576 | tf_op jit(solution)/shard_map/all_to_all | solution.py:187
  105.5 13.0 %collective-permute-start.4 = (bf16[1,32,2048]{2,1,0:T(8,128)(2,1)S(1)}, bf16[1,32,2048]{2,1,0:T(8,128)(2,1)S(1)}, u32[]{:S(2)}, u32[]{:S(2)}) collective-permute-start(bf16[1,32,2048]{2,1,0:T(8,128)(2,1)S(1)} %bitcast.16), channel_id=1, source_target_pairs={{448,0},{0,64},{64,128},{128,192},{192,256},{256,320},{320,384},{3... | collective-permute-start | bytes 393224 | tf_op jit(solution)/shard_map/ppermute | solution.py:193

commit v12 on v10

--- a/solution.py
+++ b/solution.py
@@ -93,7 +93,13 @@
 
 
 def attend_kernel(lengths_ref, place_ref, parts_ref, scale_ref, *refs):
-    caches, out_ref, pair_ref = refs[:4], refs[4], refs[5]
+    sources, out_ref, pair_ref, caches, sems = refs[:4], refs[4], refs[5], refs[6:10], refs[10]
+    copies = [
+        pltpu.make_async_copy(source, cache, sems.at[k])
+        for k, (source, cache) in enumerate(zip(sources, caches))
+    ]
+    for copy in copies:
+        copy.start()
     _, prompts, blocks, samples, _ = parts_ref.shape
     _, _, heads, chunk, dim = caches[0].shape
     per_block = 512 // dim
@@ -128,6 +134,8 @@
             scores = []
             top = own
             for k in range(len(caches)):
+                if p == 0 and g == 0:
+                    copies[k].wait()
                 block = lax.dot_general(
                     query, caches[k][p, 0, g], (((1,), (1,)), ((), ())), preferred_element_type=F32
                 )
@@ -154,8 +162,9 @@
     return pl.pallas_call(
         attend_kernel,
         out_shape=[jax.ShapeDtypeStruct((rows, 2048), BF)] * 2,
-        in_specs=[SMEM, SMEM] + [VMEM] * 6,
+        in_specs=[SMEM, SMEM, VMEM, VMEM] + [pl.BlockSpec(memory_space=pltpu.HBM)] * 4,
         out_specs=(VMEM, VMEM),
+        scratch_shapes=[pltpu.VMEM(c.shape, BF) for c in caches] + [pltpu.SemaphoreType.DMA((4,))],
         compiler_params=PARAMS,
         name="attend",
     )(lengths, place, parts, scale, *caches)

time: 120 us -> 121 us (level)
  no operation moved by 1% of the time
where the time goes in v12:
time: 121 us; the launch traced here: 120 us
  waiting for transfers between devices  52.4 us (43%)
  starting transfers between devices  40.3 us (33%)
  Pallas kernels  13.6 us (11%)
  blocking collectives  7.05 us (6%)
  local copies, waits for them, and re-layouts  3.94 us (3%)
  other arithmetic  1.86 us (2%)
    all_to_all x1, waiting for transfers between devices, shards(): lax.all_to_all(jnp.broadcast_to(sent[None], (count, rows, width)), COL, 0...  29 us
    ppermute x3, starting transfers between devices, shards(): lax.ppermute(caches[k], ROW, [(i, i ^ k) for i in range(row_count)])  10.8 us
    ppermute x1, waiting for transfers between devices, shards(): lax.ppermute(attended[None], 'z', [((i - 1) % count, i) for i in range(co...  9.65 us
    all_to_all x1, waiting for transfers between devices, shards(): parts = lax.all_to_all(arrange(both), ROW, 0, 0)  9.39 us
    all_to_all x1, starting transfers between devices, shards(): lax.all_to_all(jnp.broadcast_to(sent[None], (count, rows, width)), COL, 0...  8.68 us
    psum x1, blocking collectives, shards(): squares = lax.psum(local_squares, ROW)  7.05 us
    pallas_call x1, Pallas kernels, pick(): pl.pallas_call(pick_kernel, grid=(prompts,), out_shape=[jax.ShapeDtypeStr...  6.74 us
    all_to_all x1, starting transfers between devices, shards(): parts = lax.all_to_all(arrange(both), ROW, 0, 0)  6.14 us
  transfers between devices with their start and end apart: 8, of which 5 were waited for; matrix products, arithmetic and copies ran while one was open for 0% of the time, Pallas kernels for 8%

profile of v12, /device:TPU:1, one launch (start us, length us, event | category | flops | bytes accessed | tf_op | source)
XLA Modules:
  0.0 120.0 jit_solution(210885229900946774)
XLA Ops:
  0.6 1.1 fusion.1
  1.7 1.6 %broadcast_in_dim.27 = bf16[16,32,2048]{2,1,0:T(8,128)(2,1)} broadcast(bf16[32,2048]{1,0:T(8,128)(2,1)S(1)} %get-tuple-element.37), dimensions={1,2} | broadcast | bytes 2228224 | tf_op jit(solution)/shard_map/broadcast_in_dim | solution.py:183
  3.3 8.7 %all-to-all-start = ((bf16[16,32,2048]{2,1,0:T(8,128)(2,1)}), bf16[16,32,2048]{2,1,0:T(8,128)(2,1)S(1)}, u32[]{:S(2)}, u32[]{:S(2)}) async-start(bf16[16,32,2048]{2,1,0:T(8,128)(2,1)} %broadcast_in_dim.27), calls=%async_computation | async-start | bytes 4194304 | tf_op jit(solution)/shard_map/all_to_all | solution.py:183
  12.0 0.0 copy-start.1
  12.0 6.7 %pick.1 = (bf16[2,2,2,256,128]{4,3,2,1,0:T(8,128)(2,1)}, bf16[2,2,2,256,128]{4,3,2,1,0:T(8,128)(2,1)}, bf16[2,2,2,256,128]{4,3,2,1,0:T(8,128)(2,1)}, bf16[2,2,2,256,128]{4,3,2,1,0:T(8,128)(2,1)}) custom-call(s32[1]{0:T(128)} %bitcast.place_ref, bf16[2,256,2,1024]{3,2,1,0:T(2,128)(2,1)} %bitcast.17), custom_call_target="tpu_custom_call" | custom-call | tf_op jit(solution)/shard_map/pick/pallas_call | solution.py:63
  18.7 4.3 %collective-permute-start = (bf16[2,2,2,256,128]{4,3,2,1,0:T(8,128)(2,1)}, bf16[2,2,2,256,128]{4,3,2,1,0:T(8,128)(2,1)S(1)}, u32[]{:S(2)}, u32[]{:S(2)}) collective-permute-start(bf16[2,2,2,256,128]{4,3,2,1,0:T(8,128)(2,1)} %get-tuple-element.22), channel_id=1, source_target_pairs={{0,32},{16,48},{32,0},{48,16},{1,33},{17,49},{33,1},{49,17},{2,34}... | collective-permute-start | bytes 1572872 | tf_op jit(solution)/shard_map/ppermute | solution.py:186
  23.1 4.5 %collective-permute-start.1 = (bf16[2,2,2,256,128]{4,3,2,1,0:T(8,128)(2,1)}, bf16[2,2,2,256,128]{4,3,2,1,0:T(8,128)(2,1)}, u32[]{:S(2)}, u32[]{:S(2)}) collective-permute-start(bf16[2,2,2,256,128]{4,3,2,1,0:T(8,128)(2,1)} %get-tuple-element.23), channel_id=1, source_target_pairs={{0,48},{16,32},{32,16},{48,0},{1,49},{17,33},{33,17},{49,1},{2,50}... | collective-permute-start | bytes 1572872 | tf_op jit(solution)/shard_map/ppermute | solution.py:186
  27.6 1.9 %collective-permute-start.2 = (bf16[2,2,2,256,128]{4,3,2,1,0:T(8,128)(2,1)}, bf16[2,2,2,256,128]{4,3,2,1,0:T(8,128)(2,1)}, u32[]{:S(2)}, u32[]{:S(2)}) collective-permute-start(bf16[2,2,2,256,128]{4,3,2,1,0:T(8,128)(2,1)} %get-tuple-element.24), channel_id=1, source_target_pairs={{0,16},{16,0},{32,48},{48,32},{1,17},{17,1},{33,49},{49,33},{2,18}... | collective-permute-start | bytes 1572872 | tf_op jit(solution)/shard_map/ppermute | solution.py:186
  29.5 29.0 %all-to-all-done.gathered_ref = bf16[16,32,2048]{2,1,0:T(8,128)(2,1)S(1)} async-done(((bf16[16,32,2048]{2,1,0:T(8,128)(2,1)}), bf16[16,32,2048]{2,1,0:T(8,128)(2,1)S(1)}, u32[]{:S(2)}, u32[]{:S(2)}) %all-to-all-start) | async-done | bytes 2097184 | tf_op jit(solution)/shard_map/all_to_all | solution.py:183
  58.5 0.0 copy-done.1
  58.5 0.0 copy-start
  58.5 1.6 %copy-done = bf16[1,2048,512]{2,1,0:T(8,128)(2,1)S(1)} copy-done((bf16[1,2048,512]{2,1,0:T(8,128)(2,1)S(1)}, bf16[1,2048,512]{2,1,0:T(8,128)(2,1)}, u32[]{:S(2)}) %copy-start) | copy-done | bytes 2097176
  60.1 2.3 %project.1 = (bf16[16,16,640]{2,1,0:T(8,128)(2,1)S(1)}, bf16[16,16,640]{2,1,0:T(8,128)(2,1)S(1)}) custom-call(s32[1]{0:T(128)} %bitcast.1.place_ref, bf16[16,32,2048]{2,1,0:T(8,128)(2,1)S(1)} %all-to-all-done.gathered_ref, bf16[2048,512]{1,0:T(8,128)(2,1)S(1)} %bitcast.13, bf16[2048,128]{1,0:T(8,128)(2,1)S(1)} %bitcast.15), custom_call_target="tpu_custom_call" | custom-call | tf_op jit(solution)/shard_map/project/pallas_call | solution.py:41
  62.5 0.0 copy-start.2
  62.5 0.0 copy-start.3
  62.5 0.0 collective-permute-done.refs_2_
  62.5 0.0 collective-permute-done.1.refs_3_
  62.5 0.0 collective-permute-done.2.refs_1_
  62.5 6.1 %collective-permute-start.3 = (bf16[16,16,640]{2,1,0:T(8,128)(2,1)S(1)}, bf16[16,16,640]{2,1,0:T(8,128)(2,1)S(1)}, u32[]{:S(2)}, u32[]{:S(2)}) collective-permute-start(bf16[16,16,640]{2,1,0:T(8,128)(2,1)S(1)} %get-tuple-element.25), channel_id=1, source_target_pairs={{0,16},{16,0},{1,17},{17,1},{2,18},{18,2},{3,19},{19,3},{4,20},{20... | collective-permute-start | bytes 983048 | tf_op jit(solution)/shard_map/ppermute | solution.py:190
  68.6 1.2 %collective-permute-done.3 = bf16[16,16,640]{2,1,0:T(8,128)(2,1)S(1)} collective-permute-done((bf16[16,16,640]{2,1,0:T(8,128)(2,1)S(1)}, bf16[16,16,640]{2,1,0:T(8,128)(2,1)S(1)}, u32[]{:S(2)}, u32[]{:S(2)}) %collective-permute-start.3) | collective-permute-done | bytes 327712 | tf_op jit(solution)/shard_map/ppermute | solution.py:190
  69.8 0.8 add_convert_fusion
  70.6 4.7 %all-to-all-start.1 = ((bf16[16,16,640]{2,1,0:T(8,128)(2,1)}), bf16[16,16,640]{2,1,0:T(8,128)(2,1)S(1)}, u32[]{:S(2)}, u32[]{:S(2)}) async-start(bf16[16,16,640]{2,1,0:T(8,128)(2,1)} %add_convert_fusion), calls=%async_computation.1 | async-start | bytes 655360 | tf_op jit(solution)/shard_map/all_to_all | solution.py:192
  75.3 7.1 %psum.7 = f32[32]{0:T(128)S(1)} all-reduce(f32[32]{0:T(128)S(1)} %get-tuple-element.27), channel_id=1, replica_groups=mesh['z'=8,'xh'=2,'co'=2,'xl'=2,'y'=8] {'xh','co'}, use_global_device_ids=true, to_apply=%region_1.0 | all-reduce | flops 32 | bytes 256 | tf_op jit(solution)/shard_map/psum | solution.py:193
  82.4 3.1 %all-to-all-done.1.both_ref = bf16[16,16,640]{2,1,0:T(8,128)(2,1)S(1)} async-done(((bf16[16,16,640]{2,1,0:T(8,128)(2,1)}), bf16[16,16,640]{2,1,0:T(8,128)(2,1)S(1)}, u32[]{:S(2)}, u32[]{:S(2)}) %all-to-all-start.1) | async-done | bytes 327712 | tf_op jit(solution)/shard_map/all_to_all | solution.py:192
  85.5 0.8 arrange.1
  86.3 6.1 %all-to-all-start.2 = ((bf16[4,4,16,1024]{3,2,1,0:T(8,128)(2,1)}), bf16[4,4,16,1024]{3,2,1,0:T(8,128)(2,1)S(1)}, u32[]{:S(2)}, u32[]{:S(2)}) async-start(bf16[4,4,16,1024]{3,2,1,0:T(8,128)(2,1)} %arrange.1), calls=%async_computation.2 | async-start | bytes 1048576 | tf_op jit(solution)/shard_map/all_to_all | solution.py:195
  92.5 0.1 copy.8.scale_ref
  92.6 9.4 %all-to-all-done.2 = bf16[4,4,16,1024]{3,2,1,0:T(8,128)(2,1)S(1)} async-done(((bf16[4,4,16,1024]{3,2,1,0:T(8,128)(2,1)}), bf16[4,4,16,1024]{3,2,1,0:T(8,128)(2,1)S(1)}, u32[]{:S(2)}, u32[]{:S(2)}) %all-to-all-start.2) | async-done | bytes 524320 | tf_op jit(solution)/shard_map/all_to_all | solution.py:195
  102.0 0.0 copy-done.2
  102.0 0.0 copy-done.3
  102.0 3.7 %attend.1 = (bf16[32,2048]{1,0:T(8,128)(2,1)S(1)}, bf16[32,2048]{1,0:T(8,128)(2,1)}) custom-call(s32[1,2]{1,0:T(1,128)S(1)} %copy-done.3, s32[1]{0:T(128)} %bitcast.place_ref, bf16[2,2,4,16,1024]{4,3,2,1,0:T(8,128)(2,1)S(1)} %bitcast.14, f32[32,1]{1,0:T(8,128)S(1)} %copy.8.scale_ref, bf16[2,2,2,256,128]{4,3,2,1,0:T(8,128)(2,1)S(1)} %copy-done.2, ...), custom_call_target="tpu_custom_call" | custom-call | tf_op jit(solution)/shard_map/attend/pallas_call | solution.py:162
  105.7 4.0 %collective-permute-start.4 = (bf16[1,32,2048]{2,1,0:T(8,128)(2,1)S(1)}, bf16[1,32,2048]{2,1,0:T(8,128)(2,1)S(1)}, u32[]{:S(2)}, u32[]{:S(2)}) collective-permute-start(bf16[1,32,2048]{2,1,0:T(8,128)(2,1)S(1)} %bitcast.16), channel_id=1, source_target_pairs={{448,0},{0,64},{64,128},{128,192},{192,256},{256,320},{320,384},{3... | collective-permute-start | bytes 393224 | tf_op jit(solution)/shard_map/ppermute | solution.py:201
  109.7 9.6 %collective-permute-done.4 = bf16[1,32,2048]{2,1,0:T(8,128)(2,1)S(1)} collective-permute-done((bf16[1,32,2048]{2,1,0:T(8,128)(2,1)S(1)}, bf16[1,32,2048]{2,1,0:T(8,128)(2,1)S(1)}, u32[]{:S(2)}, u32[]{:S(2)}) %collective-permute-start.4) | collective-permute-done | bytes 131104 | tf_op jit(solution)/shard_map/ppermute | solution.py:201
  119.3 0.7 copy.10
  (1 shorter events, 0.0 us)
Async XLA Ops:
  3.3 55.3 %all-to-all-start = ((bf16[16,32,2048]{2,1,0:T(8,128)(2,1)}), bf16[16,32,2048]{2,1,0:T(8,128)(2,1)S(1)}, u32[]{:S(2)}, u32[]{:S(2)}) async-start(bf16[16,32,2048]{2,1,0:T(8,128)(2,1)} %broadcast_in_dim.27), calls=%async_computation | async-start | bytes 4194304 | tf_op jit(solution)/shard_map/all_to_all | solution.py:183
  12.0 46.6 %copy-start.1 = (bf16[1,2048,128]{2,1,0:T(8,128)(2,1)S(1)}, bf16[1,2048,128]{2,1,0:T(8,128)(2,1)}, u32[]{:S(2)}) copy-start(bf16[1,2048,128]{2,1,0:T(8,128)(2,1)} %param.9) | copy-start | bytes 1572868
  18.7 43.8 %collective-permute-start = (bf16[2,2,2,256,128]{4,3,2,1,0:T(8,128)(2,1)}, bf16[2,2,2,256,128]{4,3,2,1,0:T(8,128)(2,1)S(1)}, u32[]{:S(2)}, u32[]{:S(2)}) collective-permute-start(bf16[2,2,2,256,128]{4,3,2,1,0:T(8,128)(2,1)} %get-tuple-element.22), channel_id=1, source_target_pairs={{0,32},{16,48},{32,0},{48,16},{1,33},{17,49},{33,1},{49,17},{2,34}... | collective-permute-start | bytes 1572872 | tf_op jit(solution)/shard_map/ppermute | solution.py:186
  23.1 39.4 %collective-permute-start.1 = (bf16[2,2,2,256,128]{4,3,2,1,0:T(8,128)(2,1)}, bf16[2,2,2,256,128]{4,3,2,1,0:T(8,128)(2,1)}, u32[]{:S(2)}, u32[]{:S(2)}) collective-permute-start(bf16[2,2,2,256,128]{4,3,2,1,0:T(8,128)(2,1)} %get-tuple-element.23), channel_id=1, source_target_pairs={{0,48},{16,32},{32,16},{48,0},{1,49},{17,33},{33,17},{49,1},{2,50}... | collective-permute-start | bytes 1572872 | tf_op jit(solution)/shard_map/ppermute | solution.py:186
  27.6 34.9 %collective-permute-start.2 = (bf16[2,2,2,256,128]{4,3,2,1,0:T(8,128)(2,1)}, bf16[2,2,2,256,128]{4,3,2,1,0:T(8,128)(2,1)}, u32[]{:S(2)}, u32[]{:S(2)}) collective-permute-start(bf16[2,2,2,256,128]{4,3,2,1,0:T(8,128)(2,1)} %get-tuple-element.24), channel_id=1, source_target_pairs={{0,16},{16,0},{32,48},{48,32},{1,17},{17,1},{33,49},{49,33},{2,18}... | collective-permute-start | bytes 1572872 | tf_op jit(solution)/shard_map/ppermute | solution.py:186
  58.5 1.6 %copy-start = (bf16[1,2048,512]{2,1,0:T(8,128)(2,1)S(1)}, bf16[1,2048,512]{2,1,0:T(8,128)(2,1)}, u32[]{:S(2)}) copy-start(bf16[1,2048,512]{2,1,0:T(8,128)(2,1)} %param.8) | copy-start | bytes 6291460
  62.5 39.5 %copy-start.2 = (bf16[2,2,2,256,128]{4,3,2,1,0:T(8,128)(2,1)S(1)}, bf16[2,2,2,256,128]{4,3,2,1,0:T(8,128)(2,1)}, u32[]{:S(2)}) copy-start(bf16[2,2,2,256,128]{4,3,2,1,0:T(8,128)(2,1)} %get-tuple-element.30.refs_0_) | copy-start | bytes 1572868
  62.5 39.5 %copy-start.3 = (s32[1,2]{1,0:T(1,128)S(1)}, s32[1,2]{1,0:T(1,128)}, u32[]{:S(2)}) copy-start(s32[1,2]{1,0:T(1,128)} %lengths_ref.1) | copy-start | bytes 28
  62.5 7.3 %collective-permute-start.3 = (bf16[16,16,640]{2,1,0:T(8,128)(2,1)S(1)}, bf16[16,16,640]{2,1,0:T(8,128)(2,1)S(1)}, u32[]{:S(2)}, u32[]{:S(2)}) collective-permute-start(bf16[16,16,640]{2,1,0:T(8,128)(2,1)S(1)} %get-tuple-element.25), channel_id=1, source_target_pairs={{0,16},{16,0},{1,17},{17,1},{2,18},{18,2},{3,19},{19,3},{4,20},{20... | collective-permute-start | bytes 983048 | tf_op jit(solution)/shard_map/ppermute | solution.py:190
  70.6 14.9 %all-to-all-start.1 = ((bf16[16,16,640]{2,1,0:T(8,128)(2,1)}), bf16[16,16,640]{2,1,0:T(8,128)(2,1)S(1)}, u32[]{:S(2)}, u32[]{:S(2)}) async-start(bf16[16,16,640]{2,1,0:T(8,128)(2,1)} %add_convert_fusion), calls=%async_computation.1 | async-start | bytes 655360 | tf_op jit(solution)/shard_map/all_to_all | solution.py:192
  86.3 15.6 %all-to-all-start.2 = ((bf16[4,4,16,1024]{3,2,1,0:T(8,128)(2,1)}), bf16[4,4,16,1024]{3,2,1,0:T(8,128)(2,1)S(1)}, u32[]{:S(2)}, u32[]{:S(2)}) async-start(bf16[4,4,16,1024]{3,2,1,0:T(8,128)(2,1)} %arrange.1), calls=%async_computation.2 | async-start | bytes 1048576 | tf_op jit(solution)/shard_map/all_to_all | solution.py:195
  105.7 13.7 %collective-permute-start.4 = (bf16[1,32,2048]{2,1,0:T(8,128)(2,1)S(1)}, bf16[1,32,2048]{2,1,0:T(8,128)(2,1)S(1)}, u32[]{:S(2)}, u32[]{:S(2)}) collective-permute-start(bf16[1,32,2048]{2,1,0:T(8,128)(2,1)S(1)} %bitcast.16), channel_id=1, source_target_pairs={{448,0},{0,64},{64,128},{128,192},{192,256},{256,320},{320,384},{3... | collective-permute-start | bytes 393224 | tf_op jit(solution)/shard_map/ppermute | solution.py:201
